TPU v7x, 32 devices: a whole 2x2x4 slice. The times are simulated.
32 devices in a mesh: dom: 8 (over y, x, core), batch: 4 (over z).
Axes of the slice: x: 2, y: 2, z: 4, core: 2. Of those that a mesh axis runs over, the one named last changes fastest.
Arguments:
- heat_state_element: float32 [8, 8, 16, 8, 8, 128], P('dom', None, 'batch'), may hold values from -6 to 6
- wind_reference_flux: bfloat16 [3, 8, 8, 16, 8, 8, 128], P(None, 'dom', None, 'batch'), may hold values from -6 to 6
- geometric_pure_factors: bfloat16 [3, 8, 8, 16, 8, 8, 128], P(None, 'dom', None, 'batch'), may hold values from 1 to 2.5
- geometric_mixed_factors: bfloat16 [3, 8, 8, 16, 8, 8, 128], P(None, 'dom', None, 'batch'), may hold values from -0.3984375 to 0.3984375
- mapping_determinant: bfloat16 [8, 8, 16, 8, 8, 128], P('dom', None, 'batch'), may hold values from 0.5 to 2
- velocity_source_spread: float32 [8, 8, 16, 8, 8, 128], P('dom', None, 'batch'), may hold values from -1.5 to 1.5
- prior_head_state: float32 [8, 8, 16, 8, 8, 128], P('dom', None, 'batch'), may hold values from -6 to 6
- exit_boundary_marks: int32 [8, 8, 16, 8], P('dom', None, 'batch'), may hold values from 0 to 1, as said below
Outputs:
- heat_state_next: float32 [8, 8, 16, 8, 8, 128], P('dom', None, 'batch')
- head_iterate: float32 [8, 8, 16, 8, 8, 128], P('dom', None, 'batch')
- precond_residual: float32 [8, 8, 16, 8, 8, 128], P('dom', None, 'batch')
Inputs may be any that keep to these rules, and one draw needn't show every extreme that they name: `exit_boundary_marks`: the flag is the same on every element copy of a shared node, the first and second directions being periodic; 1 marks an outflow node where the pressure is held at zero.
All inputs are finite; a program needn't handle non-finite values.
Results may differ from a plain program's by a relative error of at most 0.0085.
Values sent between devices are 32-bit elements; how exact they have to be, the bound alone decides.
No kernel may reach another device: no remote copies, remote signals or barrier semaphores. Data moves between devices by JAX's collectives and lax.ppermute only.
A program may use at most 128 MiB of HBM per device.

v0:
```python
import math

import jax
import jax.numpy as jnp
import numpy as np
from jax import lax
from jax.sharding import PartitionSpec as P

QUAD_POINT_TALLY = 8
ITERS = 2


transport_increment = 0.02
conduction_increment = 0.002
step_dt = 0.02


def padded(block, sides, width):
    for axis, dim in sides:
        count = lax.axis_size(axis)
        forward = [(i, i + 1) for i in range(count - 1)]
        forward.append((count - 1, 0))
        backward = [(target, source) for source, target in forward]
        low = lax.ppermute(
            lax.slice_in_dim(block, block.shape[dim] - width, None, axis=dim), axis, forward
        )
        high = lax.ppermute(lax.slice_in_dim(block, 0, width, axis=dim), axis, backward)
        block = jnp.concatenate([low, block, high], axis=dim)
    return block


def legendre_pair(order, point):
    before, current = (1.0, point)
    for level in range(2, order + 1):
        before, current = (
            current,
            ((2 * level - 1) * point * current - (level - 1) * before) / level,
        )
    return (current, before)


def tables():
    degree = QUAD_POINT_TALLY - 1
    points = [math.cos(math.pi * index / degree) for index in range(QUAD_POINT_TALLY)]
    for sweep in range(60):
        updated = []
        for point in points:
            top_value, below_value = legendre_pair(degree, point)
            updated.append(
                point - (point * top_value - below_value) / (QUAD_POINT_TALLY * top_value)
            )
        points = updated
    gll_nodes = points[::-1]
    values = [legendre_pair(degree, point)[0] for point in gll_nodes]
    gll_weights = [2.0 / (degree * QUAD_POINT_TALLY * value * value) for value in values]
    deriv_rows = []
    for row_index in range(QUAD_POINT_TALLY):
        row_items = []
        for col_index in range(QUAD_POINT_TALLY):
            if row_index == col_index:
                row_items.append(0.0)
            else:
                row_items.append(
                    values[row_index]
                    / values[col_index]
                    / (gll_nodes[row_index] - gll_nodes[col_index])
                )
        deriv_rows.append(row_items)
    corner_value = degree * QUAD_POINT_TALLY / 4.0
    deriv_rows[0][0] = -corner_value
    deriv_rows[QUAD_POINT_TALLY - 1][QUAD_POINT_TALLY - 1] = corner_value
    spectral_differentiator = np.array(deriv_rows)
    ends_list = [deriv_rows[index][index] for index in range(QUAD_POINT_TALLY)]
    weight_array = np.array(gll_weights)
    quad_table = (
        weight_array[:, None, None] * weight_array[None, :, None] * weight_array[None, None, :]
    )
    return (
        jnp.asarray(spectral_differentiator, jnp.float32),
        jnp.asarray(
            quad_table.reshape(1, QUAD_POINT_TALLY, 1, QUAD_POINT_TALLY, QUAD_POINT_TALLY, 1),
            jnp.float32,
        ),
        jnp.asarray(np.array(ends_list), jnp.float32),
    )


def slope_components_out(field_in, spectral_differentiator):
    highest = lax.Precision.HIGHEST
    along_r = jnp.einsum("il,albjkz->aibjkz", spectral_differentiator, field_in, precision=highest)
    along_s = jnp.einsum("jl,aiblkz->aibjkz", spectral_differentiator, field_in, precision=highest)
    along_t = jnp.einsum("kl,aibjlz->aibjkz", spectral_differentiator, field_in, precision=highest)
    return (along_r, along_s, along_t)


def laplace_from(
    slope_component_list,
    geometric_pure_factors,
    geometric_mixed_factors,
    spectral_differentiator,
    quadrature_coefficients,
):
    highest = lax.Precision.HIGHEST
    along_r, along_s, along_t = slope_component_list
    diag_r = geometric_pure_factors[0].astype(jnp.float32)
    diag_s = geometric_pure_factors[1].astype(jnp.float32)
    diag_t = geometric_pure_factors[2].astype(jnp.float32)
    off_rs = geometric_mixed_factors[0].astype(jnp.float32)
    off_rt = geometric_mixed_factors[1].astype(jnp.float32)
    off_st = geometric_mixed_factors[2].astype(jnp.float32)
    flux_r = quadrature_coefficients * (diag_r * along_r + off_rs * along_s + off_rt * along_t)
    flux_s = quadrature_coefficients * (off_rs * along_r + diag_s * along_s + off_st * along_t)
    flux_t = quadrature_coefficients * (off_rt * along_r + off_st * along_s + diag_t * along_t)
    result = jnp.einsum("li,albjkz->aibjkz", spectral_differentiator, flux_r, precision=highest)
    result = result + jnp.einsum(
        "lj,aiblkz->aibjkz", spectral_differentiator, flux_s, precision=highest
    )
    return result + jnp.einsum(
        "lk,aibjlz->aibjkz", spectral_differentiator, flux_t, precision=highest
    )


def local_apply(
    field_in,
    geometric_pure_factors,
    geometric_mixed_factors,
    spectral_differentiator,
    quadrature_coefficients,
):
    return laplace_from(
        slope_components_out(field_in, spectral_differentiator),
        geometric_pure_factors,
        geometric_mixed_factors,
        spectral_differentiator,
        quadrature_coefficients,
    )


def subdomain_source_term(
    heat_state_element,
    wind_reference_flux,
    geometric_pure_factors,
    geometric_mixed_factors,
    mapping_determinant,
    spectral_differentiator,
    quadrature_coefficients,
):
    slope_component_list = slope_components_out(heat_state_element, spectral_differentiator)
    stiffness_operator = laplace_from(
        slope_component_list,
        geometric_pure_factors,
        geometric_mixed_factors,
        spectral_differentiator,
        quadrature_coefficients,
    )
    convect_scalar = (
        wind_reference_flux[0].astype(jnp.float32) * slope_component_list[0]
        + wind_reference_flux[1].astype(jnp.float32) * slope_component_list[1]
        + wind_reference_flux[2].astype(jnp.float32) * slope_component_list[2]
    )
    element_lumped_weights = quadrature_coefficients * mapping_determinant.astype(jnp.float32)
    return (
        element_lumped_weights * heat_state_element
        - transport_increment * quadrature_coefficients * convect_scalar
        - conduction_increment * stiffness_operator
    )


def jacobi_diagonal(
    geometric_pure_factors,
    geometric_mixed_factors,
    spectral_differentiator,
    quadrature_coefficients,
    deriv_ends,
):
    highest = lax.Precision.HIGHEST
    squares = spectral_differentiator * spectral_differentiator
    result = jnp.einsum(
        "li,albjkz->aibjkz",
        squares,
        quadrature_coefficients * geometric_pure_factors[0].astype(jnp.float32),
        precision=highest,
    )
    result = result + jnp.einsum(
        "lj,aiblkz->aibjkz",
        squares,
        quadrature_coefficients * geometric_pure_factors[1].astype(jnp.float32),
        precision=highest,
    )
    result = result + jnp.einsum(
        "lk,aibjlz->aibjkz",
        squares,
        quadrature_coefficients * geometric_pure_factors[2].astype(jnp.float32),
        precision=highest,
    )
    end_i = deriv_ends.reshape(1, QUAD_POINT_TALLY, 1, 1, 1, 1)
    end_j = deriv_ends.reshape(1, 1, 1, QUAD_POINT_TALLY, 1, 1)
    end_k = deriv_ends.reshape(1, 1, 1, 1, QUAD_POINT_TALLY, 1)
    cross = (
        geometric_mixed_factors[0].astype(jnp.float32) * end_i * end_j
        + geometric_mixed_factors[1].astype(jnp.float32) * end_i * end_k
        + geometric_mixed_factors[2].astype(jnp.float32) * end_j * end_k
    )
    return result + 2.0 * quadrature_coefficients * cross


def vertical_sums(node_grid):
    upper = node_grid[..., QUAD_POINT_TALLY - 1, :]
    lower = node_grid[..., 0, :]
    joined = upper[..., :-1] + lower[..., 1:]
    new_upper = jnp.concatenate([joined, upper[..., -1:]], axis=-1)
    new_lower = jnp.concatenate([lower[..., :1], joined], axis=-1)
    return jnp.concatenate(
        [
            new_lower[..., None, :],
            node_grid[..., 1 : QUAD_POINT_TALLY - 1, :],
            new_upper[..., None, :],
        ],
        axis=-2,
    )


def node_weights(vertical_layer_tally):
    points = jnp.arange(QUAD_POINT_TALLY)
    layers = jnp.arange(vertical_layer_tally)
    edge_copies = jnp.where((points == 0) | (points == QUAD_POINT_TALLY - 1), 2.0, 1.0).astype(
        jnp.float32
    )
    vertical = jnp.where(
        (points[:, None] == 0) & (layers[None, :] > 0)
        | (points[:, None] == QUAD_POINT_TALLY - 1) & (layers[None, :] < vertical_layer_tally - 1),
        2.0,
        1.0,
    ).astype(jnp.float32)
    copies = (
        edge_copies.reshape(1, QUAD_POINT_TALLY, 1, 1, 1, 1)
        * edge_copies.reshape(1, 1, 1, QUAD_POINT_TALLY, 1, 1)
        * vertical.reshape(1, 1, 1, 1, QUAD_POINT_TALLY, vertical_layer_tally)
    )
    return 1.0 / copies


def keep_mask(exit_boundary_marks, vertical_layer_tally):
    points = jnp.arange(QUAD_POINT_TALLY)
    layers = jnp.arange(vertical_layer_tally)
    top_face = (
        (points[:, None] == QUAD_POINT_TALLY - 1) & (layers[None, :] == vertical_layer_tally - 1)
    ).astype(jnp.float32)
    return 1.0 - exit_boundary_marks.astype(jnp.float32)[:, :, :, :, None, None] * top_face


def pair_sums(extended, dim):
    length = extended.shape[dim]
    elements = (length - 2) // QUAD_POINT_TALLY
    owned_part = lax.slice_in_dim(extended, 1, length - 1, axis=dim)
    new_shape = owned_part.shape[:dim] + (elements, QUAD_POINT_TALLY) + owned_part.shape[dim + 1 :]
    blocks = owned_part.reshape(new_shape)
    first_rows = lax.index_in_dim(blocks, 0, dim + 1, keepdims=False)
    last_rows = lax.index_in_dim(blocks, QUAD_POINT_TALLY - 1, dim + 1, keepdims=False)
    left_ghost = lax.slice_in_dim(extended, 0, 1, axis=dim)
    right_ghost = lax.slice_in_dim(extended, length - 1, length, axis=dim)
    before_first = jnp.concatenate(
        [left_ghost, lax.slice_in_dim(last_rows, 0, elements - 1, axis=dim)], axis=dim
    )
    after_last = jnp.concatenate(
        [lax.slice_in_dim(first_rows, 1, elements, axis=dim), right_ghost], axis=dim
    )
    new_first = jnp.expand_dims(first_rows + before_first, dim + 1)
    new_last = jnp.expand_dims(last_rows + after_last, dim + 1)
    middle = lax.slice_in_dim(blocks, 1, QUAD_POINT_TALLY - 1, axis=dim + 1)
    blocks = jnp.concatenate([new_first, middle, new_last], axis=dim + 1)
    return blocks.reshape(owned_part.shape)


def assemble(stacked):
    count_f, count_x, points_x, count_y, points_y, points_z, vertical_layer_tally = stacked.shape
    node_grid = stacked.reshape(
        count_f,
        count_x * QUAD_POINT_TALLY,
        count_y * QUAD_POINT_TALLY,
        QUAD_POINT_TALLY,
        vertical_layer_tally,
    )
    node_grid = vertical_sums(node_grid)
    extended = padded(node_grid, (("dom", 1),), 1)
    node_grid = pair_sums(extended, 1)
    extended = padded(node_grid, (("batch", 2),), 1)
    node_grid = pair_sums(extended, 2)
    return node_grid.reshape(stacked.shape)


def norm_sum(residual, preconditioned_defect, weights):
    return lax.psum(jnp.sum(residual * preconditioned_defect * weights), ("dom", "batch"))


def shards(
    heat_state_element,
    wind_reference_flux,
    geometric_pure_factors,
    geometric_mixed_factors,
    mapping_determinant,
    velocity_source_spread,
    prior_head_state,
    exit_boundary_marks,
):
    spectral_differentiator, quadrature_coefficients, deriv_ends = tables()
    vertical_layer_tally = heat_state_element.shape[-1]
    element_lumped_weights = quadrature_coefficients * mapping_determinant.astype(jnp.float32)
    quotient_top_part = subdomain_source_term(
        heat_state_element,
        wind_reference_flux,
        geometric_pure_factors,
        geometric_mixed_factors,
        mapping_determinant,
        spectral_differentiator,
        quadrature_coefficients,
    )
    element_main_entries = jacobi_diagonal(
        geometric_pure_factors,
        geometric_mixed_factors,
        spectral_differentiator,
        quadrature_coefficients,
        deriv_ends,
    )
    summed_amounts = assemble(
        jnp.stack(
            [
                quotient_top_part,
                element_lumped_weights,
                element_lumped_weights * prior_head_state,
                element_main_entries,
            ]
        )
    )
    assembled_lumped_weights = summed_amounts[1]
    heat_state_next = summed_amounts[0] / assembled_lumped_weights
    keep_nodes = keep_mask(exit_boundary_marks, vertical_layer_tally)
    weights = node_weights(vertical_layer_tally)
    jacobi_diag = summed_amounts[3]
    head_iterate = keep_nodes * summed_amounts[2] / assembled_lumped_weights
    source_local = -element_lumped_weights * velocity_source_spread / step_dt
    residual = (
        keep_nodes
        * assemble(
            (
                source_local
                - local_apply(
                    head_iterate,
                    geometric_pure_factors,
                    geometric_mixed_factors,
                    spectral_differentiator,
                    quadrature_coefficients,
                )
            )[None]
        )[0]
    )
    preconditioned_defect = residual / jacobi_diag
    precond_dot = norm_sum(residual, preconditioned_defect, weights)
    direction = preconditioned_defect
    for iteration in range(ITERS):
        image_vec = (
            keep_nodes
            * assemble(
                local_apply(
                    direction,
                    geometric_pure_factors,
                    geometric_mixed_factors,
                    spectral_differentiator,
                    quadrature_coefficients,
                )[None]
            )[0]
        )
        step_size = precond_dot / lax.psum(
            jnp.sum(direction * image_vec * weights), ("dom", "batch")
        )
        head_iterate = head_iterate + step_size * direction
        residual = residual - step_size * image_vec
        preconditioned_defect = residual / jacobi_diag
        if iteration + 1 < ITERS:
            dot_next = norm_sum(residual, preconditioned_defect, weights)
            direction = preconditioned_defect + dot_next / precond_dot * direction
            precond_dot = dot_next
    return (heat_state_next, head_iterate, preconditioned_defect)


def solution(mesh):
    placed = (
        P("dom", None, "batch", None, None, None),
        P(None, "dom", None, "batch", None, None, None),
        P(None, "dom", None, "batch", None, None, None),
        P(None, "dom", None, "batch", None, None, None),
        P("dom", None, "batch", None, None, None),
        P("dom", None, "batch", None, None, None),
        P("dom", None, "batch", None, None, None),
        P("dom", None, "batch", None),
    )
    return jax.shard_map(
        shards,
        mesh=mesh,
        in_specs=placed,
        out_specs=(
            P("dom", None, "batch", None, None, None),
            P("dom", None, "batch", None, None, None),
            P("dom", None, "batch", None, None, None),
        ),
        check_vma=False,
    )
```

profile of v0, /device:TPU:14, one launch (start us, length us, event | category | flops | bytes accessed | tf_op | source)
XLA Modules:
  0.0 315.3 jit_solution(9531078419586909276)
XLA Ops:
  0.7 2.4 fusion.180
  3.0 2.7 convolution_bitcast_fusion.8
  12.0 3.8 %fusion.6 = f32[1,8,4,8,8,128]{5,1,4,3,2,0:T(8,128)S(1)} fusion(f32[8,8,1,1,1]{0,1,4,3,2:T(8,128)S(1)} %copy-done.27, f32[8,4,8,128,8]{3,4,2,1,0:T(8,128)S(1)} %fusion.132, f32[8,4,8,128,8]{3,4,2,1,0:T(8,128)S(1)} %fusion.134, f32[8]{0:T(128)S(1)} %copy-done.30, f32[8,8,8]{0,2,1:T(8,128)S(1)} %copy-done.29, f32[8,8,8]{0,2,1:T(8,128)S(1)} %copy-done.15, ...), kind=kOutput, calls=%fused_computation.52 | convolution fusion | flops 29622272 | bytes 5247264 | tf_op jit(solution)/shard_map/li,albjkz->aibjkz/dot_general | solution.py:178
  16.9 6.4 %fusion.51 = (f32[8,4,8,8,128]{4,0,3,2,1:T(8,128)S(1)}, f32[8,4,8,8,128]{4,0,3,2,1:T(8,128)S(1)}, f32[1,8,4,8,8,128]{5,1,4,3,2,0:T(8,128)S(1)}, f32[1,8,4,8,8,128]{5,1,4,3,2,0:T(8,128)S(1)}) fusion(f32[1,8,4,8,8,128]{5,1,4,3,2,0:T(8,128)S(1)} %convolution_bitcast_fusion.8, f32[8,8,4,8,128]{4,0,3,2,1:T(8,128)S(1)} %fusion.180, ...), kind=kLoop, calls=%fused_computation.98 | loop fusion | flops 5242880 | bytes 11536384 | tf_op jit(solution)/shard_map/reshape.11
  26.6 10.6 %fusion.138 = f32[8,4,8,128,8]{3,4,2,1,0:T(8,128)S(1)} fusion(f32[8,8,1,1,1]{1,0,4,3,2:T(8,128)S(1)} %copy-done.16, f32[8,4,8,8,128]{4,0,3,2,1:T(8,128)S(1)} %get-tuple-element.33), kind=kOutput, calls=%fused_computation.204 | convolution fusion | flops 25165824 | bytes 2097408 | tf_op jit(solution)/shard_map/lj,aiblkz->aibjkz/dot_general | solution.py:115
  37.3 8.4 %fusion.3 = f32[1,8,4,8,8,128]{5,1,4,3,2,0:T(8,128)S(1)} fusion(f32[8,8,1,1,1]{1,0,4,3,2:T(8,128)S(1)} %copy-done.16, f32[1,8,4,8,8,128]{5,1,4,3,2,0:T(8,128)S(1)} %convolution_bitcast_fusion.8, f32[8,4,8,128,8]{3,4,2,1,0:T(8,128)S(1)} %fusion.136, f32[8,4,8,128,8]{3,4,2,1,0:T(8,128)S(1)} %fusion.138, f32[1,8,4,8,8,128]{5,4,3,2,1,0:T(8,128)S(1)} %copy-done.7, ...), kind=kOutput, calls=%fused_computation.49 | convolution fusion | flops 31981568 | bytes 11014400 | tf_op jit(solution)/shard_map/li,albjkz->aibjkz/dot_general | solution.py:114
  47.8 3.5 %pad_maximum_fusion.4 = f32[4,8,32,6,128]{4,0,2,1,3:T(4,128)S(1)} fusion(f32[1,8,32,8,128]{4,0,2,1,3:T(1,128)S(1)} %copy.44, f32[1,8,32,8,128]{4,0,2,1,3:T(1,128)S(1)} %copy.43, f32[1,8,32,8,128]{4,0,2,1,3:T(1,128)S(1)} %copy.42, f32[1,8,32,8,128]{4,0,2,1,3:T(1,128)S(1)} %copy.41), kind=kLoop, calls=%fused_computation.5 | loop fusion | flops 2359296 | bytes 7340032 | tf_op jit(solution)/shard_map/stack | solution.py:326
  56.0 2.1 collective-permute-start.1
  60.7 7.4 %collective-permute-done = f32[4,1,32,8,128]{4,3,0,2,1:T(8,128)S(1)} collective-permute-done((f32[4,1,32,8,128]{4,3,0,2,1:T(8,128)S(1)}, f32[4,1,32,8,128]{4,3,0,2,1:T(8,128)S(1)}, u32[]{:S(2)}, u32[]{:S(2)}) %collective-permute-start) | collective-permute-done | bytes 524320 | tf_op jit(solution)/shard_map/ppermute | solution.py:24
  71.3 8.2 %collective-permute-done.2 = f32[4,8,1,8,128]{4,3,1,0,2:T(8,128)S(1)} collective-permute-done((f32[4,8,1,8,128]{4,3,1,0,2:T(8,128)S(1)}, f32[4,8,1,8,128]{4,3,1,0,2:T(8,128)S(1)}, u32[]{:S(2)}, u32[]{:S(2)}) %collective-permute-start.2) | collective-permute-done | bytes 131104 | tf_op jit(solution)/shard_map/ppermute | solution.py:24
  84.6 5.1 %fusion.55 = (f32[8,4,8,8,128]{4,0,3,2,1:T(8,128)S(1)}, f32[8,4,8,8,128]{4,0,3,2,1:T(8,128)S(1)}) fusion(f32[1,8,4,8,8,128]{5,1,4,3,2,0:T(8,128)S(1)} %convolution_bitcast_fusion.5, f32[8,4,8,128,8]{3,4,2,1,0:T(8,128)S(1)} %fusion.178, f32[8,4,8,128,8]{3,4,2,1,0:T(8,128)S(1)} %fusion.128, f32[8,8,8]{0,2,1:T(8,128)S(1)} %copy-done.15, ...), kind=kLoop, calls=%fused_computation.102 | loop fusion | flops 4456448 | bytes 7866368 | tf_op jit(solution)/shard_map/reshape.62
  92.7 5.9 %fusion.9 = f32[1,8,4,8,8,128]{5,1,4,3,2,0:T(8,128)S(1)} fusion(f32[8,8,1,1,1]{1,0,4,3,2:T(8,128)S(1)} %copy-done.16, f32[1,8,4,8,8,128]{5,1,4,3,2,0:T(8,128)S(1)} %convolution_bitcast_fusion.5, f32[8,4,8,128,8]{3,4,2,1,0:T(8,128)S(1)} %fusion.124, f32[8,4,8,128,8]{3,4,2,1,0:T(8,128)S(1)} %fusion.126, f32[1,8,4,8,8,128]{5,4,3,2,1,0:T(8,128)S(1)} %copy-done.24, ...), kind=kOutput, calls=%fused_computation.55 | convolution fusion | flops 29622272 | bytes 9439488 | tf_op jit(solution)/shard_map/li,albjkz->aibjkz/dot_general | solution.py:114
  101.9 2.2 collective-permute-done.4
  106.8 3.3 %collective-permute-done.6 = f32[1,8,1,8,128]{4,3,1,2,0:T(8,128)S(1)} collective-permute-done((f32[1,8,1,8,128]{4,3,1,2,0:T(8,128)S(1)}, f32[1,8,1,8,128]{4,3,1,2,0:T(8,128)S(1)}, u32[]{:S(2)}, u32[]{:S(2)}) %collective-permute-start.6) | collective-permute-done | bytes 32800 | tf_op jit(solution)/shard_map/ppermute | solution.py:24
  114.4 5.1 %fusion.59 = (f32[8,4,8,8,128]{4,0,3,2,1:T(8,128)S(1)}, f32[8,4,8,8,128]{4,0,3,2,1:T(8,128)S(1)}) fusion(f32[1,8,4,8,8,128]{5,1,4,3,2,0:T(8,128)S(1)} %convolution_bitcast_fusion.3, f32[8,4,8,128,8]{3,4,2,1,0:T(8,128)S(1)} %fusion.176, f32[8,4,8,128,8]{3,4,2,1,0:T(8,128)S(1)} %fusion.121, f32[8,8,8]{0,2,1:T(8,128)S(1)} %copy-done.15, ...), kind=kLoop, calls=%fused_computation.106 | loop fusion | flops 4456448 | bytes 7866368 | tf_op jit(solution)/shard_map/reshape.81
  120.6 2.0 fusion.119
  122.6 4.9 %fusion.11 = f32[1,8,4,8,8,128]{5,1,4,3,2,0:T(8,128)S(1)} fusion(f32[8,8,1,1,1]{1,0,4,3,2:T(8,128)S(1)} %copy-done.16, f32[1,8,4,8,8,128]{5,1,4,3,2,0:T(8,128)S(1)} %convolution_bitcast_fusion.3, f32[8,4,8,128,8]{3,4,2,1,0:T(8,128)S(1)} %fusion.117, f32[8,4,8,128,8]{3,4,2,1,0:T(8,128)S(1)} %fusion.119, f32[8,4,8,128,8]{3,4,2,1,0:T(8,128)S(1)} %fusion.176, ...), kind=kOutput, calls=%fused_computation.57 | convolution fusion | flops 28049408 | bytes 7866624 | tf_op jit(solution)/shard_map/li,albjkz->aibjkz/dot_general | solution.py:114
  130.9 2.2 collective-permute-done.8
  134.2 3.4 %collective-permute-start.11 = (f32[1,8,1,8,128]{4,3,1,2,0:T(8,128)S(1)}, f32[1,8,1,8,128]{4,3,1,2,0:T(8,128)S(1)}, u32[]{:S(2)}, u32[]{:S(2)}) collective-permute-start(f32[1,8,1,8,128]{4,3,1,2,0:T(8,128)S(1)} %get-tuple-element.53), channel_id=1, source_target_pairs={{1,0},{2,1},{3,2},{0,3},{5,4},{6,5},{7,6},{4,7},{9,8},{10,9},{11,1... | collective-permute-start | bytes 98312 | tf_op jit(solution)/shard_map/ppermute | solution.py:27
  137.6 4.1 %collective-permute-done.10 = f32[1,8,1,8,128]{4,3,1,2,0:T(8,128)S(1)} collective-permute-done((f32[1,8,1,8,128]{4,3,1,2,0:T(8,128)S(1)}, f32[1,8,1,8,128]{4,3,1,2,0:T(8,128)S(1)}, u32[]{:S(2)}, u32[]{:S(2)}) %collective-permute-start.10) | collective-permute-done | bytes 32800 | tf_op jit(solution)/shard_map/ppermute | solution.py:24
  143.1 43.7 %all-reduce = (f32[]{:T(128)}, f32[]{:T(128)}) all-reduce(f32[]{:T(128)} %get-tuple-element.4, f32[]{:T(128)} %get-tuple-element.3), channel_id=1, replica_groups=mesh['dom'=8,'batch'=4] {'dom','batch'}, use_global_device_ids=true, to_apply=%region_1.2 | all-reduce | flops 2 | bytes 16 | tf_op jit(solution)/shard_map/psum | solution.py:293
  188.2 3.4 %multiply_reduce_fusion.1 = (f32[]{:T(128)}, f32[1,8,4,8,8,128]{5,4,3,2,1,0:T(8,128)}) fusion(f32[8,8,8,128]{3,2,1,0:T(8,128)} %copy-done.13, f32[4,8,4,8,8,128]{5,4,3,2,1,0:T(8,128)} %copy-done, f32[1,8,4,1,8,128]{5,4,3,2,1,0:T(8,128)} %copy-done.22, f32[1,1,4,8,8,128]{5,4,3,2,1,0:T(8,128)S(1)} %bitcast.753, f32[1,6,4,8,8,128]{5,4,3,2,1,0:T(8,128)} %bitcast.704, ...), kind=kLoop, calls=%fused_computation.214 | loop fusion | flops 7077887 | bytes 4985864 | tf_op jit(solution)/shard_map/reduce_sum | solution.py:293
  191.6 39.0 %psum.30 = f32[]{:T(128)} all-reduce(f32[]{:T(128)} %get-tuple-element.9), channel_id=1, replica_groups=mesh['dom'=8,'batch'=4] {'dom','batch'}, use_global_device_ids=true, to_apply=%region_5.6 | all-reduce | flops 1 | bytes 8 | tf_op jit(solution)/shard_map/psum | solution.py:293
  232.0 1.9 multiply_add_fusion.1
  237.7 5.1 %fusion.63 = (f32[8,4,8,8,128]{4,0,3,2,1:T(8,128)S(1)}, f32[8,4,8,8,128]{4,0,3,2,1:T(8,128)S(1)}) fusion(f32[1,8,4,8,8,128]{5,1,4,3,2,0:T(8,128)S(1)} %convolution_bitcast_fusion.1, f32[8,4,8,128,8]{3,4,2,1,0:T(8,128)S(1)} %fusion.174, f32[8,4,8,128,8]{3,4,2,1,0:T(8,128)S(1)} %fusion.114, f32[8,8,8]{0,2,1:T(8,128)S(1)} %copy-done.15, ...), kind=kLoop, calls=%fused_computation.110 | loop fusion | flops 4456448 | bytes 7866368 | tf_op jit(solution)/shard_map/reshape.94
  243.8 1.8 fusion.112
  245.7 4.9 %fusion.13 = f32[1,8,4,8,8,128]{5,1,4,3,2,0:T(8,128)S(1)} fusion(f32[8,8,1,1,1]{1,0,4,3,2:T(8,128)S(1)} %copy-done.16, f32[1,8,4,8,8,128]{5,1,4,3,2,0:T(8,128)S(1)} %convolution_bitcast_fusion.1, f32[8,4,8,128,8]{3,4,2,1,0:T(8,128)S(1)} %fusion.110, f32[8,4,8,128,8]{3,4,2,1,0:T(8,128)S(1)} %fusion.112, f32[8,4,8,128,8]{3,4,2,1,0:T(8,128)S(1)} %fusion.174, ...), kind=kOutput, calls=%fused_computation.59 | convolution fusion | flops 28049408 | bytes 7866624 | tf_op jit(solution)/shard_map/li,albjkz->aibjkz/dot_general | solution.py:114
  254.0 2.2 collective-permute-done.12
  256.4 1.9 collective-permute-start.15
  258.5 3.7 %collective-permute-done.14 = f32[1,8,1,8,128]{4,3,1,2,0:T(8,128)S(1)} collective-permute-done((f32[1,8,1,8,128]{4,3,1,2,0:T(8,128)S(1)}, f32[1,8,1,8,128]{4,3,1,2,0:T(8,128)S(1)}, u32[]{:S(2)}, u32[]{:S(2)}) %collective-permute-start.14) | collective-permute-done | bytes 32800 | tf_op jit(solution)/shard_map/ppermute | solution.py:24
  263.3 44.7 %psum.31 = f32[]{:T(128)} all-reduce(f32[]{:T(128)} %multiply_reduce_fusion), channel_id=1, replica_groups=mesh['dom'=8,'batch'=4] {'dom','batch'}, use_global_device_ids=true, to_apply=%region_7.8 | all-reduce | flops 1 | bytes 8 | tf_op jit(solution)/shard_map/psum | solution.py:373
  309.3 3.6 %subtract_divide_fusion = (f32[1,8,4,8,8,128]{5,4,3,2,1,0:T(8,128)}, f32[1,8,4,8,8,128]{5,4,3,2,1,0:T(8,128)}) fusion(f32[1,8,4,8,8,128]{5,4,3,2,1,0:T(8,128)} %get-tuple-element.10, f32[4,8,4,8,8,128]{5,4,3,2,1,0:T(8,128)} %copy-done, f32[]{:T(128)S(6)} %div.57, f32[1,8,4,1,8,128]{5,4,3,2,1,0:T(8,128)S(1)} %maximum_add_fusion.7, ...), kind=kLoop, calls=%fused_computation.210 | loop fusion | flops 4456448 | bytes 7607300 | tf_op jit(solution)/shard_map/div | solution.py:378
  (201 shorter events, 59.2 us)
Async XLA Ops:
  0.7 6.2 %copy-start.20 = (bf16[3,1,8,4,8,8,128]{6,5,4,3,2,1,0:T(8,128)(2,1)S(1)}, bf16[3,1,8,4,8,8,128]{6,5,4,3,2,1,0:T(8,128)(2,1)}, u32[]{:S(2)}) copy-start(bf16[3,1,8,4,8,8,128]{6,5,4,3,2,1,0:T(8,128)(2,1)} %param.14) | copy-start | bytes 4718596
  0.7 6.2 %copy-start.21 = (bf16[3,1,8,4,8,8,128]{6,5,4,3,2,1,0:T(8,128)(2,1)S(1)}, bf16[3,1,8,4,8,8,128]{6,5,4,3,2,1,0:T(8,128)(2,1)}, u32[]{:S(2)}) copy-start(bf16[3,1,8,4,8,8,128]{6,5,4,3,2,1,0:T(8,128)(2,1)} %param.13) | copy-start | bytes 4718596
  7.6 106.7 %copy-start.3 = (bf16[1,1,8,4,8,8,128]{6,5,4,3,2,1,0:T(8,128)(2,1)}, bf16[1,1,8,4,8,8,128]{6,5,4,3,2,1,0:T(8,128)(2,1)S(1)}, u32[]{:S(2)}) copy-start(bf16[1,1,8,4,8,8,128]{6,5,4,3,2,1,0:T(8,128)(2,1)S(1)} %get-tuple-element.86) | copy-start | bytes 1572868
  7.6 106.7 %copy-start.5 = (bf16[1,1,8,4,8,8,128]{6,5,4,3,2,1,0:T(8,128)(2,1)}, bf16[1,1,8,4,8,8,128]{6,5,4,3,2,1,0:T(8,128)(2,1)S(1)}, u32[]{:S(2)}) copy-start(bf16[1,1,8,4,8,8,128]{6,5,4,3,2,1,0:T(8,128)(2,1)S(1)} %get-tuple-element.87) | copy-start | bytes 1572868
  7.6 106.7 %copy-start.10 = (bf16[1,1,8,4,8,8,128]{6,5,4,3,2,1,0:T(8,128)(2,1)}, bf16[1,1,8,4,8,8,128]{6,5,4,3,2,1,0:T(8,128)(2,1)S(1)}, u32[]{:S(2)}) copy-start(bf16[1,1,8,4,8,8,128]{6,5,4,3,2,1,0:T(8,128)(2,1)S(1)} %get-tuple-element.38) | copy-start | bytes 1572868
  7.6 115.0 %copy-start.8 = (bf16[1,1,8,4,8,8,128]{6,5,4,3,2,1,0:T(8,128)(2,1)}, bf16[1,1,8,4,8,8,128]{6,5,4,3,2,1,0:T(8,128)(2,1)S(1)}, u32[]{:S(2)}) copy-start(bf16[1,1,8,4,8,8,128]{6,5,4,3,2,1,0:T(8,128)(2,1)S(1)} %get-tuple-element.88) | copy-start | bytes 1572868
  23.2 13.9 %copy-start.19 = (bf16[3,1,8,4,8,8,128]{6,5,4,3,2,1,0:T(8,128)(2,1)S(1)}, bf16[3,1,8,4,8,8,128]{6,5,4,3,2,1,0:T(8,128)(2,1)}, u32[]{:S(2)}) copy-start(bf16[3,1,8,4,8,8,128]{6,5,4,3,2,1,0:T(8,128)(2,1)} %param.12) | copy-start | bytes 4718596
  25.4 11.9 %copy-start.26 = (f32[8,8,8]{0,2,1:T(8,128)S(1)}, f32[8,8,8]{0,2,1:T(8,128)}, u32[]{:S(2)}) copy-start(f32[8,8,8]{0,2,1:T(8,128)} %constant.44) | copy-start | bytes 6148
  56.0 12.1 %collective-permute-start = (f32[4,1,32,8,128]{4,3,0,2,1:T(8,128)S(1)}, f32[4,1,32,8,128]{4,3,0,2,1:T(8,128)S(1)}, u32[]{:S(2)}, u32[]{:S(2)}) collective-permute-start(f32[4,1,32,8,128]{4,3,0,2,1:T(8,128)S(1)} %get-tuple-element.23), channel_id=1, source_target_pairs={{0,4},{4,8},{8,12},{12,16},{16,20},{20,24},{24,28},{28,0},{1,5},{5... | collective-permute-start | bytes 1572872 | tf_op jit(solution)/shard_map/ppermute | solution.py:24
  56.0 12.2 %collective-permute-start.1 = (f32[4,1,32,8,128]{4,3,0,2,1:T(8,128)S(1)}, f32[4,1,32,8,128]{4,3,0,2,1:T(8,128)S(1)}, u32[]{:S(2)}, u32[]{:S(2)}) collective-permute-start(f32[4,1,32,8,128]{4,3,0,2,1:T(8,128)S(1)} %get-tuple-element.24), channel_id=1, source_target_pairs={{4,0},{8,4},{12,8},{16,12},{20,16},{24,20},{28,24},{0,28},{5,1},{9... | collective-permute-start | bytes 1572872 | tf_op jit(solution)/shard_map/ppermute | solution.py:27
  60.7 81.2 %copy-start.13 = (f32[8,8,8,128]{3,2,1,0:T(8,128)}, f32[8,8,8,128]{3,2,1,0:T(8,128)S(1)}, u32[]{:S(2)}) copy-start(f32[8,8,8,128]{3,2,1,0:T(8,128)S(1)} %multiply_divide_fusion) | copy-start | bytes 786436
  69.0 10.7 %collective-permute-start.3 = (f32[4,8,1,8,128]{4,3,1,0,2:T(8,128)S(1)}, f32[4,8,1,8,128]{4,3,1,0,2:T(8,128)S(1)}, u32[]{:S(2)}, u32[]{:S(2)}) collective-permute-start(f32[4,8,1,8,128]{4,3,1,0,2:T(8,128)S(1)} %get-tuple-element.18), channel_id=1, source_target_pairs={{1,0},{2,1},{3,2},{0,3},{5,4},{6,5},{7,6},{4,7},{9,8},{10,9},{11,1... | collective-permute-start | bytes 393224 | tf_op jit(solution)/shard_map/ppermute | solution.py:27
  69.5 10.1 %collective-permute-start.2 = (f32[4,8,1,8,128]{4,3,1,0,2:T(8,128)S(1)}, f32[4,8,1,8,128]{4,3,1,0,2:T(8,128)S(1)}, u32[]{:S(2)}, u32[]{:S(2)}) collective-permute-start(f32[4,8,1,8,128]{4,3,1,0,2:T(8,128)S(1)} %get-tuple-element.17), channel_id=1, source_target_pairs={{0,1},{1,2},{2,3},{3,0},{4,5},{5,6},{6,7},{7,4},{8,9},{9,10},{10,1... | collective-permute-start | bytes 393224 | tf_op jit(solution)/shard_map/ppermute | solution.py:24
  80.3 29.9 %copy-start = (f32[4,8,4,8,8,128]{5,4,3,2,1,0:T(8,128)}, f32[4,8,4,8,8,128]{5,4,3,2,1,0:T(8,128)S(1)}, u32[]{:S(2)}) copy-start(f32[4,8,4,8,8,128]{5,4,3,2,1,0:T(8,128)S(1)} %pad_maximum_fusion.1) | copy-start | bytes 12582916
  84.6 8.0 %copy-start.24 = (f32[1,8,4,8,8,128]{5,4,3,2,1,0:T(8,128)S(1)}, f32[1,8,4,8,8,128]{5,4,3,2,1,0:T(8,128)}, u32[]{:S(2)}) copy-start(f32[1,8,4,8,8,128]{5,4,3,2,1,0:T(8,128)} %param.16) | copy-start | bytes 3145732
  99.6 4.4 %collective-permute-start.4 = (f32[1,1,32,8,128]{4,3,2,1,0:T(8,128)S(1)}, f32[1,1,32,8,128]{4,3,2,1,0:T(8,128)S(1)}, u32[]{:S(2)}, u32[]{:S(2)}) collective-permute-start(f32[1,1,32,8,128]{4,3,2,1,0:T(8,128)S(1)} %get-tuple-element.64), channel_id=1, source_target_pairs={{0,4},{4,8},{8,12},{12,16},{16,20},{20,24},{24,28},{28,0},{1,5},{5... | collective-permute-start | bytes 393224 | tf_op jit(solution)/shard_map/ppermute | solution.py:24
  100.3 4.2 %collective-permute-start.5 = (f32[1,1,32,8,128]{4,3,2,1,0:T(8,128)S(1)}, f32[1,1,32,8,128]{4,3,2,1,0:T(8,128)S(1)}, u32[]{:S(2)}, u32[]{:S(2)}) collective-permute-start(f32[1,1,32,8,128]{4,3,2,1,0:T(8,128)S(1)} %get-tuple-element.65), channel_id=1, source_target_pairs={{4,0},{8,4},{12,8},{16,12},{20,16},{24,20},{28,24},{0,28},{5,1},{9... | collective-permute-start | bytes 393224 | tf_op jit(solution)/shard_map/ppermute | solution.py:27
  104.7 5.5 %collective-permute-start.7 = (f32[1,8,1,8,128]{4,3,1,2,0:T(8,128)S(1)}, f32[1,8,1,8,128]{4,3,1,2,0:T(8,128)S(1)}, u32[]{:S(2)}, u32[]{:S(2)}) collective-permute-start(f32[1,8,1,8,128]{4,3,1,2,0:T(8,128)S(1)} %get-tuple-element.61), channel_id=1, source_target_pairs={{1,0},{2,1},{3,2},{0,3},{5,4},{6,5},{7,6},{4,7},{9,8},{10,9},{11,1... | collective-permute-start | bytes 98312 | tf_op jit(solution)/shard_map/ppermute | solution.py:27
  106.2 3.9 %collective-permute-start.6 = (f32[1,8,1,8,128]{4,3,1,2,0:T(8,128)S(1)}, f32[1,8,1,8,128]{4,3,1,2,0:T(8,128)S(1)}, u32[]{:S(2)}, u32[]{:S(2)}) collective-permute-start(f32[1,8,1,8,128]{4,3,1,2,0:T(8,128)S(1)} %get-tuple-element.60), channel_id=1, source_target_pairs={{0,1},{1,2},{2,3},{3,0},{4,5},{5,6},{6,7},{7,4},{8,9},{9,10},{10,1... | collective-permute-start | bytes 98312 | tf_op jit(solution)/shard_map/ppermute | solution.py:24
  110.1 31.7 %copy-start.18 = (f32[1,8,4,1,8,128]{5,4,3,2,1,0:T(8,128)}, f32[1,8,4,1,8,128]{5,4,3,2,1,0:T(8,128)S(1)}, u32[]{:S(2)}) copy-start(f32[1,8,4,1,8,128]{5,4,3,2,1,0:T(8,128)S(1)} %get-tuple-element.13) | copy-start | bytes 393220
  110.2 31.7 %copy-start.17 = (f32[1,8,4,1,8,128]{5,4,3,2,1,0:T(8,128)}, f32[1,8,4,1,8,128]{5,4,3,2,1,0:T(8,128)S(1)}, u32[]{:S(2)}) copy-start(f32[1,8,4,1,8,128]{5,4,3,2,1,0:T(8,128)S(1)} %maximum_add_fusion.3) | copy-start | bytes 393220
  128.7 4.4 %collective-permute-start.8 = (f32[1,1,32,8,128]{4,3,2,1,0:T(8,128)S(1)}, f32[1,1,32,8,128]{4,3,2,1,0:T(8,128)S(1)}, u32[]{:S(2)}, u32[]{:S(2)}) collective-permute-start(f32[1,1,32,8,128]{4,3,2,1,0:T(8,128)S(1)} %get-tuple-element.56), channel_id=1, source_target_pairs={{0,4},{4,8},{8,12},{12,16},{16,20},{20,24},{24,28},{28,0},{1,5},{5... | collective-permute-start | bytes 393224 | tf_op jit(solution)/shard_map/ppermute | solution.py:24
  129.5 4.6 %collective-permute-start.9 = (f32[1,1,32,8,128]{4,3,2,1,0:T(8,128)S(1)}, f32[1,1,32,8,128]{4,3,2,1,0:T(8,128)S(1)}, u32[]{:S(2)}, u32[]{:S(2)}) collective-permute-start(f32[1,1,32,8,128]{4,3,2,1,0:T(8,128)S(1)} %get-tuple-element.57), channel_id=1, source_target_pairs={{4,0},{8,4},{12,8},{16,12},{20,16},{24,20},{28,24},{0,28},{5,1},{9... | collective-permute-start | bytes 393224 | tf_op jit(solution)/shard_map/ppermute | solution.py:27
  130.9 12.2 %copy-start.2 = (f32[1,1,6,32,8,128]{5,4,3,2,1,0:T(8,128)}, f32[1,1,6,32,8,128]{5,4,3,2,1,0:T(8,128)S(1)}, u32[]{:S(2)}) copy-start(f32[1,1,6,32,8,128]{5,4,3,2,1,0:T(8,128)S(1)} %slice.426) | copy-start | bytes 2359300
  134.2 7.6 %collective-permute-start.11 = (f32[1,8,1,8,128]{4,3,1,2,0:T(8,128)S(1)}, f32[1,8,1,8,128]{4,3,1,2,0:T(8,128)S(1)}, u32[]{:S(2)}, u32[]{:S(2)}) collective-permute-start(f32[1,8,1,8,128]{4,3,1,2,0:T(8,128)S(1)} %get-tuple-element.53), channel_id=1, source_target_pairs={{1,0},{2,1},{3,2},{0,3},{5,4},{6,5},{7,6},{4,7},{9,8},{10,9},{11,1... | collective-permute-start | bytes 98312 | tf_op jit(solution)/shard_map/ppermute | solution.py:27
  137.6 4.2 %collective-permute-start.10 = (f32[1,8,1,8,128]{4,3,1,2,0:T(8,128)S(1)}, f32[1,8,1,8,128]{4,3,1,2,0:T(8,128)S(1)}, u32[]{:S(2)}, u32[]{:S(2)}) collective-permute-start(f32[1,8,1,8,128]{4,3,1,2,0:T(8,128)S(1)} %get-tuple-element.52), channel_id=1, source_target_pairs={{0,1},{1,2},{2,3},{3,0},{4,5},{5,6},{6,7},{7,4},{8,9},{9,10},{10,1... | collective-permute-start | bytes 98312 | tf_op jit(solution)/shard_map/ppermute | solution.py:24
  237.7 8.0 %copy-start.9 = (bf16[1,1,8,4,8,8,128]{6,5,4,3,2,1,0:T(8,128)(2,1)S(1)}, bf16[1,1,8,4,8,8,128]{6,5,4,3,2,1,0:T(8,128)(2,1)}, u32[]{:S(2)}) copy-start(bf16[1,1,8,4,8,8,128]{6,5,4,3,2,1,0:T(8,128)(2,1)} %copy-done.8) | copy-start | bytes 1572868
  251.7 4.4 %collective-permute-start.12 = (f32[1,1,32,8,128]{4,3,2,1,0:T(8,128)S(1)}, f32[1,1,32,8,128]{4,3,2,1,0:T(8,128)S(1)}, u32[]{:S(2)}, u32[]{:S(2)}) collective-permute-start(f32[1,1,32,8,128]{4,3,2,1,0:T(8,128)S(1)} %get-tuple-element.48), channel_id=1, source_target_pairs={{0,4},{4,8},{8,12},{12,16},{16,20},{20,24},{24,28},{28,0},{1,5},{5... | collective-permute-start | bytes 393224 | tf_op jit(solution)/shard_map/ppermute | solution.py:24
  251.8 4.4 %collective-permute-start.13 = (f32[1,1,32,8,128]{4,3,2,1,0:T(8,128)S(1)}, f32[1,1,32,8,128]{4,3,2,1,0:T(8,128)S(1)}, u32[]{:S(2)}, u32[]{:S(2)}) collective-permute-start(f32[1,1,32,8,128]{4,3,2,1,0:T(8,128)S(1)} %get-tuple-element.49), channel_id=1, source_target_pairs={{4,0},{8,4},{12,8},{16,12},{20,16},{24,20},{28,24},{0,28},{5,1},{9... | collective-permute-start | bytes 393224 | tf_op jit(solution)/shard_map/ppermute | solution.py:27
  253.9 8.4 %copy-start.14 = (f32[8,8,8,128]{3,2,1,0:T(8,128)S(1)}, f32[8,8,8,128]{3,2,1,0:T(8,128)}, u32[]{:S(2)}) copy-start(f32[8,8,8,128]{3,2,1,0:T(8,128)} %copy-done.13) | copy-start | bytes 786436
  256.4 5.9 %collective-permute-start.15 = (f32[1,8,1,8,128]{4,3,1,2,0:T(8,128)S(1)}, f32[1,8,1,8,128]{4,3,1,2,0:T(8,128)S(1)}, u32[]{:S(2)}, u32[]{:S(2)}) collective-permute-start(f32[1,8,1,8,128]{4,3,1,2,0:T(8,128)S(1)} %get-tuple-element.45), channel_id=1, source_target_pairs={{1,0},{2,1},{3,2},{0,3},{5,4},{6,5},{7,6},{4,7},{9,8},{10,9},{11,1... | collective-permute-start | bytes 98312 | tf_op jit(solution)/shard_map/ppermute | solution.py:27
  258.3 3.9 %collective-permute-start.14 = (f32[1,8,1,8,128]{4,3,1,2,0:T(8,128)S(1)}, f32[1,8,1,8,128]{4,3,1,2,0:T(8,128)S(1)}, u32[]{:S(2)}, u32[]{:S(2)}) collective-permute-start(f32[1,8,1,8,128]{4,3,1,2,0:T(8,128)S(1)} %get-tuple-element.44), channel_id=1, source_target_pairs={{0,1},{1,2},{2,3},{3,0},{4,5},{5,6},{6,7},{7,4},{8,9},{9,10},{10,1... | collective-permute-start | bytes 98312 | tf_op jit(solution)/shard_map/ppermute | solution.py:24
  (15 other events, 51.8 us)
where the time goes:
time: 320 us; the launch traced here: 315 us
  blocking collectives  127 us (40%)
  matrix products  68.7 us (21%)
  other arithmetic  50.1 us (16%)
  waiting for transfers between devices  35 us (11%)
  starting transfers between devices  17.2 us (5%)
  local copies, waits for them, and re-layouts  10.5 us (3%)
  between operations  6.3 us (2%)
    psum x2, blocking collectives, norm_sum(): lax.psum(jnp.sum(residual * preconditioned_defect * weights), ('dom', 'ba...  82.8 us
    psum x1, blocking collectives, shards(): lax.psum(jnp.sum(direction * image_vec * weights), ('dom', 'batch'))  44.7 us
    ppermute x8, waiting for transfers between devices, padded(): lax.ppermute(lax.slice_in_dim(block, block.shape[dim] - width, None, axis...  33.5 us
    dot_general x4, matrix products, laplace_from(): jnp.einsum('li,albjkz->aibjkz', spectral_differentiator, flux_r, precisio...  24.1 us
    another operation x5, other arithmetic  22 us
    dot_general x4, matrix products, laplace_from(): jnp.einsum('lj,aiblkz->aibjkz', spectral_differentiator, flux_s, precisio...  16.3 us
    ppermute x8, starting transfers between devices, padded(): lax.ppermute(lax.slice_in_dim(block, 0, width, axis=dim), axis, backward)  13.2 us
    dot_general x4, matrix products, slope_components_out(): jnp.einsum('il,albjkz->aibjkz', spectral_differentiator, field_in, precis...  7.6 us
  transfers between devices with their start and end apart: 16, of which 11 were waited for; matrix products, arithmetic and copies ran while one was open for 1% of the time, Pallas kernels for 0%

commit v1 on v0

v1 whole, which is shorter than its diff:
```python
import functools
import math

import jax
import jax.numpy as jnp
import numpy as np
from jax import lax
from jax.experimental import pallas as pl
from jax.experimental.pallas import tpu as pltpu
from jax.sharding import PartitionSpec as P

QUAD_POINT_TALLY = 8
ROWS = QUAD_POINT_TALLY * QUAD_POINT_TALLY
LAST = ROWS - QUAD_POINT_TALLY
ITERS = 2

transport_increment = 0.02
conduction_increment = 0.002
step_dt = 0.02

VMEM_LIMIT = 24 * 1024 * 1024


def legendre_pair(order, point):
    before, current = (1.0, point)
    for level in range(2, order + 1):
        before, current = (
            current,
            ((2 * level - 1) * point * current - (level - 1) * before) / level,
        )
    return (current, before)


def tables():
    degree = QUAD_POINT_TALLY - 1
    points = [math.cos(math.pi * index / degree) for index in range(QUAD_POINT_TALLY)]
    for sweep in range(60):
        updated = []
        for point in points:
            top_value, below_value = legendre_pair(degree, point)
            updated.append(
                point - (point * top_value - below_value) / (QUAD_POINT_TALLY * top_value)
            )
        points = updated
    nodes = points[::-1]
    values = [legendre_pair(degree, point)[0] for point in nodes]
    weights = [2.0 / (degree * QUAD_POINT_TALLY * value * value) for value in values]
    deriv = np.zeros((QUAD_POINT_TALLY, QUAD_POINT_TALLY))
    for row in range(QUAD_POINT_TALLY):
        for col in range(QUAD_POINT_TALLY):
            if row != col:
                deriv[row, col] = values[row] / values[col] / (nodes[row] - nodes[col])
    corner_value = degree * QUAD_POINT_TALLY / 4.0
    deriv[0, 0] = -corner_value
    deriv[degree, degree] = corner_value
    return deriv, np.array(weights)


DERIV, WEIGHTS = tables()
HALF = QUAD_POINT_TALLY // 2


def line_tables(matrix):
    flipped = matrix[:, ::-1]
    even = (matrix + flipped)[:HALF, :HALF] / 2
    odd = (matrix - flipped)[:HALF, :HALF] / 2
    return even, odd


def line_product(matrix, values, sign):
    even, odd = line_tables(matrix)
    plus = [values[l] + values[7 - l] for l in range(HALF)]
    minus = [values[l] - values[7 - l] for l in range(HALF)]
    result = [None] * QUAD_POINT_TALLY
    for i in range(HALF):
        from_plus = sum(float(even[i, l]) * plus[l] for l in range(HALF))
        from_minus = sum(float(odd[i, l]) * minus[l] for l in range(HALF))
        result[i] = from_plus + from_minus
        flip = from_plus - from_minus
        result[7 - i] = flip if sign > 0 else -flip
    return result


def deriv_line(matrix, values):
    even, odd = line_tables(matrix)
    plus = [values[l] + values[7 - l] for l in range(HALF)]
    minus = [values[l] - values[7 - l] for l in range(HALF)]
    result = [None] * QUAD_POINT_TALLY
    for i in range(HALF):
        from_plus = sum(float(even[i, l]) * plus[l] for l in range(HALF))
        from_minus = sum(float(odd[i, l]) * minus[l] for l in range(HALF))
        result[i] = from_minus + from_plus
        result[7 - i] = from_minus - from_plus
    return result


def square_line(matrix, values):
    even, odd = line_tables(matrix)
    plus = [values[l] + values[7 - l] for l in range(HALF)]
    minus = [values[l] - values[7 - l] for l in range(HALF)]
    result = [None] * QUAD_POINT_TALLY
    for i in range(HALF):
        from_plus = sum(float(even[i, l]) * plus[l] for l in range(HALF))
        from_minus = sum(float(odd[i, l]) * minus[l] for l in range(HALF))
        result[i] = from_plus + from_minus
        result[7 - i] = from_plus - from_minus
    return result


def stacked_matrix(matrix):
    whole = np.kron(np.eye(QUAD_POINT_TALLY), matrix).astype(np.float32)
    high = whole.astype(jnp.bfloat16)
    low = (whole - high.astype(np.float32)).astype(jnp.bfloat16)
    return np.concatenate([high, low, high], axis=1)


def height_product(stacked, values):
    high = values.astype(jnp.bfloat16)
    low = (values - high.astype(jnp.float32)).astype(jnp.bfloat16)
    both = jnp.concatenate([high, high, low], axis=0)
    return jnp.dot(stacked, both, preferred_element_type=jnp.float32)


def rows_of(j):
    return slice(QUAD_POINT_TALLY * j, QUAD_POINT_TALLY * (j + 1))


def height_weights(shape):
    level = lax.broadcasted_iota(jnp.int32, shape, 0)
    result = jnp.full(shape, float(WEIGHTS[0]), jnp.float32)
    for k in range(1, QUAD_POINT_TALLY):
        result = jnp.where(level == k, float(WEIGHTS[k]), result)
    return result


def copy_weights(shape):
    level = lax.broadcasted_iota(jnp.int32, shape, 0)
    layer = lax.broadcasted_iota(jnp.int32, shape, 1)
    shared = ((level == 0) & (layer > 0)) | (
        (level == QUAD_POINT_TALLY - 1) & (layer < shape[1] - 1)
    )
    return jnp.where(shared, 0.5, 1.0)


def side_weight(i, j):
    return (0.5 if i in (0, 7) else 1.0) * (0.5 if j in (0, 7) else 1.0)


def dom_sides():
    odd = lax.rem(lax.axis_index("dom"), 2)
    return 7 * (1 - odd), 7 * odd


def batch_sides():
    odd = lax.rem(lax.axis_index("batch"), 2)
    return 1 - odd, odd


def sum_within(field):
    blocks, layers = field.shape[1], field.shape[3]
    lane = lax.broadcasted_iota(jnp.int32, (QUAD_POINT_TALLY, layers), 1)
    upper_rows = pl.ds(QUAD_POINT_TALLY - 1, QUAD_POINT_TALLY, stride=QUAD_POINT_TALLY)
    lower_rows = pl.ds(0, QUAD_POINT_TALLY, stride=QUAD_POINT_TALLY)
    for i in range(QUAD_POINT_TALLY):
        for b in range(blocks):
            upper = field[i, b, upper_rows, :]
            lower = field[i, b, lower_rows, :]
            above = jnp.where(lane < layers - 1, pltpu.roll(lower, layers - 1, 1), 0.0)
            below = jnp.where(lane > 0, pltpu.roll(upper, 1, 1), 0.0)
            field[i, b, upper_rows, :] = upper + above
            field[i, b, lower_rows, :] = lower + below
        for b in range(blocks - 1):
            joined = field[i, b, LAST:ROWS, :] + field[i, b + 1, 0:QUAD_POINT_TALLY, :]
            field[i, b, LAST:ROWS, :] = joined
            field[i, b + 1, 0:QUAD_POINT_TALLY, :] = joined


def emit_faces(field, first, second, ends):
    blocks = field.shape[1]
    side_first, side_second = dom_sides()
    for b in range(blocks):
        first[b] = field[side_first, b]
        second[b] = field[side_second, b]
    for i in range(QUAD_POINT_TALLY):
        ends[0, i] = field[i, 0, 0:QUAD_POINT_TALLY, :]
        ends[1, i] = field[i, blocks - 1, LAST:ROWS, :]


def add_received(field, dom_first, dom_second, batch_first, batch_second):
    blocks = field.shape[1]
    side_first, side_second = dom_sides()
    for b in range(blocks):
        field[side_first, b] = field[side_first, b] + dom_first[b]
        field[side_second, b] = field[side_second, b] + dom_second[b]
    for side, received in zip(batch_sides(), (batch_first, batch_second)):
        block = side * (blocks - 1)
        rows = pl.ds(pl.multiple_of(side * LAST, QUAD_POINT_TALLY), QUAD_POINT_TALLY)
        for i in range(QUAD_POINT_TALLY):
            field[i, block, rows, :] = field[i, block, rows, :] + received[i]


def clear_top(field, keep):
    upper_rows = pl.ds(QUAD_POINT_TALLY - 1, QUAD_POINT_TALLY, stride=QUAD_POINT_TALLY)
    for i in range(QUAD_POINT_TALLY):
        for b in range(field.shape[1]):
            field[i, b, upper_rows, :] = field[i, b, upper_rows, :] * keep[i, b]


def apply_block(field, metric, scratch_s, scratch_t, out, b, scale, height, height_back, extra=None):
    back = scale * DERIV.T
    for i in range(QUAD_POINT_TALLY):
        block = field[i, b]
        along_s = deriv_line(DERIV, [block[rows_of(j)] for j in range(QUAD_POINT_TALLY)])
        for j in range(QUAD_POINT_TALLY):
            scratch_s[i, rows_of(j), :] = along_s[j]
        scratch_t[i] = height_product(height, block)
    for j in range(QUAD_POINT_TALLY):
        rows = rows_of(j)
        along_r = deriv_line(DERIV, [field[i, b, rows, :] for i in range(QUAD_POINT_TALLY)])
        flux_r = []
        additions = []
        for i in range(QUAD_POINT_TALLY):
            along_s, along_t = scratch_s[i, rows, :], scratch_t[i, rows, :]
            rr, ss, tt = (metric[n, i, b, rows, :] for n in range(3))
            rs, rt, st = (metric[n, i, b, rows, :] for n in range(3, 6))
            flux_r.append(rr * along_r[i] + rs * along_s + rt * along_t)
            scratch_s[i, rows, :] = rs * along_r[i] + ss * along_s + st * along_t
            scratch_t[i, rows, :] = rt * along_r[i] + st * along_s + tt * along_t
            if extra is not None:
                additions.append(extra(i, j, along_r[i], along_s, along_t))
        result = deriv_line(back, flux_r)
        for i in range(QUAD_POINT_TALLY):
            out[i, b, rows, :] = result[i] if extra is None else result[i] + additions[i]
    total = None
    for i in range(QUAD_POINT_TALLY):
        block = scratch_s[i]
        from_s = deriv_line(back, [block[rows_of(j)] for j in range(QUAD_POINT_TALLY)])
        from_t = height_product(height_back, scratch_t[i])
        for j in range(QUAD_POINT_TALLY):
            rows = rows_of(j)
            value = out[i, b, rows, :] + from_s[j] + from_t[rows]
            out[i, b, rows, :] = value
            if extra is None:
                term = field[i, b, rows, :] * value
                total = term if total is None else total + term
    return total


def dot_weighted(left, right):
    blocks, layers = left.shape[1], left.shape[3]
    sums = {}
    for i in range(QUAD_POINT_TALLY):
        for b in range(blocks):
            for j in range(QUAD_POINT_TALLY):
                weight = side_weight(i, j)
                term = left[i, b, rows_of(j), :] * right[i, b, rows_of(j), :]
                sums[weight] = sums[weight] + term if weight in sums else term
    total = sums[1.0] + 0.5 * sums[0.5] + 0.25 * sums[0.25]
    return total * copy_weights((QUAD_POINT_TALLY, layers))


def mass_kernel(determinant, prior, mass, mass_prior, first, second, ends):
    blocks, layers = mass.shape[1], mass.shape[3]
    weights = height_weights((QUAD_POINT_TALLY, layers))

    def block(b, carry):
        for i in range(QUAD_POINT_TALLY):
            for j in range(QUAD_POINT_TALLY):
                weight = weights * float(WEIGHTS[i] * WEIGHTS[j])
                value = weight * determinant[i, b, j].astype(jnp.float32)
                mass[i, b, rows_of(j), :] = value
                mass_prior[i, b, rows_of(j), :] = value * prior[i, b, rows_of(j), :]
        return carry

    lax.fori_loop(0, blocks, block, 0)
    for n, field in enumerate((mass, mass_prior)):
        sum_within(field)
        emit_faces(field, first.at[n], second.at[n], ends.at[n])


def metric_kernel(pure, mixed, height_square, metric, diagonal):
    blocks, layers = diagonal.shape[1], diagonal.shape[3]
    weights = height_weights((QUAD_POINT_TALLY, layers))
    level = lax.broadcasted_iota(jnp.int32, (QUAD_POINT_TALLY, layers), 0)
    ends = [float(DERIV[i, i]) for i in range(QUAD_POINT_TALLY)]
    height_ends = jnp.where(level == 0, ends[0], jnp.where(level == 7, ends[7], 0.0))
    squares = DERIV * DERIV

    def block(b, carry):
        for i in range(QUAD_POINT_TALLY):
            for j in range(QUAD_POINT_TALLY):
                weight = weights * float(WEIGHTS[i] * WEIGHTS[j])
                for n in range(3):
                    metric[n, i, b, rows_of(j), :] = weight * pure[n, i, b, j].astype(jnp.float32)
                    metric[n + 3, i, b, rows_of(j), :] = weight * mixed[n, i, b, j].astype(
                        jnp.float32
                    )
        for j in range(QUAD_POINT_TALLY):
            line = square_line(
                squares.T, [metric[0, i, b, rows_of(j), :] for i in range(QUAD_POINT_TALLY)]
            )
            for i in range(QUAD_POINT_TALLY):
                diagonal[i, b, rows_of(j), :] = line[i]
        for i in range(QUAD_POINT_TALLY):
            line = square_line(
                squares.T, [metric[1, i, b, rows_of(j), :] for j in range(QUAD_POINT_TALLY)]
            )
            from_t = height_product(height_square[...], metric[2, i, b])
            for j in range(QUAD_POINT_TALLY):
                rows = rows_of(j)
                value = diagonal[i, b, rows, :] + line[j] + from_t[rows]
                if ends[i] != 0.0 and ends[j] != 0.0:
                    value = value + (2.0 * ends[i] * ends[j]) * metric[3, i, b, rows, :]
                if ends[i] != 0.0:
                    value = value + (2.0 * ends[i]) * height_ends * metric[4, i, b, rows, :]
                if ends[j] != 0.0:
                    value = value + (2.0 * ends[j]) * height_ends * metric[5, i, b, rows, :]
                diagonal[i, b, rows, :] = value
        return carry

    lax.fori_loop(0, blocks, block, 0)
    sum_within(diagonal)


def source_kernel(
    metric, heat, wind, determinant, diagonal, height, height_back,
    numerator, first, second, ends, scratch_s, scratch_t,
):
    blocks, layers = numerator.shape[1], numerator.shape[3]
    weights = height_weights((QUAD_POINT_TALLY, layers))

    def block(b, carry):
        def extra(i, j, along_r, along_s, along_t):
            weight = weights * float(WEIGHTS[i] * WEIGHTS[j])
            convection = (
                wind[0, i, b, j].astype(jnp.float32) * along_r
                + wind[1, i, b, j].astype(jnp.float32) * along_s
                + wind[2, i, b, j].astype(jnp.float32) * along_t
            )
            return weight * (
                determinant[i, b, j].astype(jnp.float32) * heat[i, b, rows_of(j), :]
                - transport_increment * convection
            )

        apply_block(
            heat, metric, scratch_s, scratch_t, numerator, b, -conduction_increment,
            height[...], height_back[...], extra,
        )
        return carry

    lax.fori_loop(0, blocks, block, 0)
    sum_within(numerator)
    for n, field in enumerate((diagonal, numerator)):
        emit_faces(field, first.at[n], second.at[n], ends.at[n])


def ends_kernel(groups, *refs):
    inputs, (first, second) = refs[: 3 * groups], refs[3 * groups :]
    side_first, side_second = dom_sides()
    base = 0
    for group in range(groups):
        ends, dom_first, dom_second = inputs[3 * group : 3 * group + 3]
        blocks = dom_first.shape[1]
        for n in range(ends.shape[0]):
            for side, target in zip(batch_sides(), (first, second)):
                block = side * (blocks - 1)
                rows = pl.ds(pl.multiple_of(side * LAST, QUAD_POINT_TALLY), QUAD_POINT_TALLY)
                for i in range(QUAD_POINT_TALLY):
                    target[base + n, i] = ends[n, side, i]
                for dom_side, received in (
                    (side_first, dom_first),
                    (side_second, dom_second),
                ):
                    target[base + n, dom_side] = (
                        target[base + n, dom_side] + received[n, block, rows, :]
                    )
        base += ends.shape[0]


def start_kernel(
    mass_local, prior_local, dom_first, dom_second, batch_first, batch_second,
    metric, spread, determinant, keep, height, height_back,
    head, mass_inverse, residual, first, second, ends, scratch_s, scratch_t,
):
    blocks, layers = head.shape[1], head.shape[3]
    weights = height_weights((QUAD_POINT_TALLY, layers))
    head[...] = prior_local[...]
    mass_inverse[...] = mass_local[...]
    for n, field in enumerate((mass_inverse, head)):
        add_received(
            field, dom_first.at[n], dom_second.at[n], batch_first.at[n], batch_second.at[n]
        )
    clear_top(head, keep)

    def divide(b, carry):
        for i in range(QUAD_POINT_TALLY):
            inverse = 1.0 / mass_inverse[i, b]
            mass_inverse[i, b] = inverse
            head[i, b] = head[i, b] * inverse
        return carry

    lax.fori_loop(0, blocks, divide, 0)

    def block(b, carry):
        def extra(i, j, along_r, along_s, along_t):
            weight = weights * float(WEIGHTS[i] * WEIGHTS[j] / step_dt)
            return -(weight * determinant[i, b, j].astype(jnp.float32)) * spread[i, b, rows_of(j), :]

        apply_block(
            head, metric, scratch_s, scratch_t, residual, b, -1.0,
            height[...], height_back[...], extra,
        )
        return carry

    lax.fori_loop(0, blocks, block, 0)
    sum_within(residual)
    emit_faces(residual, first.at[0], second.at[0], ends.at[0])


def apply_all(field, metric, scratch_s, scratch_t, out, height, height_back):
    blocks, layers = field.shape[1], field.shape[3]

    def block(b, total):
        return total + apply_block(
            field, metric, scratch_s, scratch_t, out, b, 1.0, height[...], height_back[...]
        )

    return lax.fori_loop(
        0, blocks, block, jnp.zeros((QUAD_POINT_TALLY, layers), jnp.float32)
    )


def first_kernel(
    residual_local, diagonal_local, res_first, res_second, diag_first, diag_second,
    batch_first, batch_second, metric, keep, height, height_back,
    direction, diag_inverse, image, first, second, ends, dots, scratch_s, scratch_t, residual,
):
    blocks = direction.shape[1]
    residual[...] = residual_local[...]
    diag_inverse[...] = diagonal_local[...]
    add_received(residual, res_first.at[0], res_second.at[0], batch_first.at[0], batch_second.at[0])
    add_received(
        diag_inverse, diag_first.at[0], diag_second.at[0], batch_first.at[1], batch_second.at[1]
    )
    clear_top(residual, keep)

    def divide(b, carry):
        for i in range(QUAD_POINT_TALLY):
            inverse = 1.0 / diag_inverse[i, b]
            diag_inverse[i, b] = inverse
            direction[i, b] = residual[i, b] * inverse
        return carry

    lax.fori_loop(0, blocks, divide, 0)
    inner = dot_weighted(residual, direction)
    energy = apply_all(direction, metric, scratch_s, scratch_t, image, height, height_back)
    sum_within(image)
    emit_faces(image, first.at[0], second.at[0], ends.at[0])
    dots[...] = jnp.concatenate(
        [jnp.sum(inner, axis=0, keepdims=True), jnp.sum(energy, axis=0, keepdims=True),
         jnp.zeros((6, inner.shape[1]), jnp.float32)], axis=0,
    )


def second_kernel(
    image_local, dom_first, dom_second, batch_first, batch_second,
    diag_inverse, metric, keep, dots, height, height_back,
    scaled, image_two, first, second, ends, all_dots, scratch_s, scratch_t, image,
):
    blocks = scaled.shape[1]
    image[...] = image_local[...]
    add_received(image, dom_first.at[0], dom_second.at[0], batch_first.at[0], batch_second.at[0])
    clear_top(image, keep)

    def divide(b, carry):
        for i in range(QUAD_POINT_TALLY):
            scaled[i, b] = image[i, b] * diag_inverse[i, b]
        return carry

    lax.fori_loop(0, blocks, divide, 0)
    inner = dot_weighted(image, scaled)
    energy = apply_all(scaled, metric, scratch_s, scratch_t, image_two, height, height_back)
    sum_within(image_two)
    emit_faces(image_two, first.at[0], second.at[0], ends.at[0])
    total = jnp.concatenate(
        [dots[0:2], jnp.sum(inner, axis=0, keepdims=True), jnp.sum(energy, axis=0, keepdims=True),
         dots[4:8]], axis=0,
    )
    for n in range(all_dots.shape[0]):
        all_dots[n] = total


def heat_kernel(
    numerator, dom_first, dom_second, batch_first, batch_second, mass_inverse, heat
):
    heat[...] = numerator[...]
    add_received(heat, dom_first.at[1], dom_second.at[1], batch_first.at[2], batch_second.at[2])
    for b in range(heat.shape[1]):
        for i in range(QUAD_POINT_TALLY):
            heat[i, b] = heat[i, b] * mass_inverse[i, b]


def last_kernel(
    image_local, dom_first, dom_second, batch_first, batch_second,
    diag_inverse, head, direction, scaled, keep, all_dots, out_head, out_defect, image,
):
    blocks = head.shape[1]
    image[...] = image_local[...]
    add_received(image, dom_first.at[0], dom_second.at[0], batch_first.at[0], batch_second.at[0])
    clear_top(image, keep)
    sums = all_dots[0]
    for n in range(1, all_dots.shape[0]):
        sums = sums + all_dots[n]
    sums = jnp.sum(sums, axis=1, keepdims=True)
    inner, energy, cross, energy_two = (sums[n : n + 1] for n in range(4))
    step = inner / energy
    following = step * step * cross - inner
    growth = 1.0 + following / inner
    curvature = growth * growth * energy - 2.0 * growth * step * cross + step * step * energy_two
    step_two = following / curvature
    along_direction = step + step_two * growth
    along_scaled = step * step_two

    def block(b, carry):
        for i in range(QUAD_POINT_TALLY):
            start, change = direction[i, b], scaled[i, b]
            second_change = image[i, b] * diag_inverse[i, b]
            out_head[i, b] = head[i, b] + along_direction * start - along_scaled * change
            out_defect[i, b] = start - along_direction * change + along_scaled * second_change
        return carry

    lax.fori_loop(0, blocks, block, 0)


def call(kernel, name, outs, args, scratch=()):
    whole = pl.BlockSpec(memory_space=pltpu.VMEM)
    return pl.pallas_call(
        kernel,
        name=name,
        out_shape=[jax.ShapeDtypeStruct(shape, jnp.float32) for shape in outs],
        in_specs=[whole] * len(args),
        out_specs=[whole] * len(outs),
        scratch_shapes=[pltpu.VMEM(shape, jnp.float32) for shape in scratch],
        compiler_params=pltpu.CompilerParams(vmem_limit_bytes=VMEM_LIMIT),
    )(*args)


def swaps(first, second, axis):
    count = lax.axis_size(axis)
    near = [(index, index ^ 1) for index in range(count)]
    far = [(index, (((index + 1) ^ 1) - 1) % count) for index in range(count)]
    return lax.ppermute(first, axis, near), lax.ppermute(second, axis, far)


def shards(
    heat_state_element,
    wind_reference_flux,
    geometric_pure_factors,
    geometric_mixed_factors,
    mapping_determinant,
    velocity_source_spread,
    prior_head_state,
    exit_boundary_marks,
):
    _, points, blocks, _, _, layers = heat_state_element.shape
    block_shape = (points, blocks, ROWS, layers)
    heat = heat_state_element.reshape(block_shape)
    spread = velocity_source_spread.reshape(block_shape)
    prior = prior_head_state.reshape(block_shape)
    wind, pure, mixed = (
        array.reshape(array.shape[:1] + array.shape[2:])
        for array in (wind_reference_flux, geometric_pure_factors, geometric_mixed_factors)
    )
    determinant = mapping_determinant[0]
    layer = lax.broadcasted_iota(jnp.int32, (points, blocks, points, layers), 3)
    marks = exit_boundary_marks[0].astype(jnp.float32)[:, :, :, None]
    keep = jnp.where(layer == layers - 1, 1.0 - marks, 1.0)

    height = jnp.asarray(stacked_matrix(DERIV))
    height_back = jnp.asarray(stacked_matrix(DERIV.T))
    height_back_minus = jnp.asarray(stacked_matrix(-DERIV.T))
    height_back_heat = jnp.asarray(stacked_matrix(-conduction_increment * DERIV.T))
    height_square = jnp.asarray(stacked_matrix((DERIV * DERIV).T))

    def faces(count):
        return [(count, blocks, ROWS, layers)] * 2 + [(count, 2, points, points, layers)]

    def ends_call(name, *groups):
        count = sum(group[0].shape[0] for group in groups)
        return call(
            functools.partial(ends_kernel, len(groups)),
            name,
            [(count, points, points, layers)] * 2,
            [array for group in groups for array in group],
        )

    pair = [(points, ROWS, layers)] * 2

    mass, mass_prior, *mass_faces, mass_ends = call(
        mass_kernel, "mass", [block_shape] * 2 + faces(2), [determinant, prior]
    )
    mass_dom = swaps(*mass_faces, "dom")
    metric, diagonal = call(
        metric_kernel, "metric", [(6,) + block_shape, block_shape], [pure, mixed, height_square]
    )
    numerator, *source_faces, source_ends = call(
        source_kernel, "source", [block_shape] + faces(2),
        [metric, heat, wind, determinant, diagonal, height, height_back_heat], pair,
    )
    source_dom = swaps(*source_faces, "dom")
    mass_batch = swaps(*ends_call("mass_ends", (mass_ends, *mass_dom)), "batch")
    head, mass_inverse, residual, *res_faces, res_ends = call(
        start_kernel, "start", [block_shape] * 3 + faces(1),
        [mass, mass_prior, *mass_dom, *mass_batch, metric, spread, determinant, keep,
         height, height_back_minus], pair,
    )
    res_dom = swaps(*res_faces, "dom")
    res_batch = swaps(
        *ends_call("res_ends", (res_ends, *res_dom), (source_ends, *source_dom)), "batch"
    )
    direction, diag_inverse, image, *image_faces, image_ends, dots = call(
        first_kernel, "first", [block_shape] * 3 + faces(1) + [(points, layers)],
        [residual, diagonal, *res_dom, *source_dom, *res_batch, metric, keep,
         height, height_back], pair + [block_shape],
    )
    image_dom = swaps(*image_faces, "dom")
    image_batch = swaps(*ends_call("image_ends", (image_ends, *image_dom)), "batch")
    count = lax.axis_size("dom") * lax.axis_size("batch")
    scaled, image_two, *two_faces, two_ends, all_dots = call(
        second_kernel, "second",
        [block_shape] * 2 + faces(1) + [(count, points, layers)],
        [image, *image_dom, *image_batch, diag_inverse, metric, keep, dots, height, height_back],
        pair + [block_shape],
    )
    two_dom = swaps(*two_faces, "dom")
    all_dots = lax.all_to_all(all_dots, ("dom", "batch"), 0, 0)
    two_batch = swaps(*ends_call("two_ends", (two_ends, *two_dom)), "batch")
    heat_next, = call(
        heat_kernel, "heat", [block_shape],
        [numerator, *source_dom, *res_batch, mass_inverse],
    )
    head_next, defect = call(
        last_kernel, "last", [block_shape] * 2,
        [image_two, *two_dom, *two_batch, diag_inverse, head, direction, scaled, keep, all_dots],
        [block_shape],
    )
    shape = heat_state_element.shape
    return heat_next.reshape(shape), head_next.reshape(shape), defect.reshape(shape)


def solution(mesh):
    field = P("dom", None, "batch", None, None, None)
    triple = P(None, "dom", None, "batch", None, None, None)
    return jax.shard_map(
        shards,
        mesh=mesh,
        in_specs=(
            field, triple, triple, triple, field, field, field, P("dom", None, "batch", None),
        ),
        out_specs=(field, field, field),
        check_vma=False,
    )
```

time: 320 us -> 93.9 us (0.29)
  the two profiles are of different devices: /device:TPU:14 before, /device:TPU:0 now
where the time goes in v1:
time: 93.9 us; the launch traced here: 93.2 us
  starting transfers between devices  30 us (32%)
  waiting for transfers between devices  26 us (28%)
  Pallas kernels  20.1 us (21%)
  local copies, waits for them, and re-layouts  16.2 us (17%)
    ppermute x18, starting transfers between devices, swaps(): return (lax.ppermute(first, axis, near), lax.ppermute(second, axis, far))  26.5 us
    ppermute x18, waiting for transfers between devices, swaps(): return (lax.ppermute(first, axis, near), lax.ppermute(second, axis, far))  26 us
    pallas_call x12, Pallas kernels, call(): pl.pallas_call(kernel, name=name, out_shape=[jax.ShapeDtypeStruct(shape,...  20.1 us
    unnamed x48, local copies, waits for them, and re-layouts  16.2 us
    all_to_all x1, starting transfers between devices, shards(): all_dots = lax.all_to_all(all_dots, ('dom', 'batch'), 0, 0)  3.48 us
  transfers between devices with their start and end apart: 19, of which 10 were waited for; matrix products, arithmetic and copies ran while one was open for 0% of the time, Pallas kernels for 11%

profile of v1, /device:TPU:0, one launch (start us, length us, event | category | flops | bytes accessed | tf_op | source)
XLA Modules:
  0.0 93.2 jit_solution(4453127081918205125)
XLA Ops:
  1.7 1.2 %copy-done.6 = f32[1,8,4,8,8,128]{5,4,3,2,1,0:T(8,128)S(1)} copy-done((f32[1,8,4,8,8,128]{5,4,3,2,1,0:T(8,128)S(1)}, f32[1,8,4,8,8,128]{5,4,3,2,1,0:T(8,128)}, u32[]{:S(2)}) %copy-start.6) | copy-done | bytes 1048600
  3.9 3.6 %collective-permute-start.3 = (f32[2,4,64,128]{3,2,1,0:T(8,128)S(1)}, f32[2,4,64,128]{3,2,1,0:T(8,128)S(1)}, u32[]{:S(2)}, u32[]{:S(2)}) collective-permute-start(f32[2,4,64,128]{3,2,1,0:T(8,128)S(1)} %get-tuple-element.51), channel_id=1, source_target_pairs={{0,28},{4,8},{8,4},{12,16},{16,12},{20,24},{24,20},{28,0},{1,29},{... | collective-permute-start | bytes 786440 | tf_op jit(solution)/shard_map/ppermute | solution.py:552
  7.5 1.4 %copy-done.4 = bf16[3,1,8,4,8,8,128]{6,5,4,3,2,1,0:T(8,128)(2,1)S(1)} copy-done((bf16[3,1,8,4,8,8,128]{6,5,4,3,2,1,0:T(8,128)(2,1)S(1)}, bf16[3,1,8,4,8,8,128]{6,5,4,3,2,1,0:T(8,128)(2,1)}, u32[]{:S(2)}) %copy-start.4) | copy-done | bytes 1572888
  9.7 1.9 %metric.1 = (f32[6,8,4,64,128]{4,3,2,1,0:T(8,128)S(1)}, f32[8,4,64,128]{3,2,1,0:T(8,128)S(1)}) custom-call(bf16[3,8,4,8,8,128]{5,4,3,2,1,0:T(8,128)(2,1)S(1)} %bitcast.16, bf16[3,8,4,8,8,128]{5,4,3,2,1,0:T(8,128)(2,1)S(1)} %bitcast.17, bf16[64,192]{1,0:T(8,128)(2,1)S(1)} %copy-done.21), custom_call_target="tpu_custom_call" | custom-call | tf_op jit(solution)/shard_map/metric/pallas_call | solution.py:537
  12.4 3.4 %source.1 = (f32[8,4,64,128]{3,2,1,0:T(8,128)S(1)}, f32[2,4,64,128]{3,2,1,0:T(8,128)S(1)}, f32[2,4,64,128]{3,2,1,0:T(8,128)S(1)}, f32[2,2,8,8,128]{4,3,2,1,0:T(8,128)S(1)}) custom-call(f32[6,8,4,64,128]{4,3,2,1,0:T(8,128)S(1)} %get-tuple-element.43.metric, f32[8,4,64,128]{3,2,1,0:T(8,128)S(1)} %bitcast.18, bf16[3,8,4,8,8,128]{5,4,3,2,1,0:T(8,128)(2,1)S(1)} %bitcast.15, ...), custom_call_target="tpu_custom_call" | custom-call | tf_op jit(solution)/shard_map/source/pallas_call | solution.py:537
  16.7 1.6 %collective-permute-start.4 = (f32[2,8,8,128]{3,2,1,0:T(8,128)S(1)}, f32[2,8,8,128]{3,2,1,0:T(8,128)S(1)}, u32[]{:S(2)}, u32[]{:S(2)}) collective-permute-start(f32[2,8,8,128]{3,2,1,0:T(8,128)S(1)} %get-tuple-element.53), channel_id=1, source_target_pairs={{0,1},{1,0},{2,3},{3,2},{4,5},{5,4},{6,7},{7,6},{8,9},{9,8},{10,11... | collective-permute-start | bytes 196616 | tf_op jit(solution)/shard_map/ppermute | solution.py:552
  18.4 2.5 %collective-permute-start.5 = (f32[2,8,8,128]{3,2,1,0:T(8,128)S(1)}, f32[2,8,8,128]{3,2,1,0:T(8,128)S(1)}, u32[]{:S(2)}, u32[]{:S(2)}) collective-permute-start(f32[2,8,8,128]{3,2,1,0:T(8,128)S(1)} %get-tuple-element.54), channel_id=1, source_target_pairs={{0,3},{1,2},{2,1},{3,0},{4,7},{5,6},{6,5},{7,4},{8,11},{9,10},{10,... | collective-permute-start | bytes 196616 | tf_op jit(solution)/shard_map/ppermute | solution.py:552
  21.1 3.5 %collective-permute-done.5.batch_second = f32[2,8,8,128]{3,2,1,0:T(8,128)S(1)} collective-permute-done((f32[2,8,8,128]{3,2,1,0:T(8,128)S(1)}, f32[2,8,8,128]{3,2,1,0:T(8,128)S(1)}, u32[]{:S(2)}, u32[]{:S(2)}) %collective-permute-start.5) | collective-permute-done | bytes 65568 | tf_op jit(solution)/shard_map/ppermute | solution.py:552
  24.6 3.5 %start.1 = (f32[8,4,64,128]{3,2,1,0:T(8,128)S(1)}, f32[8,4,64,128]{3,2,1,0:T(8,128)S(1)}, f32[8,4,64,128]{3,2,1,0:T(8,128)S(1)}, f32[1,4,64,128]{3,2,1,0:T(8,128...) custom-call(f32[8,4,64,128]{3,2,1,0:T(8,128)S(1)} %get-tuple-element.48.mass_local, ...), custom_call_target="tpu_custom_call" | custom-call | tf_op jit(solution)/shard_map/start/pallas_call | solution.py:537
  30.0 2.1 %collective-permute-start.7 = (f32[1,4,64,128]{3,2,1,0:T(8,128)S(1)}, f32[1,4,64,128]{3,2,1,0:T(8,128)S(1)}, u32[]{:S(2)}, u32[]{:S(2)}) collective-permute-start(f32[1,4,64,128]{3,2,1,0:T(8,128)S(1)} %get-tuple-element.57), channel_id=1, source_target_pairs={{0,28},{4,8},{8,4},{12,16},{16,12},{20,24},{24,20},{28,0},{1,29},{... | collective-permute-start | bytes 393224 | tf_op jit(solution)/shard_map/ppermute | solution.py:552
  32.1 4.6 %collective-permute-done.7.refs_2_.res_second = f32[1,4,64,128]{3,2,1,0:T(8,128)S(1)} collective-permute-done((f32[1,4,64,128]{3,2,1,0:T(8,128)S(1)}, f32[1,4,64,128]{3,2,1,0:T(8,128)S(1)}, u32[]{:S(2)}, u32[]{:S(2)}) %collective-permute-start.7) | collective-permute-done | bytes 131104 | tf_op jit(solution)/shard_map/ppermute | solution.py:552
  36.8 2.6 %collective-permute-start.9 = (f32[3,8,8,128]{3,2,1,0:T(8,128)S(1)}, f32[3,8,8,128]{3,2,1,0:T(8,128)S(1)}, u32[]{:S(2)}, u32[]{:S(2)}) collective-permute-start(f32[3,8,8,128]{3,2,1,0:T(8,128)S(1)} %get-tuple-element.60), channel_id=1, source_target_pairs={{0,3},{1,2},{2,1},{3,0},{4,7},{5,6},{6,5},{7,4},{8,11},{9,10},{10,... | collective-permute-start | bytes 294920 | tf_op jit(solution)/shard_map/ppermute | solution.py:552
  39.4 2.8 %collective-permute-done.8.batch_first = f32[3,8,8,128]{3,2,1,0:T(8,128)S(1)} collective-permute-done((f32[3,8,8,128]{3,2,1,0:T(8,128)S(1)}, f32[3,8,8,128]{3,2,1,0:T(8,128)S(1)}, u32[]{:S(2)}, u32[]{:S(2)}) %collective-permute-start.8) | collective-permute-done | bytes 98336 | tf_op jit(solution)/shard_map/ppermute | solution.py:552
  42.2 1.8 %collective-permute-done.9.batch_second = f32[3,8,8,128]{3,2,1,0:T(8,128)S(1)} collective-permute-done((f32[3,8,8,128]{3,2,1,0:T(8,128)S(1)}, f32[3,8,8,128]{3,2,1,0:T(8,128)S(1)}, u32[]{:S(2)}, u32[]{:S(2)}) %collective-permute-start.9) | collective-permute-done | bytes 98336 | tf_op jit(solution)/shard_map/ppermute | solution.py:552
  44.0 3.5 %first.1 = (f32[8,4,64,128]{3,2,1,0:T(8,128)S(1)}, f32[8,4,64,128]{3,2,1,0:T(8,128)S(1)}, f32[8,4,64,128]{3,2,1,0:T(8,128)S(1)}, f32[1,4,64,128]{3,2,1,0:T(8,128...) custom-call(f32[8,4,64,128]{3,2,1,0:T(8,128)S(1)} %get-tuple-element.62.residual_local,, ...), custom_call_target="tpu_custom_call" | custom-call | tf_op jit(solution)/shard_map/first/pallas_call | solution.py:537
  48.5 2.1 %collective-permute-start.11 = (f32[1,4,64,128]{3,2,1,0:T(8,128)S(1)}, f32[1,4,64,128]{3,2,1,0:T(8,128)S(1)}, u32[]{:S(2)}, u32[]{:S(2)}) collective-permute-start(f32[1,4,64,128]{3,2,1,0:T(8,128)S(1)} %get-tuple-element.65), channel_id=1, source_target_pairs={{0,28},{4,8},{8,4},{12,16},{16,12},{20,24},{24,20},{28,0},{1,29},{... | collective-permute-start | bytes 393224 | tf_op jit(solution)/shard_map/ppermute | solution.py:552
  50.6 4.2 %collective-permute-done.11.refs_2_.dom_second = f32[1,4,64,128]{3,2,1,0:T(8,128)S(1)} collective-permute-done((f32[1,4,64,128]{3,2,1,0:T(8,128)S(1)}, f32[1,4,64,128]{3,2,1,0:T(8,128)S(1)}, u32[]{:S(2)}, u32[]{:S(2)}) %collective-permute-start.11) | collective-permute-done | bytes 131104 | tf_op jit(solution)/shard_map/ppermute | solution.py:552
  55.9 2.4 %collective-permute-start.13 = (f32[1,8,8,128]{3,2,1,0:T(8,128)S(1)}, f32[1,8,8,128]{3,2,1,0:T(8,128)S(1)}, u32[]{:S(2)}, u32[]{:S(2)}) collective-permute-start(f32[1,8,8,128]{3,2,1,0:T(8,128)S(1)} %get-tuple-element.68), channel_id=1, source_target_pairs={{0,3},{1,2},{2,1},{3,0},{4,7},{5,6},{6,5},{7,4},{8,11},{9,10},{10,... | collective-permute-start | bytes 98312 | tf_op jit(solution)/shard_map/ppermute | solution.py:552
  58.8 2.8 %collective-permute-done.13.batch_second = f32[1,8,8,128]{3,2,1,0:T(8,128)S(1)} collective-permute-done((f32[1,8,8,128]{3,2,1,0:T(8,128)S(1)}, f32[1,8,8,128]{3,2,1,0:T(8,128)S(1)}, u32[]{:S(2)}, u32[]{:S(2)}) %collective-permute-start.13) | collective-permute-done | bytes 32800 | tf_op jit(solution)/shard_map/ppermute | solution.py:552
  61.7 4.0 %second.1 = (f32[8,4,64,128]{3,2,1,0:T(8,128)S(1)}, f32[8,4,64,128]{3,2,1,0:T(8,128)S(1)}, f32[1,4,64,128]{3,2,1,0:T(8,128)}, f32[1,4,64,128]{3,2,1,0:T(8,128)S(...) custom-call(f32[8,4,64,128]{3,2,1,0:T(8,128)S(1)} %get-tuple-element.63.image_local, ...), custom_call_target="tpu_custom_call" | custom-call | tf_op jit(solution)/shard_map/second/pallas_call | solution.py:537
  67.6 3.5 %all-to-all-start = ((f32[32,8,128]{2,1,0:T(8,128)}), f32[32,8,128]{2,1,0:T(8,128)S(1)}, u32[]{:S(2)}, u32[]{:S(2)}) async-start(f32[32,8,128]{2,1,0:T(8,128)} %get-tuple-element.80), calls=%async_computation | async-start | bytes 262144 | tf_op jit(solution)/shard_map/all_to_all | solution.py:636
  71.4 2.5 %collective-permute-start.15 = (f32[1,4,64,128]{3,2,1,0:T(8,128)S(1)}, f32[1,4,64,128]{3,2,1,0:T(8,128)S(1)}, u32[]{:S(2)}, u32[]{:S(2)}) collective-permute-start(f32[1,4,64,128]{3,2,1,0:T(8,128)S(1)} %get-tuple-element.73), channel_id=1, source_target_pairs={{0,28},{4,8},{8,4},{12,16},{16,12},{20,24},{24,20},{28,0},{1,29},{... | collective-permute-start | bytes 393224 | tf_op jit(solution)/shard_map/ppermute | solution.py:552
  73.9 4.7 %collective-permute-done.15.refs_2_.dom_second = f32[1,4,64,128]{3,2,1,0:T(8,128)S(1)} collective-permute-done((f32[1,4,64,128]{3,2,1,0:T(8,128)S(1)}, f32[1,4,64,128]{3,2,1,0:T(8,128)S(1)}, u32[]{:S(2)}, u32[]{:S(2)}) %collective-permute-start.15) | collective-permute-done | bytes 131104 | tf_op jit(solution)/shard_map/ppermute | solution.py:552
  78.6 1.9 %collective-permute-start.16 = (f32[1,8,8,128]{3,2,1,0:T(8,128)S(1)}, f32[1,8,8,128]{3,2,1,0:T(8,128)S(1)}, u32[]{:S(2)}, u32[]{:S(2)}) collective-permute-start(f32[1,8,8,128]{3,2,1,0:T(8,128)S(1)} %get-tuple-element.75), channel_id=1, source_target_pairs={{0,1},{1,0},{2,3},{3,2},{4,5},{5,4},{6,7},{7,6},{8,9},{9,8},{10,11... | collective-permute-start | bytes 98312 | tf_op jit(solution)/shard_map/ppermute | solution.py:552
  80.6 2.3 %collective-permute-start.17 = (f32[1,8,8,128]{3,2,1,0:T(8,128)S(1)}, f32[1,8,8,128]{3,2,1,0:T(8,128)S(1)}, u32[]{:S(2)}, u32[]{:S(2)}) collective-permute-start(f32[1,8,8,128]{3,2,1,0:T(8,128)S(1)} %get-tuple-element.76), channel_id=1, source_target_pairs={{0,3},{1,2},{2,1},{3,0},{4,7},{5,6},{6,5},{7,4},{8,11},{9,10},{10,... | collective-permute-start | bytes 98312 | tf_op jit(solution)/shard_map/ppermute | solution.py:552
  82.9 1.2 %copy-done.10 = f32[8,4,64,128]{3,2,1,0:T(8,128)S(1)} copy-done((f32[8,4,64,128]{3,2,1,0:T(8,128)S(1)}, f32[8,4,64,128]{3,2,1,0:T(8,128)}, u32[]{:S(2)}) %copy-start.10) | copy-done | bytes 1048600
  84.1 1.2 %heat.1 = f32[8,4,64,128]{3,2,1,0:T(8,128)} custom-call(f32[8,4,64,128]{3,2,1,0:T(8,128)S(1)} %get-tuple-element.45.numerator, f32[2,4,64,128]{3,2,1,0:T(8,128)S(1)} %collective-permute-done.refs_4_.dom_first.diag_first, f32[2,4,64,128]{3,2,1,0:T(8,128)S(1)} %collective-permute-done.1.refs_5_.dom_second.diag_second, ...), custom_call_target="tpu_custom_call" | custom-call | tf_op jit(solution)/shard_map/heat/pallas_call | solution.py:537
  86.3 1.2 %copy-done.8 = f32[8,4,64,128]{3,2,1,0:T(8,128)S(1)} copy-done((f32[8,4,64,128]{3,2,1,0:T(8,128)S(1)}, f32[8,4,64,128]{3,2,1,0:T(8,128)}, u32[]{:S(2)}) %copy-start.8) | copy-done | bytes 1048600
  87.5 1.2 %copy-done.12 = f32[8,4,64,128]{3,2,1,0:T(8,128)S(1)} copy-done((f32[8,4,64,128]{3,2,1,0:T(8,128)S(1)}, f32[8,4,64,128]{3,2,1,0:T(8,128)}, u32[]{:S(2)}) %copy-start.12) | copy-done | bytes 1048600
  88.7 1.2 %copy-done.14 = f32[8,4,64,128]{3,2,1,0:T(8,128)S(1)} copy-done((f32[8,4,64,128]{3,2,1,0:T(8,128)S(1)}, f32[8,4,64,128]{3,2,1,0:T(8,128)}, u32[]{:S(2)}) %copy-start.14) | copy-done | bytes 1048600
  90.0 1.2 %copy-done.16 = f32[8,4,64,128]{3,2,1,0:T(8,128)S(1)} copy-done((f32[8,4,64,128]{3,2,1,0:T(8,128)S(1)}, f32[8,4,64,128]{3,2,1,0:T(8,128)}, u32[]{:S(2)}) %copy-start.16) | copy-done | bytes 1048600
  91.2 2.1 %last.1 = (f32[8,4,64,128]{3,2,1,0:T(8,128)}, f32[8,4,64,128]{3,2,1,0:T(8,128)}) custom-call(f32[8,4,64,128]{3,2,1,0:T(8,128)S(1)} %copy-done.16, f32[1,4,64,128]{3,2,1,0:T(8,128)S(1)} %collective-permute-done.14.refs_1_.dom_first, f32[1,4,64,128]{3,2,1,0:T(8,128)S(1)} %collective-permute-done.15.refs_2_.dom_second, ...), custom_call_target="tpu_custom_call" | custom-call | tf_op jit(solution)/shard_map/last/pallas_call | solution.py:537
  (69 shorter events, 12.7 us)
Async XLA Ops:
  1.7 1.2 %copy-start.6 = (f32[1,8,4,8,8,128]{5,4,3,2,1,0:T(8,128)S(1)}, f32[1,8,4,8,8,128]{5,4,3,2,1,0:T(8,128)}, u32[]{:S(2)}) copy-start(f32[1,8,4,8,8,128]{5,4,3,2,1,0:T(8,128)} %param.19) | copy-start | bytes 3145732
  2.9 4.6 %copy-start.3 = (bf16[3,1,8,4,8,8,128]{6,5,4,3,2,1,0:T(8,128)(2,1)S(1)}, bf16[3,1,8,4,8,8,128]{6,5,4,3,2,1,0:T(8,128)(2,1)}, u32[]{:S(2)}) copy-start(bf16[3,1,8,4,8,8,128]{6,5,4,3,2,1,0:T(8,128)(2,1)} %param.15) | copy-start | bytes 4718596
  3.4 13.3 %collective-permute-start.2 = (f32[2,4,64,128]{3,2,1,0:T(8,128)S(1)}, f32[2,4,64,128]{3,2,1,0:T(8,128)S(1)}, u32[]{:S(2)}, u32[]{:S(2)}) collective-permute-start(f32[2,4,64,128]{3,2,1,0:T(8,128)S(1)} %get-tuple-element.50), channel_id=1, source_target_pairs={{0,4},{4,0},{8,12},{12,8},{16,20},{20,16},{24,28},{28,24},{1,5},{5... | collective-permute-start | bytes 786440 | tf_op jit(solution)/shard_map/ppermute | solution.py:552
  3.9 12.8 %collective-permute-start.3 = (f32[2,4,64,128]{3,2,1,0:T(8,128)S(1)}, f32[2,4,64,128]{3,2,1,0:T(8,128)S(1)}, u32[]{:S(2)}, u32[]{:S(2)}) collective-permute-start(f32[2,4,64,128]{3,2,1,0:T(8,128)S(1)} %get-tuple-element.51), channel_id=1, source_target_pairs={{0,28},{4,8},{8,4},{12,16},{16,12},{20,24},{24,20},{28,0},{1,29},{... | collective-permute-start | bytes 786440 | tf_op jit(solution)/shard_map/ppermute | solution.py:552
  7.5 1.4 %copy-start.4 = (bf16[3,1,8,4,8,8,128]{6,5,4,3,2,1,0:T(8,128)(2,1)S(1)}, bf16[3,1,8,4,8,8,128]{6,5,4,3,2,1,0:T(8,128)(2,1)}, u32[]{:S(2)}) copy-start(bf16[3,1,8,4,8,8,128]{6,5,4,3,2,1,0:T(8,128)(2,1)} %param.16) | copy-start | bytes 4718596
  9.6 1.9 %copy-start.1 = (bf16[1,8,4,8,8,128]{5,4,3,2,1,0:T(8,128)(2,1)S(1)}, bf16[1,8,4,8,8,128]{5,4,3,2,1,0:T(8,128)(2,1)}, u32[]{:S(2)}) copy-start(bf16[1,8,4,8,8,128]{5,4,3,2,1,0:T(8,128)(2,1)} %param.17) | copy-start | bytes 1572868
  9.6 1.9 %copy-start.2 = (bf16[3,1,8,4,8,8,128]{6,5,4,3,2,1,0:T(8,128)(2,1)S(1)}, bf16[3,1,8,4,8,8,128]{6,5,4,3,2,1,0:T(8,128)(2,1)}, u32[]{:S(2)}) copy-start(bf16[3,1,8,4,8,8,128]{6,5,4,3,2,1,0:T(8,128)(2,1)} %param.14) | copy-start | bytes 4718596
  9.6 2.0 %copy-start.5 = (f32[1,8,4,8,8,128]{5,4,3,2,1,0:T(8,128)S(1)}, f32[1,8,4,8,8,128]{5,4,3,2,1,0:T(8,128)}, u32[]{:S(2)}) copy-start(f32[1,8,4,8,8,128]{5,4,3,2,1,0:T(8,128)} %param.13) | copy-start | bytes 3145732
  9.7 2.0 %copy-start.18 = (bf16[64,192]{1,0:T(8,128)(2,1)S(1)}, bf16[64,192]{1,0:T(8,128)(2,1)}, u32[]{:S(2)}) copy-start(bf16[64,192]{1,0:T(8,128)(2,1)} %constant.6.clone.height) | copy-start | bytes 73732
  12.4 4.3 %copy-start.23 = (s32[1,8,4,8]{3,2,1,0:T(4,128)S(1)}, s32[1,8,4,8]{3,2,1,0:T(4,128)}, u32[]{:S(2)}) copy-start(s32[1,8,4,8]{3,2,1,0:T(4,128)} %param.20) | copy-start | bytes 3076
  12.4 12.2 %copy-start.17 = (f32[1,8,4,8,8,128]{5,4,3,2,1,0:T(8,128)S(1)}, f32[1,8,4,8,8,128]{5,4,3,2,1,0:T(8,128)}, u32[]{:S(2)}) copy-start(f32[1,8,4,8,8,128]{5,4,3,2,1,0:T(8,128)} %param.18) | copy-start | bytes 3145732
  12.4 12.2 %copy-start.20 = (bf16[64,192]{1,0:T(8,128)(2,1)S(1)}, bf16[64,192]{1,0:T(8,128)(2,1)}, u32[]{:S(2)}) copy-start(bf16[64,192]{1,0:T(8,128)(2,1)} %constant.17.clone.height_back) | copy-start | bytes 73732
  15.8 16.3 %collective-permute-start = (f32[2,4,64,128]{3,2,1,0:T(8,128)S(1)}, f32[2,4,64,128]{3,2,1,0:T(8,128)S(1)}, u32[]{:S(2)}, u32[]{:S(2)}) collective-permute-start(f32[2,4,64,128]{3,2,1,0:T(8,128)S(1)} %get-tuple-element.46), channel_id=1, source_target_pairs={{0,4},{4,0},{8,12},{12,8},{16,20},{20,16},{24,28},{28,24},{1,5},{5... | collective-permute-start | bytes 786440 | tf_op jit(solution)/shard_map/ppermute | solution.py:552
  15.8 16.3 %collective-permute-start.1 = (f32[2,4,64,128]{3,2,1,0:T(8,128)S(1)}, f32[2,4,64,128]{3,2,1,0:T(8,128)S(1)}, u32[]{:S(2)}, u32[]{:S(2)}) collective-permute-start(f32[2,4,64,128]{3,2,1,0:T(8,128)S(1)} %get-tuple-element.47), channel_id=1, source_target_pairs={{0,28},{4,8},{8,4},{12,16},{16,12},{20,24},{24,20},{28,0},{1,29},{... | collective-permute-start | bytes 786440 | tf_op jit(solution)/shard_map/ppermute | solution.py:552
  16.7 4.3 %collective-permute-start.4 = (f32[2,8,8,128]{3,2,1,0:T(8,128)S(1)}, f32[2,8,8,128]{3,2,1,0:T(8,128)S(1)}, u32[]{:S(2)}, u32[]{:S(2)}) collective-permute-start(f32[2,8,8,128]{3,2,1,0:T(8,128)S(1)} %get-tuple-element.53), channel_id=1, source_target_pairs={{0,1},{1,0},{2,3},{3,2},{4,5},{5,4},{6,7},{7,6},{8,9},{9,8},{10,11... | collective-permute-start | bytes 196616 | tf_op jit(solution)/shard_map/ppermute | solution.py:552
  18.4 6.2 %collective-permute-start.5 = (f32[2,8,8,128]{3,2,1,0:T(8,128)S(1)}, f32[2,8,8,128]{3,2,1,0:T(8,128)S(1)}, u32[]{:S(2)}, u32[]{:S(2)}) collective-permute-start(f32[2,8,8,128]{3,2,1,0:T(8,128)S(1)} %get-tuple-element.54), channel_id=1, source_target_pairs={{0,3},{1,2},{2,1},{3,0},{4,7},{5,6},{6,5},{7,4},{8,11},{9,10},{10,... | collective-permute-start | bytes 196616 | tf_op jit(solution)/shard_map/ppermute | solution.py:552
  24.6 19.4 %copy-start.19 = (bf16[64,192]{1,0:T(8,128)(2,1)S(1)}, bf16[64,192]{1,0:T(8,128)(2,1)}, u32[]{:S(2)}) copy-start(bf16[64,192]{1,0:T(8,128)(2,1)} %constant.16.clone.height_back) | copy-start | bytes 73732
  30.0 2.1 %collective-permute-start.6 = (f32[1,4,64,128]{3,2,1,0:T(8,128)S(1)}, f32[1,4,64,128]{3,2,1,0:T(8,128)S(1)}, u32[]{:S(2)}, u32[]{:S(2)}) collective-permute-start(f32[1,4,64,128]{3,2,1,0:T(8,128)S(1)} %get-tuple-element.56), channel_id=1, source_target_pairs={{0,4},{4,0},{8,12},{12,8},{16,20},{20,16},{24,28},{28,24},{1,5},{5... | collective-permute-start | bytes 393224 | tf_op jit(solution)/shard_map/ppermute | solution.py:552
  30.0 6.7 %collective-permute-start.7 = (f32[1,4,64,128]{3,2,1,0:T(8,128)S(1)}, f32[1,4,64,128]{3,2,1,0:T(8,128)S(1)}, u32[]{:S(2)}, u32[]{:S(2)}) collective-permute-start(f32[1,4,64,128]{3,2,1,0:T(8,128)S(1)} %get-tuple-element.57), channel_id=1, source_target_pairs={{0,28},{4,8},{8,4},{12,16},{16,12},{20,24},{24,20},{28,0},{1,29},{... | collective-permute-start | bytes 393224 | tf_op jit(solution)/shard_map/ppermute | solution.py:552
  36.7 5.5 %collective-permute-start.8 = (f32[3,8,8,128]{3,2,1,0:T(8,128)S(1)}, f32[3,8,8,128]{3,2,1,0:T(8,128)S(1)}, u32[]{:S(2)}, u32[]{:S(2)}) collective-permute-start(f32[3,8,8,128]{3,2,1,0:T(8,128)S(1)} %get-tuple-element.59), channel_id=1, source_target_pairs={{0,1},{1,0},{2,3},{3,2},{4,5},{5,4},{6,7},{7,6},{8,9},{9,8},{10,11... | collective-permute-start | bytes 294920 | tf_op jit(solution)/shard_map/ppermute | solution.py:552
  36.8 7.2 %collective-permute-start.9 = (f32[3,8,8,128]{3,2,1,0:T(8,128)S(1)}, f32[3,8,8,128]{3,2,1,0:T(8,128)S(1)}, u32[]{:S(2)}, u32[]{:S(2)}) collective-permute-start(f32[3,8,8,128]{3,2,1,0:T(8,128)S(1)} %get-tuple-element.60), channel_id=1, source_target_pairs={{0,3},{1,2},{2,1},{3,0},{4,7},{5,6},{6,5},{7,4},{8,11},{9,10},{10,... | collective-permute-start | bytes 294920 | tf_op jit(solution)/shard_map/ppermute | solution.py:552
  48.5 2.1 %collective-permute-start.10 = (f32[1,4,64,128]{3,2,1,0:T(8,128)S(1)}, f32[1,4,64,128]{3,2,1,0:T(8,128)S(1)}, u32[]{:S(2)}, u32[]{:S(2)}) collective-permute-start(f32[1,4,64,128]{3,2,1,0:T(8,128)S(1)} %get-tuple-element.64), channel_id=1, source_target_pairs={{0,4},{4,0},{8,12},{12,8},{16,20},{20,16},{24,28},{28,24},{1,5},{5... | collective-permute-start | bytes 393224 | tf_op jit(solution)/shard_map/ppermute | solution.py:552
  48.5 6.4 %collective-permute-start.11 = (f32[1,4,64,128]{3,2,1,0:T(8,128)S(1)}, f32[1,4,64,128]{3,2,1,0:T(8,128)S(1)}, u32[]{:S(2)}, u32[]{:S(2)}) collective-permute-start(f32[1,4,64,128]{3,2,1,0:T(8,128)S(1)} %get-tuple-element.65), channel_id=1, source_target_pairs={{0,28},{4,8},{8,4},{12,16},{16,12},{20,24},{24,20},{28,0},{1,29},{... | collective-permute-start | bytes 393224 | tf_op jit(solution)/shard_map/ppermute | solution.py:552
  54.9 4.0 %collective-permute-start.12 = (f32[1,8,8,128]{3,2,1,0:T(8,128)S(1)}, f32[1,8,8,128]{3,2,1,0:T(8,128)S(1)}, u32[]{:S(2)}, u32[]{:S(2)}) collective-permute-start(f32[1,8,8,128]{3,2,1,0:T(8,128)S(1)} %get-tuple-element.67), channel_id=1, source_target_pairs={{0,1},{1,0},{2,3},{3,2},{4,5},{5,4},{6,7},{7,6},{8,9},{9,8},{10,11... | collective-permute-start | bytes 98312 | tf_op jit(solution)/shard_map/ppermute | solution.py:552
  55.9 5.7 %collective-permute-start.13 = (f32[1,8,8,128]{3,2,1,0:T(8,128)S(1)}, f32[1,8,8,128]{3,2,1,0:T(8,128)S(1)}, u32[]{:S(2)}, u32[]{:S(2)}) collective-permute-start(f32[1,8,8,128]{3,2,1,0:T(8,128)S(1)} %get-tuple-element.68), channel_id=1, source_target_pairs={{0,3},{1,2},{2,1},{3,0},{4,7},{5,6},{6,5},{7,4},{8,11},{9,10},{10,... | collective-permute-start | bytes 98312 | tf_op jit(solution)/shard_map/ppermute | solution.py:552
  67.6 18.7 %all-to-all-start = ((f32[32,8,128]{2,1,0:T(8,128)}), f32[32,8,128]{2,1,0:T(8,128)S(1)}, u32[]{:S(2)}, u32[]{:S(2)}) async-start(f32[32,8,128]{2,1,0:T(8,128)} %get-tuple-element.80), calls=%async_computation | async-start | bytes 262144 | tf_op jit(solution)/shard_map/all_to_all | solution.py:636
  71.1 2.9 %collective-permute-start.14 = (f32[1,4,64,128]{3,2,1,0:T(8,128)}, f32[1,4,64,128]{3,2,1,0:T(8,128)S(1)}, u32[]{:S(2)}, u32[]{:S(2)}) collective-permute-start(f32[1,4,64,128]{3,2,1,0:T(8,128)} %get-tuple-element.72), channel_id=1, source_target_pairs={{0,4},{4,0},{8,12},{12,8},{16,20},{20,16},{24,28},{28,24},{1,5},{5... | collective-permute-start | bytes 393224 | tf_op jit(solution)/shard_map/ppermute | solution.py:552
  71.4 7.2 %collective-permute-start.15 = (f32[1,4,64,128]{3,2,1,0:T(8,128)S(1)}, f32[1,4,64,128]{3,2,1,0:T(8,128)S(1)}, u32[]{:S(2)}, u32[]{:S(2)}) collective-permute-start(f32[1,4,64,128]{3,2,1,0:T(8,128)S(1)} %get-tuple-element.73), channel_id=1, source_target_pairs={{0,28},{4,8},{8,4},{12,16},{16,12},{20,24},{24,20},{28,0},{1,29},{... | collective-permute-start | bytes 393224 | tf_op jit(solution)/shard_map/ppermute | solution.py:552
  78.6 6.7 %collective-permute-start.16 = (f32[1,8,8,128]{3,2,1,0:T(8,128)S(1)}, f32[1,8,8,128]{3,2,1,0:T(8,128)S(1)}, u32[]{:S(2)}, u32[]{:S(2)}) collective-permute-start(f32[1,8,8,128]{3,2,1,0:T(8,128)S(1)} %get-tuple-element.75), channel_id=1, source_target_pairs={{0,1},{1,0},{2,3},{3,2},{4,5},{5,4},{6,7},{7,6},{8,9},{9,8},{10,11... | collective-permute-start | bytes 98312 | tf_op jit(solution)/shard_map/ppermute | solution.py:552
  80.6 5.7 %collective-permute-start.17 = (f32[1,8,8,128]{3,2,1,0:T(8,128)S(1)}, f32[1,8,8,128]{3,2,1,0:T(8,128)S(1)}, u32[]{:S(2)}, u32[]{:S(2)}) collective-permute-start(f32[1,8,8,128]{3,2,1,0:T(8,128)S(1)} %get-tuple-element.76), channel_id=1, source_target_pairs={{0,3},{1,2},{2,1},{3,0},{4,7},{5,6},{6,5},{7,4},{8,11},{9,10},{10,... | collective-permute-start | bytes 98312 | tf_op jit(solution)/shard_map/ppermute | solution.py:552
  82.9 1.2 %copy-start.10 = (f32[8,4,64,128]{3,2,1,0:T(8,128)S(1)}, f32[8,4,64,128]{3,2,1,0:T(8,128)}, u32[]{:S(2)}) copy-start(f32[8,4,64,128]{3,2,1,0:T(8,128)} %copy-done.9) | copy-start | bytes 3145732
  86.3 1.2 %copy-start.8 = (f32[8,4,64,128]{3,2,1,0:T(8,128)S(1)}, f32[8,4,64,128]{3,2,1,0:T(8,128)}, u32[]{:S(2)}) copy-start(f32[8,4,64,128]{3,2,1,0:T(8,128)} %copy-done.7) | copy-start | bytes 3145732
  (11 other events, 11.1 us)

commit v2 on v1

v2 whole, which is shorter than its diff:
```python
import functools
import math

import jax
import jax.numpy as jnp
import numpy as np
from jax import lax
from jax.experimental import pallas as pl
from jax.experimental.pallas import tpu as pltpu
from jax.sharding import PartitionSpec as P

QUAD_POINT_TALLY = 8
ROWS = QUAD_POINT_TALLY * QUAD_POINT_TALLY
LAST = ROWS - QUAD_POINT_TALLY
ITERS = 2

transport_increment = 0.02
conduction_increment = 0.002
step_dt = 0.02

VMEM_LIMIT = 12 * 1024 * 1024


def legendre_pair(order, point):
    before, current = (1.0, point)
    for level in range(2, order + 1):
        before, current = (
            current,
            ((2 * level - 1) * point * current - (level - 1) * before) / level,
        )
    return (current, before)


def tables():
    degree = QUAD_POINT_TALLY - 1
    points = [math.cos(math.pi * index / degree) for index in range(QUAD_POINT_TALLY)]
    for sweep in range(60):
        updated = []
        for point in points:
            top_value, below_value = legendre_pair(degree, point)
            updated.append(
                point - (point * top_value - below_value) / (QUAD_POINT_TALLY * top_value)
            )
        points = updated
    nodes = points[::-1]
    values = [legendre_pair(degree, point)[0] for point in nodes]
    weights = [2.0 / (degree * QUAD_POINT_TALLY * value * value) for value in values]
    deriv = np.zeros((QUAD_POINT_TALLY, QUAD_POINT_TALLY))
    for row in range(QUAD_POINT_TALLY):
        for col in range(QUAD_POINT_TALLY):
            if row != col:
                deriv[row, col] = values[row] / values[col] / (nodes[row] - nodes[col])
    corner_value = degree * QUAD_POINT_TALLY / 4.0
    deriv[0, 0] = -corner_value
    deriv[degree, degree] = corner_value
    return deriv, np.array(weights)


DERIV, WEIGHTS = tables()
HALF = QUAD_POINT_TALLY // 2


def line_tables(matrix):
    flipped = matrix[:, ::-1]
    even = (matrix + flipped)[:HALF, :HALF] / 2
    odd = (matrix - flipped)[:HALF, :HALF] / 2
    return even, odd


def deriv_line(matrix, values):
    even, odd = line_tables(matrix)
    plus = [values[l] + values[7 - l] for l in range(HALF)]
    minus = [values[l] - values[7 - l] for l in range(HALF)]
    result = [None] * QUAD_POINT_TALLY
    for i in range(HALF):
        from_plus = sum(float(even[i, l]) * plus[l] for l in range(HALF))
        from_minus = sum(float(odd[i, l]) * minus[l] for l in range(HALF))
        result[i] = from_minus + from_plus
        result[7 - i] = from_minus - from_plus
    return result


def square_line(matrix, values):
    even, odd = line_tables(matrix)
    plus = [values[l] + values[7 - l] for l in range(HALF)]
    minus = [values[l] - values[7 - l] for l in range(HALF)]
    result = [None] * QUAD_POINT_TALLY
    for i in range(HALF):
        from_plus = sum(float(even[i, l]) * plus[l] for l in range(HALF))
        from_minus = sum(float(odd[i, l]) * minus[l] for l in range(HALF))
        result[i] = from_plus + from_minus
        result[7 - i] = from_plus - from_minus
    return result


def stacked_matrix(matrix):
    whole = matrix.astype(np.float32)
    high = whole.astype(jnp.bfloat16)
    low = (whole - high.astype(np.float32)).astype(jnp.bfloat16)
    return np.concatenate([high, low, high], axis=1)


def height_product(stacked, values):
    high = values.astype(jnp.bfloat16)
    low = (values - high.astype(jnp.float32)).astype(jnp.bfloat16)
    both = jnp.concatenate([high, high, low], axis=0)
    return jnp.dot(stacked, both, preferred_element_type=jnp.float32)


def rows_of(j):
    return slice(QUAD_POINT_TALLY * j, QUAD_POINT_TALLY * (j + 1))


def height_weights(shape):
    level = lax.broadcasted_iota(jnp.int32, shape, 0)
    result = jnp.full(shape, float(WEIGHTS[0]), jnp.float32)
    for k in range(1, QUAD_POINT_TALLY):
        result = jnp.where(level == k, float(WEIGHTS[k]), result)
    return result


def copy_weights(shape):
    level = lax.broadcasted_iota(jnp.int32, shape, 0)
    layer = lax.broadcasted_iota(jnp.int32, shape, 1)
    shared = ((level == 0) & (layer > 0)) | (
        (level == QUAD_POINT_TALLY - 1) & (layer < shape[1] - 1)
    )
    return jnp.where(shared, 0.5, 1.0)


def side_weight(i, j):
    return (0.5 if i in (0, 7) else 1.0) * (0.5 if j in (0, 7) else 1.0)


HEIGHT, SIDE, HEIGHT_BACK, HEIGHT_SQUARE = (slice(n * ROWS, (n + 1) * ROWS) for n in range(4))
BOTH = slice(0, 2 * ROWS)


def constants():
    one = np.eye(QUAD_POINT_TALLY)
    return jnp.asarray(
        np.concatenate([
            stacked_matrix(np.kron(one, DERIV)),
            stacked_matrix(np.kron(DERIV, one)),
            stacked_matrix(np.kron(one, DERIV.T)),
            stacked_matrix(np.kron(one, (DERIV * DERIV).T)),
        ])
    )


def dom_sides():
    odd = lax.rem(lax.axis_index("dom"), 2)
    return 7 * (1 - odd), 7 * odd


def batch_sides():
    odd = lax.rem(lax.axis_index("batch"), 2)
    return 1 - odd, odd


UPPER = pl.ds(QUAD_POINT_TALLY - 1, QUAD_POINT_TALLY, stride=QUAD_POINT_TALLY)
LOWER = pl.ds(0, QUAD_POINT_TALLY, stride=QUAD_POINT_TALLY)
TAIL = slice(LAST, ROWS)
HEAD = slice(0, QUAD_POINT_TALLY)


def sum_heights(field, slot):
    layers = field.shape[3]
    lane = lax.broadcasted_iota(jnp.int32, (QUAD_POINT_TALLY, layers), 1)
    for i in range(field.shape[0]):
        upper = field[i, slot, UPPER, :]
        lower = field[i, slot, LOWER, :]
        above = jnp.where(lane < layers - 1, pltpu.roll(lower, layers - 1, 1), 0.0)
        below = jnp.where(lane > 0, pltpu.roll(upper, 1, 1), 0.0)
        field[i, slot, UPPER, :] = upper + above
        field[i, slot, LOWER, :] = lower + below


def face_rows(b):
    return slice(b * LAST, b * LAST + ROWS)


class Parts:
    def __init__(self, inner, ends):
        self.inner, self.ends = inner, ends
        self.blocks = inner.shape[1] + 2

    def at(self, b):
        if b in (0, self.blocks - 1):
            return self.ends, min(b, 1)
        return self.inner, b - 1

    def load(self, i, b, rows):
        field, slot = self.at(b)
        return field[i, slot, rows, :]


class Sides(Parts):
    def load(self, i, b, rows):
        field, slot = self.at(b)
        plane = jnp.minimum(i, 1) if b in (0, self.blocks - 1) else i
        return field[plane, slot, rows, :]


class Whole:
    def __init__(self, field):
        self.field, self.blocks = field, field.shape[1]

    def load(self, i, b, rows):
        return self.field[i, b, rows, :]


def joined(parts, i, b, out):
    out[...] = parts.load(i, b, slice(0, ROWS))
    if b > 0:
        out[HEAD, :] = out[HEAD, :] + parts.load(i, b - 1, TAIL)
    if b < parts.blocks - 1:
        out[TAIL, :] = out[TAIL, :] + parts.load(i, b + 1, HEAD)


def emit_faces(parts, first, second):
    for side, target in zip(dom_sides(), (first, second)):
        for b in range(parts.blocks):
            joined(parts, side, b, target.at[face_rows(b)])


def emit_ends(parts, ends):
    for i in range(QUAD_POINT_TALLY):
        ends[0, i] = parts.load(i, 0, HEAD)
        ends[1, i] = parts.load(i, parts.blocks - 1, TAIL)


def assemble(parts, b, out, slot, dom_received, batch_received):
    for i in range(QUAD_POINT_TALLY):
        joined(parts, i, b, out.at[i, slot])
    for side, received in zip(dom_sides(), dom_received):
        out[side, slot] = out[side, slot] + received[face_rows(b), :]
    if batch_received is not None and b in (0, parts.blocks - 1):
        rows = HEAD if b == 0 else TAIL
        low, _ = batch_sides()
        from_first = low == (0 if b == 0 else 1)
        for i in range(QUAD_POINT_TALLY):
            received = jnp.where(from_first, batch_received[0][i], batch_received[1][i])
            out[i, slot, rows, :] = out[i, slot, rows, :] + received


def clear_top(field, slot, keep, b):
    for i in range(QUAD_POINT_TALLY):
        field[i, slot, UPPER, :] = field[i, slot, UPPER, :] * keep[i, b]


def apply_block(field, slot, metric, b, scratch_s, scratch_t, out, matrices, scale=1.0, extra=None):
    both, height_back = matrices[BOTH], matrices[HEIGHT_BACK]
    back = DERIV.T
    for i in range(QUAD_POINT_TALLY):
        slopes = height_product(both, field[i, slot])
        scratch_t[i] = slopes[:ROWS]
        scratch_s[i] = slopes[ROWS:]
    for j in range(QUAD_POINT_TALLY):
        rows = rows_of(j)
        along_r = deriv_line(DERIV, [field[i, slot, rows, :] for i in range(QUAD_POINT_TALLY)])
        flux_r = []
        additions = []
        for i in range(QUAD_POINT_TALLY):
            along_s, along_t = scratch_s[i, rows, :], scratch_t[i, rows, :]
            rr, ss, tt = (metric[n, i, b, rows, :] for n in range(3))
            rs, rt, st = (metric[n, i, b, rows, :] for n in range(3, 6))
            flux_r.append(rr * along_r[i] + rs * along_s + rt * along_t)
            scratch_s[i, rows, :] = rs * along_r[i] + ss * along_s + st * along_t
            scratch_t[i, rows, :] = rt * along_r[i] + st * along_s + tt * along_t
            if extra is not None:
                additions.append(extra(i, j, along_r[i], along_s, along_t))
        result = deriv_line(scale * back, flux_r)
        for i in range(QUAD_POINT_TALLY):
            out[i, slot, rows, :] = result[i] if extra is None else result[i] + additions[i]
    total = None
    for i in range(QUAD_POINT_TALLY):
        block = scratch_s[i]
        from_s = deriv_line(scale * back, [block[rows_of(j)] for j in range(QUAD_POINT_TALLY)])
        from_t = height_product(height_back, scratch_t[i])
        for j in range(QUAD_POINT_TALLY):
            rows = rows_of(j)
            term = from_t[rows] if scale == 1.0 else scale * from_t[rows]
            value = out[i, slot, rows, :] + from_s[j] + term
            out[i, slot, rows, :] = value
            if extra is None:
                term = field[i, slot, rows, :] * value
                total = term if total is None else total + term
    return total


def apply_faces(field, slot, metric, b, scratch_s, scratch_t, faces, matrices, scale=1.0, extra=None):
    both, height_back = matrices[BOTH], matrices[HEIGHT_BACK]
    back = DERIV.T
    even, odd = line_tables(scale * back)
    for i in range(QUAD_POINT_TALLY):
        slopes = height_product(both, field[i, slot])
        scratch_t[i] = slopes[:ROWS]
        scratch_s[i] = slopes[ROWS:]
    for j in range(QUAD_POINT_TALLY):
        rows = rows_of(j)
        along_r = deriv_line(DERIV, [field[i, slot, rows, :] for i in range(QUAD_POINT_TALLY)])
        flux_r = []
        additions = {}
        for i in range(QUAD_POINT_TALLY):
            along_s, along_t = scratch_s[i, rows, :], scratch_t[i, rows, :]
            rr, rs, rt = (metric[n, i, b, rows, :] for n in (0, 3, 4))
            flux_r.append(rr * along_r[i] + rs * along_s + rt * along_t)
            if i in (0, 7):
                ss, tt, st = (metric[n, i, b, rows, :] for n in (1, 2, 5))
                scratch_s[i, rows, :] = rs * along_r[i] + ss * along_s + st * along_t
                scratch_t[i, rows, :] = rt * along_r[i] + st * along_s + tt * along_t
                if extra is not None:
                    additions[i] = extra(i, j, along_r[i], along_s, along_t)
        common = sum(float(odd[0, l]) * (flux_r[l] - flux_r[7 - l]) for l in range(HALF))
        change = sum(float(even[0, l]) * (flux_r[l] + flux_r[7 - l]) for l in range(HALF))
        for n, i in enumerate((0, 7)):
            value = common + change if i == 0 else common - change
            faces[n, slot, rows, :] = value if extra is None else value + additions[i]
    for n, i in enumerate((0, 7)):
        block = scratch_s[i]
        from_s = deriv_line(scale * back, [block[rows_of(j)] for j in range(QUAD_POINT_TALLY)])
        from_t = height_product(height_back, scratch_t[i])
        for j in range(QUAD_POINT_TALLY):
            rows = rows_of(j)
            term = from_t[rows] if scale == 1.0 else scale * from_t[rows]
            faces[n, slot, rows, :] = faces[n, slot, rows, :] + from_s[j] + term


def dot_weighted(left, right, slot):
    layers = left.shape[3]
    sums = {}
    for i in range(QUAD_POINT_TALLY):
        for j in range(QUAD_POINT_TALLY):
            weight = side_weight(i, j)
            term = left[i, slot, rows_of(j), :] * right[i, slot, rows_of(j), :]
            sums[weight] = sums[weight] + term if weight in sums else term
    total = sums[1.0] + 0.5 * sums[0.5] + 0.25 * sums[0.25]
    return total * copy_weights((QUAD_POINT_TALLY, layers))


def mass_faces_kernel(
    determinant, prior, first, second, ends, prior_ends, det_face, det_end, prior_face, prior_end,
    mass_face, mass_end, sems,
):
    blocks, layers = determinant.shape[1], first.shape[2]
    last = blocks - 1
    copies = []
    for n, i in enumerate((0, 7)):
        copies.append((determinant.at[i], det_face.at[n]))
        copies.append((prior.at[i], prior_face.at[n]))
    for n, (b, j) in enumerate(((0, 0), (last, 7))):
        copies.append((determinant.at[:, b, j], det_end.at[n]))
        copies.append((prior.at[:, b, j], prior_end.at[n]))
    started = [
        pltpu.make_async_copy(source, target, sems.at[n])
        for n, (source, target) in enumerate(copies)
    ]
    for copy in started:
        copy.start()
    for copy in started:
        copy.wait()
    weights = height_weights((QUAD_POINT_TALLY, layers))
    for n, i in enumerate((0, 7)):
        for b in range(blocks):
            for j in range(QUAD_POINT_TALLY):
                weight = weights * float(WEIGHTS[i] * WEIGHTS[j])
                value = weight * det_face[n, b, j].astype(jnp.float32)
                mass_face[0, n, b, rows_of(j), :] = value
                mass_face[1, n, b, rows_of(j), :] = value * prior_face[n, b, j]
    for side, j in enumerate((0, 7)):
        for i in range(QUAD_POINT_TALLY):
            weight = weights * float(WEIGHTS[i] * WEIGHTS[j])
            value = weight * det_end[side, i].astype(jnp.float32)
            mass_end[0, 0, side, rows_of(i), :] = value
            mass_end[1, 0, side, rows_of(i), :] = value * prior_end[side, i]
    for n in range(2):
        for b in range(blocks):
            sum_heights(mass_face.at[n], b)
        for side in range(2):
            sum_heights(mass_end.at[n], side)
            for i in range(QUAD_POINT_TALLY):
                (ends, prior_ends)[n][0, side, i] = mass_end[n, 0, side, rows_of(i), :]
        for b in range(blocks - 1):
            for face in range(2):
                total = mass_face[n, face, b, TAIL, :] + mass_face[n, face, b + 1, HEAD, :]
                mass_face[n, face, b, TAIL, :] = total
                mass_face[n, face, b + 1, HEAD, :] = total
        odd, _ = dom_sides()
        face_first = jnp.minimum(odd, 1)
        for b in range(blocks):
            first[n, face_rows(b), :] = mass_face[n, face_first, b]
            second[n, face_rows(b), :] = mass_face[n, 1 - face_first, b]


def prepare_kernel(
    determinant, prior, pure, mixed, matrices, mass, mass_prior, metric, diagonal,
    det_in, prior_in, pure_in, mixed_in, sems,
):
    blocks, layers = diagonal.shape[1], diagonal.shape[3]
    weights = height_weights((QUAD_POINT_TALLY, layers))
    level = lax.broadcasted_iota(jnp.int32, (QUAD_POINT_TALLY, layers), 0)
    ends = [float(DERIV[i, i]) for i in range(QUAD_POINT_TALLY)]
    height_ends = jnp.where(level == 0, ends[0], jnp.where(level == 7, ends[7], 0.0))
    squares = DERIV * DERIV

    def mass_copies(b):
        return (
            pltpu.make_async_copy(determinant.at[:, b], det_in.at[:, b], sems.at[0, b]),
            pltpu.make_async_copy(prior.at[:, b], prior_in.at[:, b], sems.at[1, b]),
        )

    def metric_copies(b):
        return (
            pltpu.make_async_copy(pure.at[:, :, b], pure_in.at[:, :, b], sems.at[2, b]),
            pltpu.make_async_copy(mixed.at[:, :, b], mixed_in.at[:, :, b], sems.at[3, b]),
        )

    for copies in (mass_copies, metric_copies):
        for b in range(blocks):
            for copy in copies(b):
                copy.start()

    def mass_block(b, carry):
        for copy in mass_copies(b):
            copy.wait()
        for i in range(QUAD_POINT_TALLY):
            for j in range(QUAD_POINT_TALLY):
                weight = weights * float(WEIGHTS[i] * WEIGHTS[j])
                value = weight * det_in[i, b, j].astype(jnp.float32)
                mass[i, b, rows_of(j), :] = value
                mass_prior[i, b, rows_of(j), :] = value * prior_in[i, b, j]
        sum_heights(mass, b)
        sum_heights(mass_prior, b)
        return carry

    def metric_block(b, carry):
        for copy in metric_copies(b):
            copy.wait()
        for i in range(QUAD_POINT_TALLY):
            for j in range(QUAD_POINT_TALLY):
                weight = weights * float(WEIGHTS[i] * WEIGHTS[j])
                for n in range(3):
                    metric[n, i, b, rows_of(j), :] = weight * pure_in[n, i, b, j].astype(
                        jnp.float32
                    )
                    metric[n + 3, i, b, rows_of(j), :] = weight * mixed_in[n, i, b, j].astype(
                        jnp.float32
                    )
        for j in range(QUAD_POINT_TALLY):
            line = square_line(
                squares.T, [metric[0, i, b, rows_of(j), :] for i in range(QUAD_POINT_TALLY)]
            )
            for i in range(QUAD_POINT_TALLY):
                diagonal[i, b, rows_of(j), :] = line[i]
        for i in range(QUAD_POINT_TALLY):
            line = square_line(
                squares.T, [metric[1, i, b, rows_of(j), :] for j in range(QUAD_POINT_TALLY)]
            )
            from_t = height_product(matrices[HEIGHT_SQUARE], metric[2, i, b])
            for j in range(QUAD_POINT_TALLY):
                rows = rows_of(j)
                value = diagonal[i, b, rows, :] + line[j] + from_t[rows]
                if ends[i] != 0.0 and ends[j] != 0.0:
                    value = value + (2.0 * ends[i] * ends[j]) * metric[3, i, b, rows, :]
                if ends[i] != 0.0:
                    value = value + (2.0 * ends[i]) * height_ends * metric[4, i, b, rows, :]
                if ends[j] != 0.0:
                    value = value + (2.0 * ends[j]) * height_ends * metric[5, i, b, rows, :]
                diagonal[i, b, rows, :] = value
        sum_heights(diagonal, b)
        return carry

    lax.fori_loop(0, blocks, mass_block, 0)
    lax.fori_loop(0, blocks, metric_block, 0)


def source_kernel(
    metric, heat, wind, determinant, diagonal, matrices,
    numerator, first, second, diag_ends, heat_ends, scratch_s, scratch_t,
):
    blocks, layers = numerator.shape[1], numerator.shape[3]
    weights = height_weights((QUAD_POINT_TALLY, layers))

    def block(b, carry):
        def extra(i, j, along_r, along_s, along_t):
            weight = weights * float(WEIGHTS[i] * WEIGHTS[j])
            convection = (
                wind[0, i, b, j].astype(jnp.float32) * along_r
                + wind[1, i, b, j].astype(jnp.float32) * along_s
                + wind[2, i, b, j].astype(jnp.float32) * along_t
            )
            return weight * (
                determinant[i, b, j].astype(jnp.float32) * heat[i, b, rows_of(j), :]
                - transport_increment * convection
            )

        apply_block(
            heat, b, metric, b, scratch_s, scratch_t, numerator, matrices,
            -conduction_increment, extra,
        )
        sum_heights(numerator, b)
        return carry

    lax.fori_loop(0, blocks, block, 0)
    for n, (field, ends) in enumerate(((diagonal, diag_ends), (numerator, heat_ends))):
        emit_faces(Whole(field), first.at[n], second.at[n])
        emit_ends(Whole(field), ends.at[0])


def ends_kernel(offsets, *refs):
    inputs, (first, second) = refs[: 3 * len(offsets)], refs[3 * len(offsets) :]
    for n, offset in enumerate(offsets):
        ends, *received = inputs[3 * n : 3 * n + 3]
        last = received[0].shape[1] - QUAD_POINT_TALLY
        for side, target in zip(batch_sides(), (first, second)):
            rows = pl.ds(pl.multiple_of(side * last, QUAD_POINT_TALLY), QUAD_POINT_TALLY)
            for i in range(QUAD_POINT_TALLY):
                target[n, i] = ends[0, side, i]
            for dom_side, face in zip(dom_sides(), received):
                target[n, dom_side] = target[n, dom_side] + face[offset, rows, :]


def elements(inner, blocks):
    return list(enumerate(range(1, blocks - 1) if inner else (0, blocks - 1)))


class Sending:
    def __init__(self, sems):
        self.sems, self.copies = sems, []

    def start(self, source, target):
        copy = pltpu.make_async_copy(source, target, self.sems.at[len(self.copies)])
        copy.start()
        self.copies.append(copy)

    def wait(self):
        for copy in self.copies:
            copy.wait()


def start_source(determinant, spread, b):
    layers = spread.shape[3]
    weights = height_weights((QUAD_POINT_TALLY, layers))

    def extra(i, j, along_r, along_s, along_t):
        weight = weights * float(-WEIGHTS[i] * WEIGHTS[j] / step_dt)
        return (weight * determinant[i, b, j].astype(jnp.float32)) * spread[i, b, rows_of(j), :]

    return extra


def assemble_head(mass, mass_prior, dom, batch, keep, slot, b, mass_inverse, head):
    for n, (field, out) in enumerate(((mass, mass_inverse), (mass_prior, head))):
        assemble(
            Whole(field), b, out, slot, tuple(face.at[n] for face in dom),
            batch and tuple(face.at[n] for face in batch),
        )
    clear_top(head, slot, keep, b)
    for i in range(QUAD_POINT_TALLY):
        inverse = 1.0 / mass_inverse[i, slot]
        mass_inverse[i, slot] = inverse
        head[i, slot] = head[i, slot] * inverse


def start_inner_kernel(
    mass, mass_prior, dom_first, dom_second, metric, spread, determinant, keep, matrices,
    head_out, mass_inverse, residual, scratch_s, scratch_t, head, sems,
):
    blocks = mass.shape[1]
    sending = Sending(sems)
    for slot, b in elements(True, blocks):
        assemble_head(
            mass, mass_prior, (dom_first, dom_second), None, keep, slot, b, mass_inverse, head
        )
        sending.start(head.at[:, slot], head_out.at[:, slot])
        apply_block(
            head, slot, metric, b, scratch_s, scratch_t, residual, matrices, -1.0,
            start_source(determinant, spread, b),
        )
        sum_heights(residual, slot)
    sending.wait()


def start_faces_kernel(
    mass, mass_prior, dom_first, dom_second, batch_first, batch_second,
    metric, spread, determinant, keep, matrices, residual_inner,
    head, mass_inverse, first, second, scratch_s, scratch_t, faces,
):
    blocks = mass.shape[1]
    for slot, b in elements(False, blocks):
        assemble_head(
            mass, mass_prior, (dom_first, dom_second), (batch_first, batch_second), keep,
            slot, b, mass_inverse, head,
        )
        apply_faces(
            head, slot, metric, b, scratch_s, scratch_t, faces, matrices, -1.0,
            start_source(determinant, spread, b),
        )
        sum_heights(faces, slot)
    emit_faces(Sides(residual_inner, faces), first.at[0], second.at[0])


def start_ends_kernel(
    head, metric, spread, determinant, matrices, residual_inner,
    head_out, residual, ends, scratch_s, scratch_t, sems,
):
    sending = Sending(sems)
    sending.start(head, head_out)
    for slot, b in elements(False, metric.shape[2]):
        apply_block(
            head, slot, metric, b, scratch_s, scratch_t, residual, matrices, -1.0,
            start_source(determinant, spread, b),
        )
        sum_heights(residual, slot)
    emit_ends(Parts(residual_inner, residual), ends.at[0])
    sending.wait()


def row_sums(*parts):
    rows = [jnp.sum(part, axis=0, keepdims=True) for part in parts]
    rows.append(jnp.zeros((QUAD_POINT_TALLY - len(parts), parts[0].shape[1]), jnp.float32))
    return jnp.concatenate(rows, axis=0)


def assemble_direction(
    residual_parts, diagonal, res_dom, diag_dom, batch, keep, slot, b,
    residual, diag_inverse, direction,
):
    assemble(
        residual_parts, b, residual, slot, tuple(face.at[0] for face in res_dom),
        batch and tuple(face.at[0] for face in batch),
    )
    assemble(
        Whole(diagonal), b, diag_inverse, slot, tuple(face.at[0] for face in diag_dom),
        batch and tuple(face.at[1] for face in batch),
    )
    clear_top(residual, slot, keep, b)
    for i in range(QUAD_POINT_TALLY):
        inverse = 1.0 / diag_inverse[i, slot]
        diag_inverse[i, slot] = inverse
        direction[i, slot] = residual[i, slot] * inverse


def apply_dots(left, field, inner, metric, scratch_s, scratch_t, out, matrices):
    energy = product = 0.0
    for slot, b in elements(inner, metric.shape[2]):
        energy += apply_block(field, slot, metric, b, scratch_s, scratch_t, out, matrices)
        product += dot_weighted(left, field, slot)
        sum_heights(out, slot)
    return product, energy


def first_inner_kernel(
    residual_inner, residual_ends, diagonal, res_first, res_second, diag_first, diag_second,
    metric, keep, matrices,
    direction_out, diag_inverse, image, dots, scratch_s, scratch_t, residual, direction, sems,
):
    sending = Sending(sems)
    for slot, b in elements(True, diagonal.shape[1]):
        assemble_direction(
            Parts(residual_inner, residual_ends), diagonal, (res_first, res_second),
            (diag_first, diag_second), None, keep, slot, b, residual, diag_inverse, direction,
        )
        sending.start(direction.at[:, slot], direction_out.at[:, slot])
    dots[...] = row_sums(
        *apply_dots(residual, direction, True, metric, scratch_s, scratch_t, image, matrices)
    )
    sending.wait()


def first_faces_kernel(
    residual_inner, residual_ends, diagonal, res_first, res_second, diag_first, diag_second,
    batch_first, batch_second, metric, keep, matrices, image_inner,
    direction, residual, diag_inverse, first, second, scratch_s, scratch_t, faces,
):
    for slot, b in elements(False, diagonal.shape[1]):
        assemble_direction(
            Parts(residual_inner, residual_ends), diagonal, (res_first, res_second),
            (diag_first, diag_second), (batch_first, batch_second), keep, slot, b,
            residual, diag_inverse, direction,
        )
        apply_faces(direction, slot, metric, b, scratch_s, scratch_t, faces, matrices)
        sum_heights(faces, slot)
    emit_faces(Sides(image_inner, faces), first.at[0], second.at[0])


def first_ends_kernel(
    direction, residual, metric, matrices, image_inner, dots_inner,
    direction_out, image, ends, dots, scratch_s, scratch_t, sems,
):
    sending = Sending(sems)
    sending.start(direction, direction_out)
    dots[...] = dots_inner[...] + row_sums(
        *apply_dots(residual, direction, False, metric, scratch_s, scratch_t, image, matrices)
    )
    emit_ends(Parts(image_inner, image), ends.at[0])
    sending.wait()


def second_inner_kernel(
    image_inner, image_ends, dom_first, dom_second, diag_inverse, metric, keep, matrices, dots_in,
    scaled_out, image_two, dots, scratch_s, scratch_t, image, scaled, sems,
):
    parts = Parts(image_inner, image_ends)
    sending = Sending(sems)
    for slot, b in elements(True, parts.blocks):
        assemble(parts, b, image, slot, (dom_first.at[0], dom_second.at[0]), None)
        clear_top(image, slot, keep, b)
        for i in range(QUAD_POINT_TALLY):
            scaled[i, slot] = image[i, slot] * diag_inverse[i, slot]
        sending.start(scaled.at[:, slot], scaled_out.at[:, slot])
    product, energy = apply_dots(
        image, scaled, True, metric, scratch_s, scratch_t, image_two, matrices
    )
    nothing = jnp.zeros_like(energy)
    dots[...] = dots_in[...] + row_sums(nothing, nothing, product, energy)
    sending.wait()


def second_ends_kernel(
    image_inner, image_ends, dom_first, dom_second, batch_first, batch_second,
    diag_inverse, metric, keep, matrices, two_inner, dots_in,
    scaled_out, image_two, first, second, ends, all_dots,
    scratch_s, scratch_t, image, scaled, sems,
):
    parts = Parts(image_inner, image_ends)
    sending = Sending(sems)
    for slot, b in elements(False, parts.blocks):
        assemble(
            parts, b, image, slot, (dom_first.at[0], dom_second.at[0]),
            (batch_first.at[0], batch_second.at[0]),
        )
        clear_top(image, slot, keep, b)
        for i in range(QUAD_POINT_TALLY):
            scaled[i, slot] = image[i, slot] * diag_inverse[i, slot]
        sending.start(scaled.at[:, slot], scaled_out.at[:, slot])
    product, energy = apply_dots(
        image, scaled, False, metric, scratch_s, scratch_t, image_two, matrices
    )
    nothing = jnp.zeros_like(energy)
    sums = dots_in[...] + row_sums(nothing, nothing, product, energy)
    for n in range(all_dots.shape[0]):
        all_dots[n] = sums
    emit_faces(Parts(two_inner, image_two), first.at[0], second.at[0])
    emit_ends(Parts(two_inner, image_two), ends.at[0])
    sending.wait()


def heat_kernel(
    numerator, dom_first, dom_second, inverse_inner, inverse_ends, heat, values, factors
):
    blocks = heat.shape[1]
    inverse = Parts(inverse_inner, inverse_ends)
    for b in range(blocks):
        assemble(Whole(numerator), b, heat, b, (dom_first.at[1], dom_second.at[1]), None)
        for i in range(QUAD_POINT_TALLY):
            heat[i, b] = heat[i, b] * inverse.load(i, b, slice(0, ROWS))
    for side, (b, rows) in enumerate(((0, HEAD), (blocks - 1, TAIL))):
        for i in range(QUAD_POINT_TALLY):
            values[side, i] = heat[i, b, rows, :]
            factors[side, i] = inverse.load(i, b, rows)


CHUNK = 1


def last_kernel(
    image_inner, image_ends, dom_first, dom_second, diag_inner, diag_ends, keep, all_dots,
    head_inner, head_ends, direction_inner, direction_ends, scaled_inner, scaled_ends,
    out_head, out_defect, end_values, end_factors,
    image, far, result_head, result_defect, sems_in, sems_out,
):
    sources = (
        head_inner, head_ends, direction_inner, direction_ends, scaled_inner, scaled_ends
    )
    chunks = QUAD_POINT_TALLY // CHUNK
    arriving = []
    for c in range(chunks):
        planes = pl.ds(c * CHUNK, CHUNK)
        arriving.append([
            pltpu.make_async_copy(
                source.at[planes], far.at[n // 2, n % 2, planes], sems_in.at[c, n]
            )
            for n, source in enumerate(sources)
        ])
        for copy in arriving[-1]:
            copy.start()
    parts, inverses = Parts(image_inner, image_ends), Parts(diag_inner, diag_ends)
    blocks, layers = parts.blocks, image.shape[3]
    level = lax.broadcasted_iota(jnp.int32, (QUAD_POINT_TALLY, layers), 0)
    sums = all_dots[0]
    for n in range(1, all_dots.shape[0]):
        sums = sums + all_dots[n]
    sums = jnp.sum(sums, axis=1, keepdims=True)
    inner, energy, cross, energy_two = (sums[n : n + 1] for n in range(4))
    step = inner / energy
    following = step * step * cross - inner
    growth = 1.0 + following / inner
    curvature = growth * growth * energy - 2.0 * growth * step * cross + step * step * energy_two
    step_two = following / curvature
    along_direction = step + step_two * growth
    along_scaled = step * step_two
    whole = slice(0, ROWS)
    for b in range(blocks):
        for i in range(QUAD_POINT_TALLY):
            joined(parts, i, b, image.at[i, b])
        for side, received in zip(dom_sides(), (dom_first, dom_second)):
            image[side, b] = image[side, b] + received[0, face_rows(b), :]
        clear_top(image, b, keep, b)
    leaving = []
    for c in range(chunks):
        planes = pl.ds(c * CHUNK, CHUNK)
        for copy in arriving[c]:
            copy.wait()
        for i in range(c * CHUNK, (c + 1) * CHUNK):
            for b in range(blocks):
                kind, slot = (1, min(b, 1)) if b in (0, blocks - 1) else (0, b - 1)
                start, change = far[1, kind, i, slot], far[2, kind, i, slot]
                inverse = inverses.load(i, b, whole)
                result_head[i, b] = (
                    far[0, kind, i, slot] + along_direction * start - along_scaled * change
                )
                result_defect[i, b] = (
                    start - along_direction * change + along_scaled * (image[i, b] * inverse)
                )
            for side, (b, j) in enumerate(((0, 0), (blocks - 1, 7))):
                end_values[side, i] = result_defect[i, b, rows_of(j), :]
                top = jnp.where(level == 7, keep[i, b, j : j + 1, :], 1.0)
                end_factors[side, i] = along_scaled * top * inverses.load(i, b, rows_of(j))
        for n, (source, target) in enumerate(
            ((result_head, out_head), (result_defect, out_defect))
        ):
            copy = pltpu.make_async_copy(source.at[planes], target.at[planes], sems_out.at[c, n])
            copy.start()
            leaving.append(copy)
    for copy in leaving:
        copy.wait()


def close_kernel(
    defect, heat, batch_first, batch_second, defect_values, defect_factors, heat_values,
    heat_factors, out_defect, out_heat, rows, sems,
):
    del defect, heat
    low, _ = batch_sides()
    copies = []
    for n, (values, factors, out) in enumerate((
        (defect_values, defect_factors, out_defect), (heat_values, heat_factors, out_heat)
    )):
        for side, (b, start) in enumerate(((0, 0), (out.shape[1] - 1, LAST))):
            for i in range(QUAD_POINT_TALLY):
                received = jnp.where(low == side, batch_first[n, i], batch_second[n, i])
                rows[n, side, i] = values[side, i] + factors[side, i] * received
            copy = pltpu.make_async_copy(
                rows.at[n, side], out.at[:, b, pl.ds(start, QUAD_POINT_TALLY), :],
                sems.at[n, side],
            )
            copy.start()
            copies.append(copy)
    for copy in copies:
        copy.wait()


COST = {
    "mass_faces": 2, "prepare": 10, "source": 14, "start_inner": 8, "start_faces": 4,
    "start_ends": 8, "first_inner": 8, "first_faces": 4, "first_ends": 6, "heat": 4,
    "second_inner": 8, "second_ends": 8, "last": 12, "close": 2,
}


def call(kernel, name, outs, args, scratch=(), far_in=(), far_out=(), aliases=None):
    near, far = pl.BlockSpec(memory_space=pltpu.VMEM), pl.BlockSpec(memory_space=pltpu.HBM)
    args = [
        pltpu.with_memory_space_constraint(arg, pltpu.HBM) if n in far_in else arg
        for n, arg in enumerate(args)
    ]
    return pl.pallas_call(
        kernel,
        name=name,
        out_shape=[
            (pltpu.HBM if n in far_out else jax.ShapeDtypeStruct)(shape, jnp.float32)
            for n, shape in enumerate(outs)
        ],
        in_specs=[far if n in far_in else near for n in range(len(args))],
        out_specs=[far if n in far_out else near for n in range(len(outs))],
        scratch_shapes=[
            shape if not isinstance(shape, tuple) else pltpu.VMEM(shape, jnp.float32)
            for shape in scratch
        ],
        input_output_aliases=aliases or {},
        cost_estimate=pl.CostEstimate(
            flops=0, bytes_accessed=COST.get(name, 0) * 1000000, transcendentals=0
        ),
        compiler_params=pltpu.CompilerParams(vmem_limit_bytes=VMEM_LIMIT),
    )(*args)


def swaps(first, second, axis):
    count = lax.axis_size(axis)
    near = [(index, index ^ 1) for index in range(count)]
    far = [(index, (((index + 1) ^ 1) - 1) % count) for index in range(count)]
    second = lax.ppermute(second, axis, far)
    return lax.ppermute(first, axis, near), second


def shards(
    heat_state_element,
    wind_reference_flux,
    geometric_pure_factors,
    geometric_mixed_factors,
    mapping_determinant,
    velocity_source_spread,
    prior_head_state,
    exit_boundary_marks,
):
    _, points, blocks, _, _, layers = heat_state_element.shape
    block_shape = (points, blocks, ROWS, layers)
    inner_shape = (points, blocks - 2, ROWS, layers)
    ends_shape = (points, 2, ROWS, layers)
    heat = heat_state_element.reshape(block_shape)
    spread = velocity_source_spread.reshape(block_shape)
    prior = prior_head_state[0]
    wind, pure, mixed = (
        array.reshape(array.shape[:1] + array.shape[2:])
        for array in (wind_reference_flux, geometric_pure_factors, geometric_mixed_factors)
    )
    determinant = mapping_determinant[0]
    layer = lax.broadcasted_iota(jnp.int32, (points, blocks, points, layers), 3)
    marks = exit_boundary_marks[0].astype(jnp.float32)[:, :, :, None]
    keep = jnp.where(layer == layers - 1, 1.0 - marks, 1.0)
    matrices = constants()

    end_shape = (1, 2, points, points, layers)

    def faces(count):
        return [(count, blocks * LAST + QUAD_POINT_TALLY, layers)] * 2

    def ends_call(name, *groups):
        return call(
            functools.partial(ends_kernel, [group[-1] for group in groups]),
            name,
            [(len(groups), points, points, layers)] * 2,
            [array for group in groups for array in group[:-1]],
        )

    pair = [(points, ROWS, layers)] * 2
    plane = (points, layers)
    side_shape = (2, 2, ROWS, layers)

    *mass_faces, mass_ends, prior_ends = call(
        mass_faces_kernel, "mass_faces", faces(2) + [end_shape] * 2, [determinant, prior],
        [
            pltpu.VMEM((2, blocks, points, points, layers), jnp.bfloat16),
            pltpu.VMEM((2, points, points, layers), jnp.bfloat16),
            (2, blocks, points, points, layers),
            (2, points, points, layers),
            (2, 2, blocks, ROWS, layers),
            (2, 1, 2, ROWS, layers),
            pltpu.SemaphoreType.DMA((8,)),
        ],
        far_in=(0, 1),
    )
    mass_dom = swaps(*mass_faces, "dom")
    mass, mass_prior, metric, diagonal = call(
        prepare_kernel, "prepare", [block_shape] * 2 + [(6,) + block_shape, block_shape],
        [determinant, prior, pure, mixed, matrices],
        [
            pltpu.VMEM(determinant.shape, jnp.bfloat16),
            prior.shape,
            pltpu.VMEM(pure.shape, jnp.bfloat16),
            pltpu.VMEM(mixed.shape, jnp.bfloat16),
            pltpu.SemaphoreType.DMA((4, blocks)),
        ],
        far_in=range(4),
    )
    numerator, *source_faces, diag_end, heat_end = call(
        source_kernel, "source", [block_shape] + faces(2) + [end_shape] * 2,
        [metric, heat, wind, determinant, diagonal, matrices], pair,
    )
    source_dom = swaps(*source_faces, "dom")
    mass_batch = swaps(
        *ends_call("mass_ends", (mass_ends, *mass_dom, 0), (prior_ends, *mass_dom, 1)), "batch"
    )
    sems = pltpu.SemaphoreType.DMA
    common = [metric, spread, determinant]
    head_inner, inverse_inner, residual_inner = call(
        start_inner_kernel, "start_inner", [inner_shape] * 3,
        [mass, mass_prior, *mass_dom, *common, keep, matrices],
        pair + [inner_shape, sems((blocks,))], far_out=(0,),
    )
    head_near, inverse_ends, *res_faces = call(
        start_faces_kernel, "start_faces", [ends_shape] * 2 + faces(1),
        [mass, mass_prior, *mass_dom, *mass_batch, *common, keep, matrices, residual_inner],
        pair + [side_shape],
    )
    res_dom = swaps(*res_faces, "dom")
    head_ends, residual_ends, res_ends = call(
        start_ends_kernel, "start_ends", [ends_shape] * 2 + [end_shape],
        [head_near, *common, matrices, residual_inner], pair + [sems((1,))], far_out=(0,),
    )
    res_batch = swaps(
        *ends_call("res_ends", (res_ends, *res_dom, 0), (diag_end, *source_dom, 0)), "batch"
    )
    residual = [residual_inner, residual_ends, diagonal, *res_dom, *source_dom]
    direction_inner, diag_inner, image_inner, dots_inner = call(
        first_inner_kernel, "first_inner", [inner_shape] * 3 + [plane],
        [*residual, metric, keep, matrices], pair + [inner_shape] * 2 + [sems((blocks,))],
        far_out=(0,),
    )
    direction_near, residual_near, diag_ends, *image_faces = call(
        first_faces_kernel, "first_faces", [ends_shape] * 3 + faces(1),
        [*residual, *res_batch, metric, keep, matrices, image_inner], pair + [side_shape],
    )
    image_dom = swaps(*image_faces, "dom")
    direction_ends, image_ends, image_out, dots = call(
        first_ends_kernel, "first_ends", [ends_shape] * 2 + [end_shape] + [plane],
        [direction_near, residual_near, metric, matrices, image_inner, dots_inner],
        pair + [sems((1,))], far_out=(0,),
    )
    heat_next, heat_values, heat_factors = call(
        heat_kernel, "heat", [block_shape] + [(2, points) + plane] * 2,
        [numerator, *source_dom, inverse_inner, inverse_ends],
    )
    heat_next, image_out = lax.optimization_barrier((heat_next, image_out))
    image_batch = swaps(*ends_call("image_ends", (image_out, *image_dom, 0)), "batch")
    count = lax.axis_size("dom") * lax.axis_size("batch")
    image = [image_inner, image_ends, *image_dom]
    scaled_inner, two_inner, dots = call(
        second_inner_kernel, "second_inner", [inner_shape] * 2 + [plane],
        [*image, diag_inner, metric, keep, matrices, dots],
        pair + [inner_shape] * 2 + [sems((blocks,))], far_out=(0,),
    )
    scaled_ends, two_ends, *two_faces, two_out, all_dots = call(
        second_ends_kernel, "second_ends",
        [ends_shape] * 2 + faces(1) + [end_shape, (count,) + plane],
        [*image, *image_batch, diag_ends, metric, keep, matrices, two_inner, dots],
        pair + [ends_shape] * 2 + [sems((2,))], far_out=(0,),
    )
    all_dots = lax.all_to_all(all_dots, ("dom", "batch"), 0, 0)
    two_dom = swaps(*two_faces, "dom")
    two_batch = swaps(
        *ends_call("two_ends", (two_out, *two_dom, 0), (heat_end, *source_dom, 1)), "batch"
    )
    chunks = points // CHUNK
    head_next, defect, end_values, end_factors = call(
        last_kernel, "last", [block_shape] * 2 + [(2, points) + plane] * 2,
        [two_inner, two_ends, *two_dom, diag_inner, diag_ends, keep, all_dots,
         head_inner, head_ends, direction_inner, direction_ends, scaled_inner, scaled_ends],
        [block_shape, (3, 2) + ends_shape, block_shape, block_shape,
         sems((chunks, 6)), sems((chunks, 2))],
        far_in=range(8, 14), far_out=(0, 1),
    )
    defect, heat_next = call(
        close_kernel, "close", [block_shape] * 2,
        [defect, heat_next, *two_batch, end_values, end_factors, heat_values, heat_factors],
        [(2, 2, points) + plane, sems((2, 2))],
        far_in=(0, 1), far_out=(0, 1), aliases={0: 0, 1: 1},
    )
    shape = heat_state_element.shape
    return heat_next.reshape(shape), head_next.reshape(shape), defect.reshape(shape)


def solution(mesh):
    field = P("dom", None, "batch", None, None, None)
    triple = P(None, "dom", None, "batch", None, None, None)
    return jax.shard_map(
        shards,
        mesh=mesh,
        in_specs=(
            field, triple, triple, triple, field, field, field, P("dom", None, "batch", None),
        ),
        out_specs=(field, field, field),
        check_vma=False,
    )
```

time: 93.9 us -> 71.5 us (0.76)
  local copies, waits for them, and re-layouts: 16.2 us -> 0.03 us
  waiting for transfers between devices: 26 us -> 13.9 us
  Pallas kernels: 20.1 us -> 27.5 us
  starting transfers between devices: 30 us -> 28.8 us
    unnamed x48 -> x12, local copies, waits for them, and re-layouts: 16.2 us -> 0.03 us
    ppermute x18, waiting for transfers between devices: 26 us -> 13.9 us  [the longest x9 13.8 us: swaps(): second = lax.ppermute(second, axis, far)]
    pallas_call x12 -> x18, Pallas kernels: 20.1 us -> 27.5 us  [call(): pl.pallas_call(kernel, name=name, out_shape=[(pltpu.HBM if n in far_out e...]
  transfers between devices with their start and end apart: 19 -> 19, of which waited for: 10 -> 7; matrix products, arithmetic and copies ran while one was open for 0% -> 0% of each run, Pallas kernels for 11% -> 31%
where the time goes in v2:
time: 71.5 us; the launch traced here: 71.3 us
  starting transfers between devices  28.8 us (40%)
  Pallas kernels  27.5 us (38%)
  waiting for transfers between devices  13.9 us (19%)
  between operations  0.91 us (1%)
    pallas_call x18, Pallas kernels, call(): pl.pallas_call(kernel, name=name, out_shape=[(pltpu.HBM if n in far_out e...  27.5 us
    ppermute x9, starting transfers between devices, swaps(): second = lax.ppermute(second, axis, far)  20.7 us
    ppermute x9, waiting for transfers between devices, swaps(): second = lax.ppermute(second, axis, far)  13.8 us
    ppermute x9, starting transfers between devices, swaps(): return (lax.ppermute(first, axis, near), second)  5.26 us
    all_to_all x1, starting transfers between devices, shards(): all_dots = lax.all_to_all(all_dots, ('dom', 'batch'), 0, 0)  2.9 us
  transfers between devices with their start and end apart: 19, of which 7 were waited for; matrix products, arithmetic and copies ran while one was open for 0% of the time, Pallas kernels for 31%

profile of v2, /device:TPU:0, one launch (start us, length us, event | category | flops | bytes accessed | tf_op | source)
XLA Modules:
  0.0 71.3 jit_solution(1940149432407984233)
XLA Ops:
  0.6 1.4 %mass_faces.1 = (f32[2,232,128]{2,1,0:T(8,128)S(1)}, f32[2,232,128]{2,1,0:T(8,128)S(1)}, f32[1,2,8,8,128]{4,3,2,1,0:T(8,128)S(1)}, f32[1,2,8,8,128]{4,3,2,1,0:T(8,128)S(1)}) custom-call(bf16[8,4,8,8,128]{4,3,2,1,0:T(8,128)(2,1)} %bitcast.12, f32[8,4,8,8,128]{4,3,2,1,0:T(8,128)} %bitcast.23), custom_call_target="tpu_custom_call" | custom-call | bytes 2000000 | tf_op jit(solution)/shard_map/mass_faces/pallas_call | solution.py:878
  2.5 3.6 %collective-permute-start.1 = (f32[2,232,128]{2,1,0:T(8,128)S(1)}, f32[2,232,128]{2,1,0:T(8,128)S(1)}, u32[]{:S(2)}, u32[]{:S(2)}) collective-permute-start(f32[2,232,128]{2,1,0:T(8,128)S(1)} %get-tuple-element.70), channel_id=1, source_target_pairs={{0,28},{4,8},{8,4},{12,16},{16,12},{20,24},{24,20},{28,0},{1,29},{... | collective-permute-start | bytes 712712 | tf_op jit(solution)/shard_map/ppermute | solution.py:903
  6.1 4.0 %prepare.1 = (f32[8,4,64,128]{3,2,1,0:T(8,128)S(1)}, f32[8,4,64,128]{3,2,1,0:T(8,128)S(1)}, f32[6,8,4,64,128]{4,3,2,1,0:T(8,128)S(1)}, f32[8,4,64,128]{3,2,1,0:T(8,128)S(1)}) custom-call(bf16[8,4,8,8,128]{4,3,2,1,0:T(8,128)(2,1)} %bitcast.13, f32[8,4,8,8,128]{4,3,2,1,0:T(8,128)} %bitcast.24, bf16[3,8,4,8,8,128]{5,4,3,2,1,0:T(8,128)(2,1)} %bitcast.25, ...), custom_call_target="tpu_custom_call" | custom-call | bytes 10000000 | tf_op jit(solution)/shard_map/prepare/pallas_call | solution.py:878
  10.2 3.6 %source.1 = (f32[8,4,64,128]{3,2,1,0:T(8,128)S(1)}, f32[2,232,128]{2,1,0:T(8,128)S(1)}, f32[2,232,128]{2,1,0:T(8,128)S(1)}, f32[1,2,8,8,128]{4,3,2,1,0:T(8,128)S(1)}, f32[1,2,8,8,128]{4,3,2,1,0:T(8,128)S(1)}) custom-call(f32[6,8,4,64,128]{4,3,2,1,0:T(8,128)S(1)} %get-tuple-element.71.metric, f32[8,4,64,128]{3,2,1,0:T(8,128)S(1)} %bitcast.22, ...), custom_call_target="tpu_custom_call" | custom-call | bytes 14000000 | tf_op jit(solution)/shard_map/source/pallas_call | solution.py:878
  13.9 0.6 collective-permute-start.7
  14.6 1.6 %collective-permute-start.2 = (f32[2,8,8,128]{3,2,1,0:T(8,128)S(1)}, f32[2,8,8,128]{3,2,1,0:T(8,128)S(1)}, u32[]{:S(2)}, u32[]{:S(2)}) collective-permute-start(f32[2,8,8,128]{3,2,1,0:T(8,128)S(1)} %get-tuple-element.75), channel_id=1, source_target_pairs={{0,1},{1,0},{2,3},{3,2},{4,5},{5,4},{6,7},{7,6},{8,9},{9,8},{10,11... | collective-permute-start | bytes 196616 | tf_op jit(solution)/shard_map/ppermute | solution.py:904
  16.2 2.5 %collective-permute-start.3 = (f32[2,8,8,128]{3,2,1,0:T(8,128)S(1)}, f32[2,8,8,128]{3,2,1,0:T(8,128)S(1)}, u32[]{:S(2)}, u32[]{:S(2)}) collective-permute-start(f32[2,8,8,128]{3,2,1,0:T(8,128)S(1)} %get-tuple-element.76), channel_id=1, source_target_pairs={{0,3},{1,2},{2,1},{3,0},{4,7},{5,6},{6,5},{7,4},{8,11},{9,10},{10,... | collective-permute-start | bytes 196616 | tf_op jit(solution)/shard_map/ppermute | solution.py:903
  18.8 1.6 %start_inner.1 = (f32[8,2,64,128]{3,2,1,0:T(8,128)}, f32[8,2,64,128]{3,2,1,0:T(8,128)S(1)}, f32[8,2,64,128]{3,2,1,0:T(8,128)S(1)}) custom-call(f32[8,4,64,128]{3,2,1,0:T(8,128)S(1)} %get-tuple-element.67.mass, f32[8,4,64,128]{3,2,1,0:T(8,128)S(1)} %get-tuple-element.68.mass_prior, f32[2,232,128]{2,1,0:T(8,128)S(1)} %collective-permute-done.dom_first.refs_1_.refs_4_, ...), custom_call_target="tpu_custom_call" | custom-call | bytes 8000000 | tf_op jit(solution)/shard_map/start_inner/pallas_call | solution.py:878
  20.4 2.0 %collective-permute-done.3.batch_second = f32[2,8,8,128]{3,2,1,0:T(8,128)S(1)} collective-permute-done((f32[2,8,8,128]{3,2,1,0:T(8,128)S(1)}, f32[2,8,8,128]{3,2,1,0:T(8,128)S(1)}, u32[]{:S(2)}, u32[]{:S(2)}) %collective-permute-start.3) | collective-permute-done | bytes 65568 | tf_op jit(solution)/shard_map/ppermute | solution.py:903
  22.4 1.1 %start_faces.1 = (f32[8,2,64,128]{3,2,1,0:T(8,128)S(1)}, f32[8,2,64,128]{3,2,1,0:T(8,128)S(1)}, f32[1,232,128]{2,1,0:T(8,128)S(1)}, f32[1,232,128]{2,1,0:T(8,128)S(1)}) custom-call(f32[8,4,64,128]{3,2,1,0:T(8,128)S(1)} %get-tuple-element.67.mass, f32[8,4,64,128]{3,2,1,0:T(8,128)S(1)} %get-tuple-element.68.mass_prior, ...), custom_call_target="tpu_custom_call" | custom-call | bytes 4000000 | tf_op jit(solution)/shard_map/start_faces/pallas_call | solution.py:878
  23.6 2.2 %collective-permute-start.5 = (f32[1,232,128]{2,1,0:T(8,128)S(1)}, f32[1,232,128]{2,1,0:T(8,128)S(1)}, u32[]{:S(2)}, u32[]{:S(2)}) collective-permute-start(f32[1,232,128]{2,1,0:T(8,128)S(1)} %get-tuple-element.81), channel_id=1, source_target_pairs={{0,28},{4,8},{8,4},{12,16},{16,12},{20,24},{24,20},{28,0},{1,29},{... | collective-permute-start | bytes 356360 | tf_op jit(solution)/shard_map/ppermute | solution.py:903
  25.8 2.3 %start_ends.1 = (f32[8,2,64,128]{3,2,1,0:T(8,128)}, f32[8,2,64,128]{3,2,1,0:T(8,128)S(1)}, f32[1,2,8,8,128]{4,3,2,1,0:T(8,128)S(1)}) custom-call(f32[8,2,64,128]{3,2,1,0:T(8,128)S(1)} %get-tuple-element.77.head, f32[6,8,4,64,128]{4,3,2,1,0:T(8,128)S(1)} %get-tuple-element.71.metric, f32[8,4,64,128]{3,2,1,0:T(8,128)S(1)} %bitcast.20, ...), custom_call_target="tpu_custom_call" | custom-call | bytes 8000000 | tf_op jit(solution)/shard_map/start_ends/pallas_call | solution.py:878
  28.1 1.9 %collective-permute-done.5.res_second.refs_2_ = f32[1,232,128]{2,1,0:T(8,128)S(1)} collective-permute-done((f32[1,232,128]{2,1,0:T(8,128)S(1)}, f32[1,232,128]{2,1,0:T(8,128)S(1)}, u32[]{:S(2)}, u32[]{:S(2)}) %collective-permute-start.5) | collective-permute-done | bytes 118816 | tf_op jit(solution)/shard_map/ppermute | solution.py:903
  30.3 3.0 %collective-permute-start.9 = (f32[2,8,8,128]{3,2,1,0:T(8,128)S(1)}, f32[2,8,8,128]{3,2,1,0:T(8,128)S(1)}, u32[]{:S(2)}, u32[]{:S(2)}) collective-permute-start(f32[2,8,8,128]{3,2,1,0:T(8,128)S(1)} %get-tuple-element.88), channel_id=1, source_target_pairs={{0,3},{1,2},{2,1},{3,0},{4,7},{5,6},{6,5},{7,4},{8,11},{9,10},{10,... | collective-permute-start | bytes 196616 | tf_op jit(solution)/shard_map/ppermute | solution.py:903
  33.2 2.1 %first_inner.1 = (f32[8,2,64,128]{3,2,1,0:T(8,128)}, f32[8,2,64,128]{3,2,1,0:T(8,128)S(1)}, f32[8,2,64,128]{3,2,1,0:T(8,128)S(1)}, f32[8,128]{1,0:T(8,128)S(1)}) custom-call(f32[8,2,64,128]{3,2,1,0:T(8,128)S(1)} %get-tuple-element.72.residual_inner, f32[8,2,64,128]{3,2,1,0:T(8,128)S(1)} %get-tuple-element.78.residual_ends, ...), custom_call_target="tpu_custom_call" | custom-call | bytes 8000000 | tf_op jit(solution)/shard_map/first_inner/pallas_call | solution.py:878
  35.4 1.0 %collective-permute-done.9.batch_second = f32[2,8,8,128]{3,2,1,0:T(8,128)S(1)} collective-permute-done((f32[2,8,8,128]{3,2,1,0:T(8,128)S(1)}, f32[2,8,8,128]{3,2,1,0:T(8,128)S(1)}, u32[]{:S(2)}, u32[]{:S(2)}) %collective-permute-start.9) | collective-permute-done | bytes 65568 | tf_op jit(solution)/shard_map/ppermute | solution.py:903
  36.4 1.1 %first_faces.1 = (f32[8,2,64,128]{3,2,1,0:T(8,128)S(1)}, f32[8,2,64,128]{3,2,1,0:T(8,128)S(1)}, f32[8,2,64,128]{3,2,1,0:T(8,128)S(1)}, f32[1,232,128]{2,1,0:T(8,128)S(1)}, f32[1,232,128]{2,1,0:T(8,128)S(1)}) custom-call(f32[8,2,64,128]{3,2,1,0:T(8,128)S(1)} %get-tuple-element.72.residual_inner, f32[8,2,64,128]{3,2,1,0:T(8,128)S(1)} %get-tuple-element.78.residual_ends, ...), custom_call_target="tpu_custom_call" | custom-call | bytes 4000000 | tf_op jit(solution)/shard_map/first_faces/pallas_call | solution.py:878
  37.5 1.8 %collective-permute-start.11 = (f32[1,232,128]{2,1,0:T(8,128)S(1)}, f32[1,232,128]{2,1,0:T(8,128)S(1)}, u32[]{:S(2)}, u32[]{:S(2)}) collective-permute-start(f32[1,232,128]{2,1,0:T(8,128)S(1)} %get-tuple-element.94), channel_id=1, source_target_pairs={{0,28},{4,8},{8,4},{12,16},{16,12},{20,24},{24,20},{28,0},{1,29},{... | collective-permute-start | bytes 356360 | tf_op jit(solution)/shard_map/ppermute | solution.py:903
  39.3 1.2 %heat.1 = (f32[8,4,64,128]{3,2,1,0:T(8,128)}, f32[2,8,8,128]{3,2,1,0:T(8,128)S(1)}, f32[2,8,8,128]{3,2,1,0:T(8,128)S(1)}) custom-call(f32[8,4,64,128]{3,2,1,0:T(8,128)S(1)} %get-tuple-element.98.numerator, f32[2,232,128]{2,1,0:T(8,128)S(1)} %collective-permute-done.6.diag_first.refs_4_.dom_first, ...), custom_call_target="tpu_custom_call" | custom-call | bytes 4000000 | tf_op jit(solution)/shard_map/heat/pallas_call | solution.py:878
  40.5 1.5 %first_ends.1 = (f32[8,2,64,128]{3,2,1,0:T(8,128)}, f32[8,2,64,128]{3,2,1,0:T(8,128)S(1)}, f32[1,2,8,8,128]{4,3,2,1,0:T(8,128)S(1)}, f32[8,128]{1,0:T(8,128)S(1)}) custom-call(f32[8,2,64,128]{3,2,1,0:T(8,128)S(1)} %get-tuple-element.89.direction, f32[8,2,64,128]{3,2,1,0:T(8,128)S(1)} %get-tuple-element.90.residual, ...), custom_call_target="tpu_custom_call" | custom-call | bytes 6000000 | tf_op jit(solution)/shard_map/first_ends/pallas_call | solution.py:878
  42.0 1.9 %collective-permute-done.11.dom_second.refs_2_ = f32[1,232,128]{2,1,0:T(8,128)S(1)} collective-permute-done((f32[1,232,128]{2,1,0:T(8,128)S(1)}, f32[1,232,128]{2,1,0:T(8,128)S(1)}, u32[]{:S(2)}, u32[]{:S(2)}) %collective-permute-start.11) | collective-permute-done | bytes 118816 | tf_op jit(solution)/shard_map/ppermute | solution.py:903
  44.4 2.2 %collective-permute-start.13 = (f32[1,8,8,128]{3,2,1,0:T(8,128)S(1)}, f32[1,8,8,128]{3,2,1,0:T(8,128)S(1)}, u32[]{:S(2)}, u32[]{:S(2)}) collective-permute-start(f32[1,8,8,128]{3,2,1,0:T(8,128)S(1)} %get-tuple-element.105), channel_id=1, source_target_pairs={{0,3},{1,2},{2,1},{3,0},{4,7},{5,6},{6,5},{7,4},{8,11},{9,10},{10,... | collective-permute-start | bytes 98312 | tf_op jit(solution)/shard_map/ppermute | solution.py:903
  46.6 1.5 %second_inner.1 = (f32[8,2,64,128]{3,2,1,0:T(8,128)}, f32[8,2,64,128]{3,2,1,0:T(8,128)S(1)}, f32[8,128]{1,0:T(8,128)S(1)}) custom-call(f32[8,2,64,128]{3,2,1,0:T(8,128)S(1)} %get-tuple-element.84.image_inner, f32[8,2,64,128]{3,2,1,0:T(8,128)S(1)} %get-tuple-element.92.image_ends, f32[1,232,128]{2,1,0:T(8,128)S(1)} %collective-permute-done.10.dom_first.refs_1_, ...), custom_call_target="tpu_custom_call" | custom-call | bytes 8000000 | tf_op jit(solution)/shard_map/second_inner/pallas_call | solution.py:878
  48.1 2.0 %collective-permute-done.13.batch_second = f32[1,8,8,128]{3,2,1,0:T(8,128)S(1)} collective-permute-done((f32[1,8,8,128]{3,2,1,0:T(8,128)S(1)}, f32[1,8,8,128]{3,2,1,0:T(8,128)S(1)}, u32[]{:S(2)}, u32[]{:S(2)}) %collective-permute-start.13) | collective-permute-done | bytes 32800 | tf_op jit(solution)/shard_map/ppermute | solution.py:903
  50.1 2.2 %second_ends.1 = (f32[8,2,64,128]{3,2,1,0:T(8,128)}, f32[8,2,64,128]{3,2,1,0:T(8,128)S(1)}, f32[1,232,128]{2,1,0:T(8,128)}, f32[1,232,128]{2,1,0:T(8,128)S(1)}, ...) custom-call(f32[8,2,64,128]{3,2,1,0:T(8,128)S(1)} %get-tuple-element.84.image_inner, ...), custom_call_target="tpu_custom_call" | custom-call | bytes 8000000 | tf_op jit(solution)/shard_map/second_ends/pallas_call | solution.py:878
  52.3 2.9 %all-to-all-start = ((f32[32,8,128]{2,1,0:T(8,128)}), f32[32,8,128]{2,1,0:T(8,128)S(1)}, u32[]{:S(2)}, u32[]{:S(2)}) async-start(f32[32,8,128]{2,1,0:T(8,128)} %get-tuple-element.111), calls=%async_computation | async-start | bytes 262144 | tf_op jit(solution)/shard_map/all_to_all | solution.py:1040
  55.6 2.5 %collective-permute-start.15 = (f32[1,232,128]{2,1,0:T(8,128)S(1)}, f32[1,232,128]{2,1,0:T(8,128)S(1)}, u32[]{:S(2)}, u32[]{:S(2)}) collective-permute-start(f32[1,232,128]{2,1,0:T(8,128)S(1)} %get-tuple-element.110), channel_id=1, source_target_pairs={{0,28},{4,8},{8,4},{12,16},{16,12},{20,24},{24,20},{28,0},{1,29},{... | collective-permute-start | bytes 356360 | tf_op jit(solution)/shard_map/ppermute | solution.py:903
  58.1 4.4 %collective-permute-done.15.dom_second.refs_2_ = f32[1,232,128]{2,1,0:T(8,128)S(1)} collective-permute-done((f32[1,232,128]{2,1,0:T(8,128)S(1)}, f32[1,232,128]{2,1,0:T(8,128)S(1)}, u32[]{:S(2)}, u32[]{:S(2)}) %collective-permute-start.15) | collective-permute-done | bytes 118816 | tf_op jit(solution)/shard_map/ppermute | solution.py:903
  62.6 1.9 %collective-permute-start.16 = (f32[2,8,8,128]{3,2,1,0:T(8,128)S(1)}, f32[2,8,8,128]{3,2,1,0:T(8,128)S(1)}, u32[]{:S(2)}, u32[]{:S(2)}) collective-permute-start(f32[2,8,8,128]{3,2,1,0:T(8,128)S(1)} %get-tuple-element.122), channel_id=1, source_target_pairs={{0,1},{1,0},{2,3},{3,2},{4,5},{5,4},{6,7},{7,6},{8,9},{9,8},{10,11... | collective-permute-start | bytes 196616 | tf_op jit(solution)/shard_map/ppermute | solution.py:904
  64.5 2.3 %collective-permute-start.17 = (f32[2,8,8,128]{3,2,1,0:T(8,128)S(1)}, f32[2,8,8,128]{3,2,1,0:T(8,128)S(1)}, u32[]{:S(2)}, u32[]{:S(2)}) collective-permute-start(f32[2,8,8,128]{3,2,1,0:T(8,128)S(1)} %get-tuple-element.123), channel_id=1, source_target_pairs={{0,3},{1,2},{2,1},{3,0},{4,7},{5,6},{6,5},{7,4},{8,11},{9,10},{10,... | collective-permute-start | bytes 196616 | tf_op jit(solution)/shard_map/ppermute | solution.py:903
  66.8 3.2 %last.1 = (f32[8,4,64,128]{3,2,1,0:T(8,128)}, f32[8,4,64,128]{3,2,1,0:T(8,128)}, f32[2,8,8,128]{3,2,1,0:T(8,128)S(1)}, f32[2,8,8,128]{3,2,1,0:T(8,128)S(1)}) custom-call(f32[8,2,64,128]{3,2,1,0:T(8,128)S(1)} %get-tuple-element.97.two_inner.image_inner, f32[8,2,64,128]{3,2,1,0:T(8,128)S(1)} %get-tuple-element.108.image_ends, ...), custom_call_target="tpu_custom_call" | custom-call | bytes 12000000 | tf_op jit(solution)/shard_map/last/pallas_call | solution.py:878
  70.6 0.7 close.1
  (39 shorter events, 2.5 us)
Async XLA Ops:
  0.6 5.5 %copy-start.1 = (bf16[256,192]{1,0:T(8,128)(2,1)S(1)}, bf16[256,192]{1,0:T(8,128)(2,1)}, u32[]{:S(2)}) copy-start(bf16[256,192]{1,0:T(8,128)(2,1)} %constant.2.clone.matrices) | copy-start | bytes 294916
  2.0 12.5 %collective-permute-start = (f32[2,232,128]{2,1,0:T(8,128)S(1)}, f32[2,232,128]{2,1,0:T(8,128)S(1)}, u32[]{:S(2)}, u32[]{:S(2)}) collective-permute-start(f32[2,232,128]{2,1,0:T(8,128)S(1)} %get-tuple-element.69), channel_id=1, source_target_pairs={{0,4},{4,0},{8,12},{12,8},{16,20},{20,16},{24,28},{28,24},{1,5},{5... | collective-permute-start | bytes 712712 | tf_op jit(solution)/shard_map/ppermute | solution.py:904
  2.5 12.0 %collective-permute-start.1 = (f32[2,232,128]{2,1,0:T(8,128)S(1)}, f32[2,232,128]{2,1,0:T(8,128)S(1)}, u32[]{:S(2)}, u32[]{:S(2)}) collective-permute-start(f32[2,232,128]{2,1,0:T(8,128)S(1)} %get-tuple-element.70), channel_id=1, source_target_pairs={{0,28},{4,8},{8,4},{12,16},{16,12},{20,24},{24,20},{28,0},{1,29},{... | collective-permute-start | bytes 712712 | tf_op jit(solution)/shard_map/ppermute | solution.py:903
  6.1 4.0 %copy-start = (bf16[1,8,4,8,8,128]{5,4,3,2,1,0:T(8,128)(2,1)S(1)}, bf16[1,8,4,8,8,128]{5,4,3,2,1,0:T(8,128)(2,1)}, u32[]{:S(2)}) copy-start(bf16[1,8,4,8,8,128]{5,4,3,2,1,0:T(8,128)(2,1)} %param.13) | copy-start | bytes 1572868
  6.1 4.0 %copy-start.3 = (bf16[3,1,8,4,8,8,128]{6,5,4,3,2,1,0:T(8,128)(2,1)S(1)}, bf16[3,1,8,4,8,8,128]{6,5,4,3,2,1,0:T(8,128)(2,1)}, u32[]{:S(2)}) copy-start(bf16[3,1,8,4,8,8,128]{6,5,4,3,2,1,0:T(8,128)(2,1)} %param.10) | copy-start | bytes 4718596
  6.1 4.0 %copy-start.4 = (f32[1,8,4,8,8,128]{5,4,3,2,1,0:T(8,128)S(1)}, f32[1,8,4,8,8,128]{5,4,3,2,1,0:T(8,128)}, u32[]{:S(2)}) copy-start(f32[1,8,4,8,8,128]{5,4,3,2,1,0:T(8,128)} %param.9) | copy-start | bytes 3145732
  10.1 4.4 %copy-start.5 = (s32[1,8,4,8]{3,2,1,0:T(4,128)S(1)}, s32[1,8,4,8]{3,2,1,0:T(4,128)}, u32[]{:S(2)}) copy-start(s32[1,8,4,8]{3,2,1,0:T(4,128)} %param.16) | copy-start | bytes 3076
  13.8 5.0 %copy-start.2 = (f32[1,8,4,8,8,128]{5,4,3,2,1,0:T(8,128)S(1)}, f32[1,8,4,8,8,128]{5,4,3,2,1,0:T(8,128)}, u32[]{:S(2)}) copy-start(f32[1,8,4,8,8,128]{5,4,3,2,1,0:T(8,128)} %param.14) | copy-start | bytes 3145732
  13.8 14.3 %collective-permute-start.6 = (f32[2,232,128]{2,1,0:T(8,128)S(1)}, f32[2,232,128]{2,1,0:T(8,128)S(1)}, u32[]{:S(2)}, u32[]{:S(2)}) collective-permute-start(f32[2,232,128]{2,1,0:T(8,128)S(1)} %get-tuple-element.82), channel_id=1, source_target_pairs={{0,4},{4,0},{8,12},{12,8},{16,20},{20,16},{24,28},{28,24},{1,5},{5... | collective-permute-start | bytes 712712 | tf_op jit(solution)/shard_map/ppermute | solution.py:904
  13.9 14.2 %collective-permute-start.7 = (f32[2,232,128]{2,1,0:T(8,128)S(1)}, f32[2,232,128]{2,1,0:T(8,128)S(1)}, u32[]{:S(2)}, u32[]{:S(2)}) collective-permute-start(f32[2,232,128]{2,1,0:T(8,128)S(1)} %get-tuple-element.83), channel_id=1, source_target_pairs={{0,28},{4,8},{8,4},{12,16},{16,12},{20,24},{24,20},{28,0},{1,29},{... | collective-permute-start | bytes 712712 | tf_op jit(solution)/shard_map/ppermute | solution.py:903
  14.6 5.8 %collective-permute-start.2 = (f32[2,8,8,128]{3,2,1,0:T(8,128)S(1)}, f32[2,8,8,128]{3,2,1,0:T(8,128)S(1)}, u32[]{:S(2)}, u32[]{:S(2)}) collective-permute-start(f32[2,8,8,128]{3,2,1,0:T(8,128)S(1)} %get-tuple-element.75), channel_id=1, source_target_pairs={{0,1},{1,0},{2,3},{3,2},{4,5},{5,4},{6,7},{7,6},{8,9},{9,8},{10,11... | collective-permute-start | bytes 196616 | tf_op jit(solution)/shard_map/ppermute | solution.py:904
  16.2 6.2 %collective-permute-start.3 = (f32[2,8,8,128]{3,2,1,0:T(8,128)S(1)}, f32[2,8,8,128]{3,2,1,0:T(8,128)S(1)}, u32[]{:S(2)}, u32[]{:S(2)}) collective-permute-start(f32[2,8,8,128]{3,2,1,0:T(8,128)S(1)} %get-tuple-element.76), channel_id=1, source_target_pairs={{0,3},{1,2},{2,1},{3,0},{4,7},{5,6},{6,5},{7,4},{8,11},{9,10},{10,... | collective-permute-start | bytes 196616 | tf_op jit(solution)/shard_map/ppermute | solution.py:903
  23.5 4.5 %collective-permute-start.4 = (f32[1,232,128]{2,1,0:T(8,128)S(1)}, f32[1,232,128]{2,1,0:T(8,128)S(1)}, u32[]{:S(2)}, u32[]{:S(2)}) collective-permute-start(f32[1,232,128]{2,1,0:T(8,128)S(1)} %get-tuple-element.80), channel_id=1, source_target_pairs={{0,4},{4,0},{8,12},{12,8},{16,20},{20,16},{24,28},{28,24},{1,5},{5... | collective-permute-start | bytes 356360 | tf_op jit(solution)/shard_map/ppermute | solution.py:904
  23.6 6.4 %collective-permute-start.5 = (f32[1,232,128]{2,1,0:T(8,128)S(1)}, f32[1,232,128]{2,1,0:T(8,128)S(1)}, u32[]{:S(2)}, u32[]{:S(2)}) collective-permute-start(f32[1,232,128]{2,1,0:T(8,128)S(1)} %get-tuple-element.81), channel_id=1, source_target_pairs={{0,28},{4,8},{8,4},{12,16},{16,12},{20,24},{24,20},{28,0},{1,29},{... | collective-permute-start | bytes 356360 | tf_op jit(solution)/shard_map/ppermute | solution.py:903
  30.0 5.4 %collective-permute-start.8 = (f32[2,8,8,128]{3,2,1,0:T(8,128)S(1)}, f32[2,8,8,128]{3,2,1,0:T(8,128)S(1)}, u32[]{:S(2)}, u32[]{:S(2)}) collective-permute-start(f32[2,8,8,128]{3,2,1,0:T(8,128)S(1)} %get-tuple-element.87), channel_id=1, source_target_pairs={{0,1},{1,0},{2,3},{3,2},{4,5},{5,4},{6,7},{7,6},{8,9},{9,8},{10,11... | collective-permute-start | bytes 196616 | tf_op jit(solution)/shard_map/ppermute | solution.py:904
  30.3 6.2 %collective-permute-start.9 = (f32[2,8,8,128]{3,2,1,0:T(8,128)S(1)}, f32[2,8,8,128]{3,2,1,0:T(8,128)S(1)}, u32[]{:S(2)}, u32[]{:S(2)}) collective-permute-start(f32[2,8,8,128]{3,2,1,0:T(8,128)S(1)} %get-tuple-element.88), channel_id=1, source_target_pairs={{0,3},{1,2},{2,1},{3,0},{4,7},{5,6},{6,5},{7,4},{8,11},{9,10},{10,... | collective-permute-start | bytes 196616 | tf_op jit(solution)/shard_map/ppermute | solution.py:903
  37.5 4.5 %collective-permute-start.10 = (f32[1,232,128]{2,1,0:T(8,128)S(1)}, f32[1,232,128]{2,1,0:T(8,128)S(1)}, u32[]{:S(2)}, u32[]{:S(2)}) collective-permute-start(f32[1,232,128]{2,1,0:T(8,128)S(1)} %get-tuple-element.93), channel_id=1, source_target_pairs={{0,4},{4,0},{8,12},{12,8},{16,20},{20,16},{24,28},{28,24},{1,5},{5... | collective-permute-start | bytes 356360 | tf_op jit(solution)/shard_map/ppermute | solution.py:904
  37.5 6.4 %collective-permute-start.11 = (f32[1,232,128]{2,1,0:T(8,128)S(1)}, f32[1,232,128]{2,1,0:T(8,128)S(1)}, u32[]{:S(2)}, u32[]{:S(2)}) collective-permute-start(f32[1,232,128]{2,1,0:T(8,128)S(1)} %get-tuple-element.94), channel_id=1, source_target_pairs={{0,28},{4,8},{8,4},{12,16},{16,12},{20,24},{24,20},{28,0},{1,29},{... | collective-permute-start | bytes 356360 | tf_op jit(solution)/shard_map/ppermute | solution.py:903
  44.0 4.2 %collective-permute-start.12 = (f32[1,8,8,128]{3,2,1,0:T(8,128)S(1)}, f32[1,8,8,128]{3,2,1,0:T(8,128)S(1)}, u32[]{:S(2)}, u32[]{:S(2)}) collective-permute-start(f32[1,8,8,128]{3,2,1,0:T(8,128)S(1)} %get-tuple-element.104), channel_id=1, source_target_pairs={{0,1},{1,0},{2,3},{3,2},{4,5},{5,4},{6,7},{7,6},{8,9},{9,8},{10,11... | collective-permute-start | bytes 98312 | tf_op jit(solution)/shard_map/ppermute | solution.py:904
  44.4 5.7 %collective-permute-start.13 = (f32[1,8,8,128]{3,2,1,0:T(8,128)S(1)}, f32[1,8,8,128]{3,2,1,0:T(8,128)S(1)}, u32[]{:S(2)}, u32[]{:S(2)}) collective-permute-start(f32[1,8,8,128]{3,2,1,0:T(8,128)S(1)} %get-tuple-element.105), channel_id=1, source_target_pairs={{0,3},{1,2},{2,1},{3,0},{4,7},{5,6},{6,5},{7,4},{8,11},{9,10},{10,... | collective-permute-start | bytes 98312 | tf_op jit(solution)/shard_map/ppermute | solution.py:903
  52.3 14.5 %all-to-all-start = ((f32[32,8,128]{2,1,0:T(8,128)}), f32[32,8,128]{2,1,0:T(8,128)S(1)}, u32[]{:S(2)}, u32[]{:S(2)}) async-start(f32[32,8,128]{2,1,0:T(8,128)} %get-tuple-element.111), calls=%async_computation | async-start | bytes 262144 | tf_op jit(solution)/shard_map/all_to_all | solution.py:1040
  55.3 2.9 %collective-permute-start.14 = (f32[1,232,128]{2,1,0:T(8,128)}, f32[1,232,128]{2,1,0:T(8,128)S(1)}, u32[]{:S(2)}, u32[]{:S(2)}) collective-permute-start(f32[1,232,128]{2,1,0:T(8,128)} %get-tuple-element.109), channel_id=1, source_target_pairs={{0,4},{4,0},{8,12},{12,8},{16,20},{20,16},{24,28},{28,24},{1,5},{5... | collective-permute-start | bytes 356360 | tf_op jit(solution)/shard_map/ppermute | solution.py:904
  55.6 7.0 %collective-permute-start.15 = (f32[1,232,128]{2,1,0:T(8,128)S(1)}, f32[1,232,128]{2,1,0:T(8,128)S(1)}, u32[]{:S(2)}, u32[]{:S(2)}) collective-permute-start(f32[1,232,128]{2,1,0:T(8,128)S(1)} %get-tuple-element.110), channel_id=1, source_target_pairs={{0,28},{4,8},{8,4},{12,16},{16,12},{20,24},{24,20},{28,0},{1,29},{... | collective-permute-start | bytes 356360 | tf_op jit(solution)/shard_map/ppermute | solution.py:903
  62.6 7.5 %collective-permute-start.16 = (f32[2,8,8,128]{3,2,1,0:T(8,128)S(1)}, f32[2,8,8,128]{3,2,1,0:T(8,128)S(1)}, u32[]{:S(2)}, u32[]{:S(2)}) collective-permute-start(f32[2,8,8,128]{3,2,1,0:T(8,128)S(1)} %get-tuple-element.122), channel_id=1, source_target_pairs={{0,1},{1,0},{2,3},{3,2},{4,5},{5,4},{6,7},{7,6},{8,9},{9,8},{10,11... | collective-permute-start | bytes 196616 | tf_op jit(solution)/shard_map/ppermute | solution.py:904
  64.5 6.1 %collective-permute-start.17 = (f32[2,8,8,128]{3,2,1,0:T(8,128)S(1)}, f32[2,8,8,128]{3,2,1,0:T(8,128)S(1)}, u32[]{:S(2)}, u32[]{:S(2)}) collective-permute-start(f32[2,8,8,128]{3,2,1,0:T(8,128)S(1)} %get-tuple-element.123), channel_id=1, source_target_pairs={{0,3},{1,2},{2,1},{3,0},{4,7},{5,6},{6,5},{7,4},{8,11},{9,10},{10,... | collective-permute-start | bytes 196616 | tf_op jit(solution)/shard_map/ppermute | solution.py:903

commit v3 on v2

--- a/solution.py
+++ b/solution.py
@@ -195,13 +195,6 @@
         return field[i, slot, rows, :]
 
 
-class Sides(Parts):
-    def load(self, i, b, rows):
-        field, slot = self.at(b)
-        plane = jnp.minimum(i, 1) if b in (0, self.blocks - 1) else i
-        return field[plane, slot, rows, :]
-
-
 class Whole:
     def __init__(self, field):
         self.field, self.blocks = field, field.shape[1]
@@ -218,10 +211,13 @@
         out[TAIL, :] = out[TAIL, :] + parts.load(i, b + 1, HEAD)
 
 
-def emit_faces(parts, first, second):
-    for side, target in zip(dom_sides(), (first, second)):
+def emit_faces(parts, first, second, corner, n=0):
+    for side, face in zip(dom_sides(), (first, second)):
         for b in range(parts.blocks):
-            joined(parts, side, b, target.at[face_rows(b)])
+            joined(parts, side, b, face.at[n, face_rows(b)])
+    _, side = dom_sides()
+    corner[n, rows_of(0), :] = parts.load(side, 0, HEAD)
+    corner[n, rows_of(1), :] = parts.load(side, parts.blocks - 1, TAIL)
 
 
 def emit_ends(parts, ends):
@@ -289,44 +285,6 @@
     return total
 
 
-def apply_faces(field, slot, metric, b, scratch_s, scratch_t, faces, matrices, scale=1.0, extra=None):
-    both, height_back = matrices[BOTH], matrices[HEIGHT_BACK]
-    back = DERIV.T
-    even, odd = line_tables(scale * back)
-    for i in range(QUAD_POINT_TALLY):
-        slopes = height_product(both, field[i, slot])
-        scratch_t[i] = slopes[:ROWS]
-        scratch_s[i] = slopes[ROWS:]
-    for j in range(QUAD_POINT_TALLY):
-        rows = rows_of(j)
-        along_r = deriv_line(DERIV, [field[i, slot, rows, :] for i in range(QUAD_POINT_TALLY)])
-        flux_r = []
-        additions = {}
-        for i in range(QUAD_POINT_TALLY):
-            along_s, along_t = scratch_s[i, rows, :], scratch_t[i, rows, :]
-            rr, rs, rt = (metric[n, i, b, rows, :] for n in (0, 3, 4))
-            flux_r.append(rr * along_r[i] + rs * along_s + rt * along_t)
-            if i in (0, 7):
-                ss, tt, st = (metric[n, i, b, rows, :] for n in (1, 2, 5))
-                scratch_s[i, rows, :] = rs * along_r[i] + ss * along_s + st * along_t
-                scratch_t[i, rows, :] = rt * along_r[i] + st * along_s + tt * along_t
-                if extra is not None:
-                    additions[i] = extra(i, j, along_r[i], along_s, along_t)
-        common = sum(float(odd[0, l]) * (flux_r[l] - flux_r[7 - l]) for l in range(HALF))
-        change = sum(float(even[0, l]) * (flux_r[l] + flux_r[7 - l]) for l in range(HALF))
-        for n, i in enumerate((0, 7)):
-            value = common + change if i == 0 else common - change
-            faces[n, slot, rows, :] = value if extra is None else value + additions[i]
-    for n, i in enumerate((0, 7)):
-        block = scratch_s[i]
-        from_s = deriv_line(scale * back, [block[rows_of(j)] for j in range(QUAD_POINT_TALLY)])
-        from_t = height_product(height_back, scratch_t[i])
-        for j in range(QUAD_POINT_TALLY):
-            rows = rows_of(j)
-            term = from_t[rows] if scale == 1.0 else scale * from_t[rows]
-            faces[n, slot, rows, :] = faces[n, slot, rows, :] + from_s[j] + term
-
-
 def dot_weighted(left, right, slot):
     layers = left.shape[3]
     sums = {}
@@ -340,7 +298,7 @@
 
 
 def mass_faces_kernel(
-    determinant, prior, first, second, ends, prior_ends, det_face, det_end, prior_face, prior_end,
+    determinant, prior, first, second, corner, ends, prior_ends, sides, planes, det_face, det_end, prior_face, prior_end,
     mass_face, mass_end, sems,
 ):
     blocks, layers = determinant.shape[1], first.shape[2]
@@ -361,6 +319,11 @@
     for copy in started:
         copy.wait()
     weights = height_weights((QUAD_POINT_TALLY, layers))
+    tile = (QUAD_POINT_TALLY, layers)
+    for n, (end, plane) in enumerate(zip(batch_sides(), dom_sides())):
+        sides[n] = jnp.full(tile, end.astype(jnp.float32))
+        for i in range(QUAD_POINT_TALLY):
+            planes[n, i] = jnp.full(tile, (plane == i).astype(jnp.float32))
     for n, i in enumerate((0, 7)):
         for b in range(blocks):
             for j in range(QUAD_POINT_TALLY):
@@ -391,6 +354,8 @@
         for b in range(blocks):
             first[n, face_rows(b), :] = mass_face[n, face_first, b]
             second[n, face_rows(b), :] = mass_face[n, 1 - face_first, b]
+        corner[n, rows_of(0), :] = mass_face[n, 1 - face_first, 0, HEAD, :]
+        corner[n, rows_of(1), :] = mass_face[n, 1 - face_first, last, TAIL, :]
 
 
 def prepare_kernel(
@@ -477,7 +442,7 @@
 
 def source_kernel(
     metric, heat, wind, determinant, diagonal, matrices,
-    numerator, first, second, diag_ends, heat_ends, scratch_s, scratch_t,
+    numerator, first, second, corner, diag_ends, heat_ends, scratch_s, scratch_t,
 ):
     blocks, layers = numerator.shape[1], numerator.shape[3]
     weights = height_weights((QUAD_POINT_TALLY, layers))
@@ -504,7 +469,7 @@
 
     lax.fori_loop(0, blocks, block, 0)
     for n, (field, ends) in enumerate(((diagonal, diag_ends), (numerator, heat_ends))):
-        emit_faces(Whole(field), first.at[n], second.at[n])
+        emit_faces(Whole(field), first, second, corner, n)
         emit_ends(Whole(field), ends.at[0])
 
 
@@ -512,12 +477,12 @@
     inputs, (first, second) = refs[: 3 * len(offsets)], refs[3 * len(offsets) :]
     for n, offset in enumerate(offsets):
         ends, *received = inputs[3 * n : 3 * n + 3]
-        last = received[0].shape[1] - QUAD_POINT_TALLY
+        lasts = [face.shape[1] - QUAD_POINT_TALLY for face in received]
         for side, target in zip(batch_sides(), (first, second)):
-            rows = pl.ds(pl.multiple_of(side * last, QUAD_POINT_TALLY), QUAD_POINT_TALLY)
             for i in range(QUAD_POINT_TALLY):
                 target[n, i] = ends[0, side, i]
-            for dom_side, face in zip(dom_sides(), received):
+            for dom_side, face, last in zip(dom_sides(), received, lasts):
+                rows = pl.ds(pl.multiple_of(side * last, QUAD_POINT_TALLY), QUAD_POINT_TALLY)
                 target[n, dom_side] = target[n, dom_side] + face[offset, rows, :]
 
 
@@ -582,38 +547,28 @@
     sending.wait()
 
 
-def start_faces_kernel(
+def start_ends_kernel(
     mass, mass_prior, dom_first, dom_second, batch_first, batch_second,
     metric, spread, determinant, keep, matrices, residual_inner,
-    head, mass_inverse, first, second, scratch_s, scratch_t, faces,
+    head_out, mass_inverse, residual, first, second, corner, ends,
+    scratch_s, scratch_t, head, sems,
 ):
     blocks = mass.shape[1]
+    sending = Sending(sems)
     for slot, b in elements(False, blocks):
         assemble_head(
             mass, mass_prior, (dom_first, dom_second), (batch_first, batch_second), keep,
             slot, b, mass_inverse, head,
         )
-        apply_faces(
-            head, slot, metric, b, scratch_s, scratch_t, faces, matrices, -1.0,
-            start_source(determinant, spread, b),
-        )
-        sum_heights(faces, slot)
-    emit_faces(Sides(residual_inner, faces), first.at[0], second.at[0])
-
-
-def start_ends_kernel(
-    head, metric, spread, determinant, matrices, residual_inner,
-    head_out, residual, ends, scratch_s, scratch_t, sems,
-):
-    sending = Sending(sems)
-    sending.start(head, head_out)
-    for slot, b in elements(False, metric.shape[2]):
+        sending.start(head.at[:, slot], head_out.at[:, slot])
         apply_block(
             head, slot, metric, b, scratch_s, scratch_t, residual, matrices, -1.0,
             start_source(determinant, spread, b),
         )
         sum_heights(residual, slot)
-    emit_ends(Parts(residual_inner, residual), ends.at[0])
+    parts = Parts(residual_inner, residual)
+    emit_faces(parts, first, second, corner)
+    emit_ends(parts, ends.at[0])
     sending.wait()
 
 
@@ -669,32 +624,26 @@
     sending.wait()
 
 
-def first_faces_kernel(
+def first_ends_kernel(
     residual_inner, residual_ends, diagonal, res_first, res_second, diag_first, diag_second,
-    batch_first, batch_second, metric, keep, matrices, image_inner,
-    direction, residual, diag_inverse, first, second, scratch_s, scratch_t, faces,
-):
+    batch_first, batch_second, metric, keep, matrices, image_inner, dots_inner,
+    direction_out, diag_inverse, image, first, second, corner, ends, dots,
+    scratch_s, scratch_t, residual, direction, sems,
+):
+    sending = Sending(sems)
     for slot, b in elements(False, diagonal.shape[1]):
         assemble_direction(
             Parts(residual_inner, residual_ends), diagonal, (res_first, res_second),
             (diag_first, diag_second), (batch_first, batch_second), keep, slot, b,
             residual, diag_inverse, direction,
         )
-        apply_faces(direction, slot, metric, b, scratch_s, scratch_t, faces, matrices)
-        sum_heights(faces, slot)
-    emit_faces(Sides(image_inner, faces), first.at[0], second.at[0])
-
-
-def first_ends_kernel(
-    direction, residual, metric, matrices, image_inner, dots_inner,
-    direction_out, image, ends, dots, scratch_s, scratch_t, sems,
-):
-    sending = Sending(sems)
-    sending.start(direction, direction_out)
+        sending.start(direction.at[:, slot], direction_out.at[:, slot])
     dots[...] = dots_inner[...] + row_sums(
         *apply_dots(residual, direction, False, metric, scratch_s, scratch_t, image, matrices)
     )
-    emit_ends(Parts(image_inner, image), ends.at[0])
+    parts = Parts(image_inner, image)
+    emit_faces(parts, first, second, corner)
+    emit_ends(parts, ends.at[0])
     sending.wait()
 
 
@@ -721,7 +670,7 @@
 def second_ends_kernel(
     image_inner, image_ends, dom_first, dom_second, batch_first, batch_second,
     diag_inverse, metric, keep, matrices, two_inner, dots_in,
-    scaled_out, image_two, first, second, ends, all_dots,
+    scaled_out, image_two, first, second, corner, ends, all_dots,
     scratch_s, scratch_t, image, scaled, sems,
 ):
     parts = Parts(image_inner, image_ends)
@@ -742,8 +691,9 @@
     sums = dots_in[...] + row_sums(nothing, nothing, product, energy)
     for n in range(all_dots.shape[0]):
         all_dots[n] = sums
-    emit_faces(Parts(two_inner, image_two), first.at[0], second.at[0])
-    emit_ends(Parts(two_inner, image_two), ends.at[0])
+    parts = Parts(two_inner, image_two)
+    emit_faces(parts, first, second, corner)
+    emit_ends(parts, ends.at[0])
     sending.wait()
 
 
@@ -896,12 +846,19 @@
     )(*args)
 
 
+def near_swap(array, axis):
+    count = lax.axis_size(axis)
+    return lax.ppermute(array, axis, [(index, index ^ 1) for index in range(count)])
+
+
+def far_swap(array, axis):
+    count = lax.axis_size(axis)
+    pairs = [(index, (((index + 1) ^ 1) - 1) % count) for index in range(count)]
+    return lax.ppermute(array, axis, pairs)
+
+
 def swaps(first, second, axis):
-    count = lax.axis_size(axis)
-    near = [(index, index ^ 1) for index in range(count)]
-    far = [(index, (((index + 1) ^ 1) - 1) % count) for index in range(count)]
-    second = lax.ppermute(second, axis, far)
-    return lax.ppermute(first, axis, near), second
+    return near_swap(first, axis), far_swap(second, axis)
 
 
 def shards(
@@ -934,22 +891,41 @@
     end_shape = (1, 2, points, points, layers)
 
     def faces(count):
-        return [(count, blocks * LAST + QUAD_POINT_TALLY, layers)] * 2
-
-    def ends_call(name, *groups):
+        face = (count, blocks * LAST + QUAD_POINT_TALLY, layers)
+        return [face] * 2 + [(count, 2 * QUAD_POINT_TALLY, layers)]
+
+    def dom_swaps(first, second, corner):
+        corner = far_swap(corner, "dom")
+        near = near_swap(first, "dom")
+        return (near, far_swap(second, "dom")), (near, corner)
+
+    def ends_call(*groups):
+        results = []
+        for side in range(2):
+            high = sides[side] > 0.0
+            fields = []
+            for ends, *received, place in groups:
+                field = jnp.where(high[None], ends[0, 1], ends[0, 0])
+                for plane_mask, face in zip(planes, received):
+                    tail = face[place, face.shape[1] - points :]
+                    rows = jnp.where(high, tail, face[place, :points])
+                    field = field + plane_mask * rows[None]
+                fields.append(field)
+            results.append(jnp.stack(fields))
+        return results
+
+    def mass_call(ends, *received):
         return call(
-            functools.partial(ends_kernel, [group[-1] for group in groups]),
-            name,
-            [(len(groups), points, points, layers)] * 2,
-            [array for group in groups for array in group[:-1]],
+            functools.partial(ends_kernel, (0, 1)), "mass_ends",
+            [(2, points, points, layers)] * 2, [ends[0], *received, ends[1], *received],
         )
 
     pair = [(points, ROWS, layers)] * 2
     plane = (points, layers)
-    side_shape = (2, 2, ROWS, layers)
-
-    *mass_faces, mass_ends, prior_ends = call(
-        mass_faces_kernel, "mass_faces", faces(2) + [end_shape] * 2, [determinant, prior],
+
+    *mass_faces, mass_end, prior_end, sides, planes = call(
+        mass_faces_kernel, "mass_faces",
+        faces(2) + [end_shape] * 2 + [(2,) + plane, (2, points) + plane], [determinant, prior],
         [
             pltpu.VMEM((2, blocks, points, points, layers), jnp.bfloat16),
             pltpu.VMEM((2, points, points, layers), jnp.bfloat16),
@@ -961,7 +937,7 @@
         ],
         far_in=(0, 1),
     )
-    mass_dom = swaps(*mass_faces, "dom")
+    mass_dom = swaps(*mass_faces[:2], "dom")
     mass, mass_prior, metric, diagonal = call(
         prepare_kernel, "prepare", [block_shape] * 2 + [(6,) + block_shape, block_shape],
         [determinant, prior, pure, mixed, matrices],
@@ -978,9 +954,9 @@
         source_kernel, "source", [block_shape] + faces(2) + [end_shape] * 2,
         [metric, heat, wind, determinant, diagonal, matrices], pair,
     )
-    source_dom = swaps(*source_faces, "dom")
+    source_dom = swaps(*source_faces[:2], "dom")
     mass_batch = swaps(
-        *ends_call("mass_ends", (mass_ends, *mass_dom, 0), (prior_ends, *mass_dom, 1)), "batch"
+        *mass_call((mass_end, prior_end), *mass_dom), "batch"
     )
     sems = pltpu.SemaphoreType.DMA
     common = [metric, spread, determinant]
@@ -989,18 +965,15 @@
         [mass, mass_prior, *mass_dom, *common, keep, matrices],
         pair + [inner_shape, sems((blocks,))], far_out=(0,),
     )
-    head_near, inverse_ends, *res_faces = call(
-        start_faces_kernel, "start_faces", [ends_shape] * 2 + faces(1),
+    head_ends, inverse_ends, residual_ends, *res_faces, res_end = call(
+        start_ends_kernel, "start_ends", [ends_shape] * 3 + faces(1) + [end_shape],
         [mass, mass_prior, *mass_dom, *mass_batch, *common, keep, matrices, residual_inner],
-        pair + [side_shape],
-    )
-    res_dom = swaps(*res_faces, "dom")
-    head_ends, residual_ends, res_ends = call(
-        start_ends_kernel, "start_ends", [ends_shape] * 2 + [end_shape],
-        [head_near, *common, matrices, residual_inner], pair + [sems((1,))], far_out=(0,),
-    )
+        pair + [ends_shape, sems((2,))], far_out=(0,),
+    )
+    res_dom, res_corners = dom_swaps(*res_faces)
     res_batch = swaps(
-        *ends_call("res_ends", (res_ends, *res_dom, 0), (diag_end, *source_dom, 0)), "batch"
+        *ends_call((res_end, *res_corners, 0), (diag_end, *source_dom, 0)),
+        "batch",
     )
     residual = [residual_inner, residual_ends, diagonal, *res_dom, *source_dom]
     direction_inner, diag_inner, image_inner, dots_inner = call(
@@ -1008,22 +981,19 @@
         [*residual, metric, keep, matrices], pair + [inner_shape] * 2 + [sems((blocks,))],
         far_out=(0,),
     )
-    direction_near, residual_near, diag_ends, *image_faces = call(
-        first_faces_kernel, "first_faces", [ends_shape] * 3 + faces(1),
-        [*residual, *res_batch, metric, keep, matrices, image_inner], pair + [side_shape],
-    )
-    image_dom = swaps(*image_faces, "dom")
-    direction_ends, image_ends, image_out, dots = call(
-        first_ends_kernel, "first_ends", [ends_shape] * 2 + [end_shape] + [plane],
-        [direction_near, residual_near, metric, matrices, image_inner, dots_inner],
-        pair + [sems((1,))], far_out=(0,),
-    )
+    direction_ends, diag_ends, image_ends, *image_faces, image_end, dots = call(
+        first_ends_kernel, "first_ends", [ends_shape] * 3 + faces(1) + [end_shape, plane],
+        [*residual, *res_batch, metric, keep, matrices, image_inner, dots_inner],
+        pair + [ends_shape] * 2 + [sems((2,))], far_out=(0,),
+    )
+    image_dom, image_corners = dom_swaps(*image_faces)
     heat_next, heat_values, heat_factors = call(
         heat_kernel, "heat", [block_shape] + [(2, points) + plane] * 2,
         [numerator, *source_dom, inverse_inner, inverse_ends],
     )
-    heat_next, image_out = lax.optimization_barrier((heat_next, image_out))
-    image_batch = swaps(*ends_call("image_ends", (image_out, *image_dom, 0)), "batch")
+    image_batch = swaps(*ends_call((image_end, *image_corners, 0)), "batch")
+    heat_next, received = lax.optimization_barrier((heat_next, image_batch[0]))
+    image_batch = (received, image_batch[1])
     count = lax.axis_size("dom") * lax.axis_size("batch")
     image = [image_inner, image_ends, *image_dom]
     scaled_inner, two_inner, dots = call(
@@ -1031,16 +1001,17 @@
         [*image, diag_inner, metric, keep, matrices, dots],
         pair + [inner_shape] * 2 + [sems((blocks,))], far_out=(0,),
     )
-    scaled_ends, two_ends, *two_faces, two_out, all_dots = call(
+    scaled_ends, two_ends, *two_faces, two_end, all_dots = call(
         second_ends_kernel, "second_ends",
         [ends_shape] * 2 + faces(1) + [end_shape, (count,) + plane],
         [*image, *image_batch, diag_ends, metric, keep, matrices, two_inner, dots],
         pair + [ends_shape] * 2 + [sems((2,))], far_out=(0,),
     )
     all_dots = lax.all_to_all(all_dots, ("dom", "batch"), 0, 0)
-    two_dom = swaps(*two_faces, "dom")
+    two_dom, two_corners = dom_swaps(*two_faces)
     two_batch = swaps(
-        *ends_call("two_ends", (two_out, *two_dom, 0), (heat_end, *source_dom, 1)), "batch"
+        *ends_call((two_end, *two_corners, 0), (heat_end, *source_dom, 1)),
+        "batch",
     )
     chunks = points // CHUNK
     head_next, defect, end_values, end_factors = call(

time: 71.5 us -> 68.3 us (0.955)
  waiting for transfers between devices: 13.9 us -> 8.99 us
  starting transfers between devices: 28.8 us -> 32.1 us
  Pallas kernels: 27.5 us -> 25.7 us
    ppermute x18 -> x21, waiting for transfers between devices: 13.9 us -> 7.3 us  [the longest x12 7.28 us: far_swap(): return lax.ppermute(array, axis, pairs)]
    ppermute x18 -> x21, starting transfers between devices: 25.9 us -> 28.4 us  [the longest x12 23.8 us: far_swap(): return lax.ppermute(array, axis, pairs)]
    pallas_call x18 -> x13, Pallas kernels: 27.5 us -> 25.7 us  [call(): pl.pallas_call(kernel, name=name, out_shape=[(pltpu.HBM if n in far_out e...]
    all_to_all x1, waiting for transfers between devices: 0.01 us -> 1.69 us  [shards(): all_dots = lax.all_to_all(all_dots, ('dom', 'batch'), 0, 0)]
    all_to_all x1, starting transfers between devices: 2.9 us -> 3.69 us  [shards(): all_dots = lax.all_to_all(all_dots, ('dom', 'batch'), 0, 0)]
  transfers between devices with their start and end apart: 19 -> 22, of which waited for: 7 -> 9; matrix products, arithmetic and copies ran while one was open for 0% -> 0% of each run, Pallas kernels for 31% -> 29%
where the time goes in v3:
time: 68.3 us; the launch traced here: 68 us
  starting transfers between devices  32.1 us (47%)
  Pallas kernels  25.7 us (38%)
  waiting for transfers between devices  8.99 us (13%)
  between operations  0.92 us (1%)
    pallas_call x13, Pallas kernels, call(): pl.pallas_call(kernel, name=name, out_shape=[(pltpu.HBM if n in far_out e...  25.7 us
    ppermute x12, starting transfers between devices, far_swap(): return lax.ppermute(array, axis, pairs)  23.8 us
    ppermute x12, waiting for transfers between devices, far_swap(): return lax.ppermute(array, axis, pairs)  7.28 us
    ppermute x9, starting transfers between devices, near_swap(): lax.ppermute(array, axis, [(index, index ^ 1) for index in range(count)])  4.57 us
    all_to_all x1, starting transfers between devices, shards(): all_dots = lax.all_to_all(all_dots, ('dom', 'batch'), 0, 0)  3.69 us
    all_to_all x1, waiting for transfers between devices, shards(): all_dots = lax.all_to_all(all_dots, ('dom', 'batch'), 0, 0)  1.69 us
  transfers between devices with their start and end apart: 22, of which 9 were waited for; matrix products, arithmetic and copies ran while one was open for 0% of the time, Pallas kernels for 29%

profile of v3, /device:TPU:0, one launch (start us, length us, event | category | flops | bytes accessed | tf_op | source)
XLA Modules:
  0.0 68.0 jit_solution(9024432129574050517)
XLA Ops:
  0.6 2.0 %mass_faces.1 = (f32[2,232,128]{2,1,0:T(8,128)S(1)}, f32[2,232,128]{2,1,0:T(8,128)S(1)}, f32[2,16,128]{2,1,0:T(8,128)}, f32[1,2,8,8,128]{4,3,2,1,0:T(8,128)S(1)}...) custom-call(bf16[8,4,8,8,128]{4,3,2,1,0:T(8,128)(2,1)} %bitcast.124, ...), custom_call_target="tpu_custom_call" | custom-call | bytes 2000000 | tf_op jit(solution)/shard_map/mass_faces/pallas_call | solution.py:828
  3.2 3.6 %collective-permute-start.1 = (f32[2,232,128]{2,1,0:T(8,128)S(1)}, f32[2,232,128]{2,1,0:T(8,128)S(1)}, u32[]{:S(2)}, u32[]{:S(2)}) collective-permute-start(f32[2,232,128]{2,1,0:T(8,128)S(1)} %get-tuple-element.66), channel_id=1, source_target_pairs={{0,28},{4,8},{8,4},{12,16},{16,12},{20,24},{24,20},{28,0},{1,29},{... | collective-permute-start | bytes 712712 | tf_op jit(solution)/shard_map/ppermute | solution.py:857
  6.7 4.0 %prepare.1 = (f32[8,4,64,128]{3,2,1,0:T(8,128)S(1)}, f32[8,4,64,128]{3,2,1,0:T(8,128)S(1)}, f32[6,8,4,64,128]{4,3,2,1,0:T(8,128)S(1)}, f32[8,4,64,128]{3,2,1,0:T(8,128)S(1)}) custom-call(bf16[8,4,8,8,128]{4,3,2,1,0:T(8,128)(2,1)} %bitcast.125, f32[8,4,8,8,128]{4,3,2,1,0:T(8,128)} %bitcast.134, bf16[3,8,4,8,8,128]{5,4,3,2,1,0:T(8,128)(2,1)} %bitcast.135, ...), custom_call_target="tpu_custom_call" | custom-call | bytes 10000000 | tf_op jit(solution)/shard_map/prepare/pallas_call | solution.py:828
  10.8 4.0 %source.1 = (f32[8,4,64,128]{3,2,1,0:T(8,128)S(1)}, f32[2,232,128]{2,1,0:T(8,128)S(1)}, f32[2,232,128]{2,1,0:T(8,128)S(1)}, f32[2,16,128]{2,1,0:T(8,128)}, f32[1...) custom-call(f32[6,8,4,64,128]{4,3,2,1,0:T(8,128)S(1)} %get-tuple-element.67.metric, ...), custom_call_target="tpu_custom_call" | custom-call | bytes 14000000 | tf_op jit(solution)/shard_map/source/pallas_call | solution.py:828
  14.8 0.6 collective-permute-start.7
  15.6 1.6 %collective-permute-start.2 = (f32[2,8,8,128]{3,2,1,0:T(8,128)S(1)}, f32[2,8,8,128]{3,2,1,0:T(8,128)S(1)}, u32[]{:S(2)}, u32[]{:S(2)}) collective-permute-start(f32[2,8,8,128]{3,2,1,0:T(8,128)S(1)} %get-tuple-element.71), channel_id=1, source_target_pairs={{0,1},{1,0},{2,3},{3,2},{4,5},{5,4},{6,7},{7,6},{8,9},{9,8},{10,11... | collective-permute-start | bytes 196616 | tf_op jit(solution)/shard_map/ppermute | solution.py:851
  17.2 2.5 %collective-permute-start.3 = (f32[2,8,8,128]{3,2,1,0:T(8,128)S(1)}, f32[2,8,8,128]{3,2,1,0:T(8,128)S(1)}, u32[]{:S(2)}, u32[]{:S(2)}) collective-permute-start(f32[2,8,8,128]{3,2,1,0:T(8,128)S(1)} %get-tuple-element.72), channel_id=1, source_target_pairs={{0,3},{1,2},{2,1},{3,0},{4,7},{5,6},{6,5},{7,4},{8,11},{9,10},{10,... | collective-permute-start | bytes 196616 | tf_op jit(solution)/shard_map/ppermute | solution.py:857
  19.7 1.5 %start_inner.1 = (f32[8,2,64,128]{3,2,1,0:T(8,128)}, f32[8,2,64,128]{3,2,1,0:T(8,128)S(1)}, f32[8,2,64,128]{3,2,1,0:T(8,128)S(1)}) custom-call(f32[8,4,64,128]{3,2,1,0:T(8,128)S(1)} %get-tuple-element.63.mass, f32[8,4,64,128]{3,2,1,0:T(8,128)S(1)} %get-tuple-element.64.mass_prior, f32[2,232,128]{2,1,0:T(8,128)S(1)} %collective-permute-done.dom_first.refs_1_.refs_4_, ...), custom_call_target="tpu_custom_call" | custom-call | bytes 8000000 | tf_op jit(solution)/shard_map/start_inner/pallas_call | solution.py:828
  21.3 2.2 %collective-permute-done.3.batch_second = f32[2,8,8,128]{3,2,1,0:T(8,128)S(1)} collective-permute-done((f32[2,8,8,128]{3,2,1,0:T(8,128)S(1)}, f32[2,8,8,128]{3,2,1,0:T(8,128)S(1)}, u32[]{:S(2)}, u32[]{:S(2)}) %collective-permute-start.3) | collective-permute-done | bytes 65568 | tf_op jit(solution)/shard_map/ppermute | solution.py:857
  23.5 2.1 %start_ends.1 = (f32[8,2,64,128]{3,2,1,0:T(8,128)}, f32[8,2,64,128]{3,2,1,0:T(8,128)S(1)}, f32[8,2,64,128]{3,2,1,0:T(8,128)S(1)}, f32[1,232,128]{2,1,0:T(8,128)S...) custom-call(f32[8,4,64,128]{3,2,1,0:T(8,128)S(1)} %get-tuple-element.63.mass, ...), custom_call_target="tpu_custom_call" | custom-call | bytes 8000000 | tf_op jit(solution)/shard_map/start_ends/pallas_call | solution.py:828
  25.6 1.8 %collective-permute-start.8 = (f32[1,16,128]{2,1,0:T(8,128)S(1)}, f32[1,16,128]{2,1,0:T(8,128)S(1)}, u32[]{:S(2)}, u32[]{:S(2)}) collective-permute-start(f32[1,16,128]{2,1,0:T(8,128)S(1)} %get-tuple-element.83), channel_id=1, source_target_pairs={{0,28},{4,8},{8,4},{12,16},{16,12},{20,24},{24,20},{28,0},{1,29},{... | collective-permute-start | bytes 24584 | tf_op jit(solution)/shard_map/ppermute | solution.py:857
  27.4 0.9 %collective-permute-start.5 = (f32[1,232,128]{2,1,0:T(8,128)S(1)}, f32[1,232,128]{2,1,0:T(8,128)S(1)}, u32[]{:S(2)}, u32[]{:S(2)}) collective-permute-start(f32[1,232,128]{2,1,0:T(8,128)S(1)} %get-tuple-element.76), channel_id=1, source_target_pairs={{0,28},{4,8},{8,4},{12,16},{16,12},{20,24},{24,20},{28,0},{1,29},{... | collective-permute-start | bytes 356360 | tf_op jit(solution)/shard_map/ppermute | solution.py:857
  28.4 1.2 %collective-permute-done.8 = f32[1,16,128]{2,1,0:T(8,128)S(1)} collective-permute-done((f32[1,16,128]{2,1,0:T(8,128)S(1)}, f32[1,16,128]{2,1,0:T(8,128)S(1)}, u32[]{:S(2)}, u32[]{:S(2)}) %collective-permute-start.8) | collective-permute-done | bytes 8224 | tf_op jit(solution)/shard_map/ppermute | solution.py:857
  30.4 2.5 %collective-permute-start.10 = (f32[2,8,8,128]{3,2,1,0:T(8,128)S(1)}, f32[2,8,8,128]{3,2,1,0:T(8,128)S(1)}, u32[]{:S(2)}, u32[]{:S(2)}) collective-permute-start(f32[2,8,8,128]{3,2,1,0:T(8,128)S(1)} %pad_maximum_fusion.1), channel_id=1, source_target_pairs={{0,3},{1,2},{2,1},{3,0},{4,7},{5,6},{6,5},{7,4},{8,11},{9,10},{10,... | collective-permute-start | bytes 196616 | tf_op jit(solution)/shard_map/ppermute | solution.py:857
  32.9 0.8 %collective-permute-done.5.res_second = f32[1,232,128]{2,1,0:T(8,128)S(1)} collective-permute-done((f32[1,232,128]{2,1,0:T(8,128)S(1)}, f32[1,232,128]{2,1,0:T(8,128)S(1)}, u32[]{:S(2)}, u32[]{:S(2)}) %collective-permute-start.5) | collective-permute-done | bytes 118816 | tf_op jit(solution)/shard_map/ppermute | solution.py:857
  33.7 2.1 %first_inner.1 = (f32[8,2,64,128]{3,2,1,0:T(8,128)}, f32[8,2,64,128]{3,2,1,0:T(8,128)S(1)}, f32[8,2,64,128]{3,2,1,0:T(8,128)S(1)}, f32[8,128]{1,0:T(8,128)S(1)}) custom-call(f32[8,2,64,128]{3,2,1,0:T(8,128)S(1)} %get-tuple-element.68.residual_inner, f32[8,2,64,128]{3,2,1,0:T(8,128)S(1)} %get-tuple-element.73.residual_ends, ...), custom_call_target="tpu_custom_call" | custom-call | bytes 8000000 | tf_op jit(solution)/shard_map/first_inner/pallas_call | solution.py:828
  35.8 0.7 collective-permute-done.10.batch_second
  36.4 1.5 %first_ends.1 = (f32[8,2,64,128]{3,2,1,0:T(8,128)}, f32[8,2,64,128]{3,2,1,0:T(8,128)S(1)}, f32[8,2,64,128]{3,2,1,0:T(8,128)S(1)}, f32[1,232,128]{2,1,0:T(8,128)S...) custom-call(f32[8,2,64,128]{3,2,1,0:T(8,128)S(1)} %get-tuple-element, ...), custom_call_target="tpu_custom_call" | custom-call | bytes 6000000 | tf_op jit(solution)/shard_map/first_ends/pallas_call | solution.py:828
  38.0 2.2 %collective-permute-start.13 = (f32[1,16,128]{2,1,0:T(8,128)S(1)}, f32[1,16,128]{2,1,0:T(8,128)S(1)}, u32[]{:S(2)}, u32[]{:S(2)}) collective-permute-start(f32[1,16,128]{2,1,0:T(8,128)S(1)} %get-tuple-element.97), channel_id=1, source_target_pairs={{0,28},{4,8},{8,4},{12,16},{16,12},{20,24},{24,20},{28,0},{1,29},{... | collective-permute-start | bytes 24584 | tf_op jit(solution)/shard_map/ppermute | solution.py:857
  40.7 1.3 %collective-permute-done.13 = f32[1,16,128]{2,1,0:T(8,128)S(1)} collective-permute-done((f32[1,16,128]{2,1,0:T(8,128)S(1)}, f32[1,16,128]{2,1,0:T(8,128)S(1)}, u32[]{:S(2)}, u32[]{:S(2)}) %collective-permute-start.13) | collective-permute-done | bytes 8224 | tf_op jit(solution)/shard_map/ppermute | solution.py:857
  42.2 2.5 %collective-permute-start.15 = (f32[1,8,8,128]{3,2,1,0:T(8,128)S(1)}, f32[1,8,8,128]{3,2,1,0:T(8,128)S(1)}, u32[]{:S(2)}, u32[]{:S(2)}) collective-permute-start(f32[1,8,8,128]{3,2,1,0:T(8,128)S(1)} %get-tuple-element.141), channel_id=1, source_target_pairs={{0,3},{1,2},{2,1},{3,0},{4,7},{5,6},{6,5},{7,4},{8,11},{9,10},{10,... | collective-permute-start | bytes 98312 | tf_op jit(solution)/shard_map/ppermute | solution.py:857
  44.7 1.2 %heat.1 = (f32[8,4,64,128]{3,2,1,0:T(8,128)}, f32[2,8,8,128]{3,2,1,0:T(8,128)S(1)}, f32[2,8,8,128]{3,2,1,0:T(8,128)S(1)}) custom-call(f32[8,4,64,128]{3,2,1,0:T(8,128)S(1)} %get-tuple-element.92.numerator, f32[2,232,128]{2,1,0:T(8,128)S(1)} %collective-permute-done.6.diag_first.dom_first, f32[2,232,128]{2,1,0:T(8,128)S(1)} %collective-permute-done.7.diag_second.dom_second, ...), custom_call_target="tpu_custom_call" | custom-call | bytes 4000000 | tf_op jit(solution)/shard_map/heat/pallas_call | solution.py:828
  45.9 1.4 %second_inner.1 = (f32[8,2,64,128]{3,2,1,0:T(8,128)}, f32[8,2,64,128]{3,2,1,0:T(8,128)S(1)}, f32[8,128]{1,0:T(8,128)S(1)}) custom-call(f32[8,2,64,128]{3,2,1,0:T(8,128)S(1)} %get-tuple-element.79.image_inner, f32[8,2,64,128]{3,2,1,0:T(8,128)S(1)} %get-tuple-element.86.image_ends, f32[1,232,128]{2,1,0:T(8,128)S(1)} %collective-permute-done.11.dom_first, ...), custom_call_target="tpu_custom_call" | custom-call | bytes 8000000 | tf_op jit(solution)/shard_map/second_inner/pallas_call | solution.py:828
  47.9 2.1 %second_ends.1 = (f32[8,2,64,128]{3,2,1,0:T(8,128)}, f32[8,2,64,128]{3,2,1,0:T(8,128)S(1)}, f32[1,232,128]{2,1,0:T(8,128)S(1)}, f32[1,232,128]{2,1,0:T(8,128)S(1...) custom-call(f32[8,2,64,128]{3,2,1,0:T(8,128)S(1)} %get-tuple-element.79.image_inner, ...), custom_call_target="tpu_custom_call" | custom-call | bytes 8000000 | tf_op jit(solution)/shard_map/second_ends/pallas_call | solution.py:828
  50.0 1.7 %collective-permute-start.18 = (f32[1,16,128]{2,1,0:T(8,128)S(1)}, f32[1,16,128]{2,1,0:T(8,128)S(1)}, u32[]{:S(2)}, u32[]{:S(2)}) collective-permute-start(f32[1,16,128]{2,1,0:T(8,128)S(1)} %get-tuple-element.114), channel_id=1, source_target_pairs={{0,28},{4,8},{8,4},{12,16},{16,12},{20,24},{24,20},{28,0},{1,29},{... | collective-permute-start | bytes 24584 | tf_op jit(solution)/shard_map/ppermute | solution.py:857
  51.8 3.7 %all-to-all-start = ((f32[32,8,128]{2,1,0:T(8,128)}), f32[32,8,128]{2,1,0:T(8,128)S(1)}, u32[]{:S(2)}, u32[]{:S(2)}) async-start(f32[32,8,128]{2,1,0:T(8,128)} %get-tuple-element.104), calls=%async_computation | async-start | bytes 262144 | tf_op jit(solution)/shard_map/all_to_all | solution.py:1010
  55.5 2.5 %collective-permute-start.17 = (f32[1,232,128]{2,1,0:T(8,128)S(1)}, f32[1,232,128]{2,1,0:T(8,128)S(1)}, u32[]{:S(2)}, u32[]{:S(2)}) collective-permute-start(f32[1,232,128]{2,1,0:T(8,128)S(1)} %get-tuple-element.103), channel_id=1, source_target_pairs={{0,28},{4,8},{8,4},{12,16},{16,12},{20,24},{24,20},{28,0},{1,29},{... | collective-permute-start | bytes 356360 | tf_op jit(solution)/shard_map/ppermute | solution.py:857
  58.0 1.5 %collective-permute-start.19 = (f32[2,8,8,128]{3,2,1,0:T(8,128)S(1)}, f32[2,8,8,128]{3,2,1,0:T(8,128)S(1)}, u32[]{:S(2)}, u32[]{:S(2)}) collective-permute-start(f32[2,8,8,128]{3,2,1,0:T(8,128)S(1)} %pad_maximum_fusion.2), channel_id=1, source_target_pairs={{0,1},{1,0},{2,3},{3,2},{4,5},{5,4},{6,7},{7,6},{8,9},{9,8},{10,11... | collective-permute-start | bytes 196616 | tf_op jit(solution)/shard_map/ppermute | solution.py:851
  59.6 2.4 %collective-permute-start.20 = (f32[2,8,8,128]{3,2,1,0:T(8,128)S(1)}, f32[2,8,8,128]{3,2,1,0:T(8,128)S(1)}, u32[]{:S(2)}, u32[]{:S(2)}) collective-permute-start(f32[2,8,8,128]{3,2,1,0:T(8,128)S(1)} %pad_maximum_fusion.3), channel_id=1, source_target_pairs={{0,3},{1,2},{2,1},{3,0},{4,7},{5,6},{6,5},{7,4},{8,11},{9,10},{10,... | collective-permute-start | bytes 196616 | tf_op jit(solution)/shard_map/ppermute | solution.py:857
  62.4 1.7 %all-to-all-done.all_dots = f32[32,8,128]{2,1,0:T(8,128)S(1)} async-done(((f32[32,8,128]{2,1,0:T(8,128)}), f32[32,8,128]{2,1,0:T(8,128)S(1)}, u32[]{:S(2)}, u32[]{:S(2)}) %all-to-all-start) | async-done | bytes 131104 | tf_op jit(solution)/shard_map/all_to_all | solution.py:1010
  64.1 3.2 %last.1 = (f32[8,4,64,128]{3,2,1,0:T(8,128)}, f32[8,4,64,128]{3,2,1,0:T(8,128)}, f32[2,8,8,128]{3,2,1,0:T(8,128)S(1)}, f32[2,8,8,128]{3,2,1,0:T(8,128)S(1)}) custom-call(f32[8,2,64,128]{3,2,1,0:T(8,128)S(1)} %get-tuple-element.91.two_inner.image_inner, f32[8,2,64,128]{3,2,1,0:T(8,128)S(1)} %get-tuple-element.101.image_ends, ...), custom_call_target="tpu_custom_call" | custom-call | bytes 12000000 | tf_op jit(solution)/shard_map/last/pallas_call | solution.py:828
  67.3 0.7 %close.1 = (f32[8,4,64,128]{3,2,1,0:T(8,128)}, f32[8,4,64,128]{3,2,1,0:T(8,128)}) custom-call(f32[8,4,64,128]{3,2,1,0:T(8,128)} %get-tuple-element.111.defect, f32[8,4,64,128]{3,2,1,0:T(8,128)} %get-tuple-element.112.heat, f32[2,8,8,128]{3,2,1,0:T(8,128)S(1)} %collective-permute-done.19.batch_first, ...), custom_call_target="tpu_custom_call", output_to_operand_aliasing={{0}: (0, {}), {1}: (1, {})} | custom-call | bytes 2000000 | tf_op jit(solution)/shard_map/close/pallas_call | solution.py:828
  (54 shorter events, 3.3 us)
Async XLA Ops:
  0.6 6.1 %copy-start.1 = (bf16[256,192]{1,0:T(8,128)(2,1)S(1)}, bf16[256,192]{1,0:T(8,128)(2,1)}, u32[]{:S(2)}) copy-start(bf16[256,192]{1,0:T(8,128)(2,1)} %constant.3.clone.matrices) | copy-start | bytes 294916
  2.6 12.9 %collective-permute-start = (f32[2,232,128]{2,1,0:T(8,128)S(1)}, f32[2,232,128]{2,1,0:T(8,128)S(1)}, u32[]{:S(2)}, u32[]{:S(2)}) collective-permute-start(f32[2,232,128]{2,1,0:T(8,128)S(1)} %get-tuple-element.65), channel_id=1, source_target_pairs={{0,4},{4,0},{8,12},{12,8},{16,20},{20,16},{24,28},{28,24},{1,5},{5... | collective-permute-start | bytes 712712 | tf_op jit(solution)/shard_map/ppermute | solution.py:851
  3.2 12.4 %collective-permute-start.1 = (f32[2,232,128]{2,1,0:T(8,128)S(1)}, f32[2,232,128]{2,1,0:T(8,128)S(1)}, u32[]{:S(2)}, u32[]{:S(2)}) collective-permute-start(f32[2,232,128]{2,1,0:T(8,128)S(1)} %get-tuple-element.66), channel_id=1, source_target_pairs={{0,28},{4,8},{8,4},{12,16},{16,12},{20,24},{24,20},{28,0},{1,29},{... | collective-permute-start | bytes 712712 | tf_op jit(solution)/shard_map/ppermute | solution.py:857
  6.7 4.0 %copy-start = (bf16[1,8,4,8,8,128]{5,4,3,2,1,0:T(8,128)(2,1)S(1)}, bf16[1,8,4,8,8,128]{5,4,3,2,1,0:T(8,128)(2,1)}, u32[]{:S(2)}) copy-start(bf16[1,8,4,8,8,128]{5,4,3,2,1,0:T(8,128)(2,1)} %param.13) | copy-start | bytes 1572868
  6.7 4.0 %copy-start.3 = (bf16[3,1,8,4,8,8,128]{6,5,4,3,2,1,0:T(8,128)(2,1)S(1)}, bf16[3,1,8,4,8,8,128]{6,5,4,3,2,1,0:T(8,128)(2,1)}, u32[]{:S(2)}) copy-start(bf16[3,1,8,4,8,8,128]{6,5,4,3,2,1,0:T(8,128)(2,1)} %param.10) | copy-start | bytes 4718596
  6.7 4.0 %copy-start.4 = (f32[1,8,4,8,8,128]{5,4,3,2,1,0:T(8,128)S(1)}, f32[1,8,4,8,8,128]{5,4,3,2,1,0:T(8,128)}, u32[]{:S(2)}) copy-start(f32[1,8,4,8,8,128]{5,4,3,2,1,0:T(8,128)} %param.9) | copy-start | bytes 3145732
  10.7 4.7 %copy-start.5 = (s32[1,8,4,8]{3,2,1,0:T(4,128)S(1)}, s32[1,8,4,8]{3,2,1,0:T(4,128)}, u32[]{:S(2)}) copy-start(s32[1,8,4,8]{3,2,1,0:T(4,128)} %param.16) | copy-start | bytes 3076
  14.8 5.0 %copy-start.2 = (f32[1,8,4,8,8,128]{5,4,3,2,1,0:T(8,128)S(1)}, f32[1,8,4,8,8,128]{5,4,3,2,1,0:T(8,128)}, u32[]{:S(2)}) copy-start(f32[1,8,4,8,8,128]{5,4,3,2,1,0:T(8,128)} %param.14) | copy-start | bytes 3145732
  14.8 5.0 %collective-permute-start.6 = (f32[2,232,128]{2,1,0:T(8,128)S(1)}, f32[2,232,128]{2,1,0:T(8,128)S(1)}, u32[]{:S(2)}, u32[]{:S(2)}) collective-permute-start(f32[2,232,128]{2,1,0:T(8,128)S(1)} %get-tuple-element.77), channel_id=1, source_target_pairs={{0,4},{4,0},{8,12},{12,8},{16,20},{20,16},{24,28},{28,24},{1,5},{5... | collective-permute-start | bytes 712712 | tf_op jit(solution)/shard_map/ppermute | solution.py:851
  14.8 13.6 %collective-permute-start.7 = (f32[2,232,128]{2,1,0:T(8,128)S(1)}, f32[2,232,128]{2,1,0:T(8,128)S(1)}, u32[]{:S(2)}, u32[]{:S(2)}) collective-permute-start(f32[2,232,128]{2,1,0:T(8,128)S(1)} %get-tuple-element.78), channel_id=1, source_target_pairs={{0,28},{4,8},{8,4},{12,16},{16,12},{20,24},{24,20},{28,0},{1,29},{... | collective-permute-start | bytes 712712 | tf_op jit(solution)/shard_map/ppermute | solution.py:857
  15.6 5.7 %collective-permute-start.2 = (f32[2,8,8,128]{3,2,1,0:T(8,128)S(1)}, f32[2,8,8,128]{3,2,1,0:T(8,128)S(1)}, u32[]{:S(2)}, u32[]{:S(2)}) collective-permute-start(f32[2,8,8,128]{3,2,1,0:T(8,128)S(1)} %get-tuple-element.71), channel_id=1, source_target_pairs={{0,1},{1,0},{2,3},{3,2},{4,5},{5,4},{6,7},{7,6},{8,9},{9,8},{10,11... | collective-permute-start | bytes 196616 | tf_op jit(solution)/shard_map/ppermute | solution.py:851
  17.2 6.2 %collective-permute-start.3 = (f32[2,8,8,128]{3,2,1,0:T(8,128)S(1)}, f32[2,8,8,128]{3,2,1,0:T(8,128)S(1)}, u32[]{:S(2)}, u32[]{:S(2)}) collective-permute-start(f32[2,8,8,128]{3,2,1,0:T(8,128)S(1)} %get-tuple-element.72), channel_id=1, source_target_pairs={{0,3},{1,2},{2,1},{3,0},{4,7},{5,6},{6,5},{7,4},{8,11},{9,10},{10,... | collective-permute-start | bytes 196616 | tf_op jit(solution)/shard_map/ppermute | solution.py:857
  25.6 4.0 %collective-permute-start.8 = (f32[1,16,128]{2,1,0:T(8,128)S(1)}, f32[1,16,128]{2,1,0:T(8,128)S(1)}, u32[]{:S(2)}, u32[]{:S(2)}) collective-permute-start(f32[1,16,128]{2,1,0:T(8,128)S(1)} %get-tuple-element.83), channel_id=1, source_target_pairs={{0,28},{4,8},{8,4},{12,16},{16,12},{20,24},{24,20},{28,0},{1,29},{... | collective-permute-start | bytes 24584 | tf_op jit(solution)/shard_map/ppermute | solution.py:857
  27.4 2.2 %collective-permute-start.4 = (f32[1,232,128]{2,1,0:T(8,128)S(1)}, f32[1,232,128]{2,1,0:T(8,128)S(1)}, u32[]{:S(2)}, u32[]{:S(2)}) collective-permute-start(f32[1,232,128]{2,1,0:T(8,128)S(1)} %get-tuple-element.75), channel_id=1, source_target_pairs={{0,4},{4,0},{8,12},{12,8},{16,20},{20,16},{24,28},{28,24},{1,5},{5... | collective-permute-start | bytes 356360 | tf_op jit(solution)/shard_map/ppermute | solution.py:851
  27.4 6.3 %collective-permute-start.5 = (f32[1,232,128]{2,1,0:T(8,128)S(1)}, f32[1,232,128]{2,1,0:T(8,128)S(1)}, u32[]{:S(2)}, u32[]{:S(2)}) collective-permute-start(f32[1,232,128]{2,1,0:T(8,128)S(1)} %get-tuple-element.76), channel_id=1, source_target_pairs={{0,28},{4,8},{8,4},{12,16},{16,12},{20,24},{24,20},{28,0},{1,29},{... | collective-permute-start | bytes 356360 | tf_op jit(solution)/shard_map/ppermute | solution.py:857
  29.7 6.0 %collective-permute-start.9 = (f32[2,8,8,128]{3,2,1,0:T(8,128)S(1)}, f32[2,8,8,128]{3,2,1,0:T(8,128)S(1)}, u32[]{:S(2)}, u32[]{:S(2)}) collective-permute-start(f32[2,8,8,128]{3,2,1,0:T(8,128)S(1)} %pad_maximum_fusion), channel_id=1, source_target_pairs={{0,1},{1,0},{2,3},{3,2},{4,5},{5,4},{6,7},{7,6},{8,9},{9,8},{10,11... | collective-permute-start | bytes 196616 | tf_op jit(solution)/shard_map/ppermute | solution.py:851
  30.4 6.1 %collective-permute-start.10 = (f32[2,8,8,128]{3,2,1,0:T(8,128)S(1)}, f32[2,8,8,128]{3,2,1,0:T(8,128)S(1)}, u32[]{:S(2)}, u32[]{:S(2)}) collective-permute-start(f32[2,8,8,128]{3,2,1,0:T(8,128)S(1)} %pad_maximum_fusion.1), channel_id=1, source_target_pairs={{0,3},{1,2},{2,1},{3,0},{4,7},{5,6},{6,5},{7,4},{8,11},{9,10},{10,... | collective-permute-start | bytes 196616 | tf_op jit(solution)/shard_map/ppermute | solution.py:857
  37.9 4.1 %collective-permute-start.11 = (f32[1,232,128]{2,1,0:T(8,128)S(1)}, f32[1,232,128]{2,1,0:T(8,128)S(1)}, u32[]{:S(2)}, u32[]{:S(2)}) collective-permute-start(f32[1,232,128]{2,1,0:T(8,128)S(1)} %get-tuple-element.87), channel_id=1, source_target_pairs={{0,4},{4,0},{8,12},{12,8},{16,20},{20,16},{24,28},{28,24},{1,5},{5... | collective-permute-start | bytes 356360 | tf_op jit(solution)/shard_map/ppermute | solution.py:851
  38.0 4.0 %collective-permute-start.13 = (f32[1,16,128]{2,1,0:T(8,128)S(1)}, f32[1,16,128]{2,1,0:T(8,128)S(1)}, u32[]{:S(2)}, u32[]{:S(2)}) collective-permute-start(f32[1,16,128]{2,1,0:T(8,128)S(1)} %get-tuple-element.97), channel_id=1, source_target_pairs={{0,28},{4,8},{8,4},{12,16},{16,12},{20,24},{24,20},{28,0},{1,29},{... | collective-permute-start | bytes 24584 | tf_op jit(solution)/shard_map/ppermute | solution.py:857
  40.2 5.8 %collective-permute-start.12 = (f32[1,232,128]{2,1,0:T(8,128)S(1)}, f32[1,232,128]{2,1,0:T(8,128)S(1)}, u32[]{:S(2)}, u32[]{:S(2)}) collective-permute-start(f32[1,232,128]{2,1,0:T(8,128)S(1)} %get-tuple-element.88), channel_id=1, source_target_pairs={{0,28},{4,8},{8,4},{12,16},{16,12},{20,24},{24,20},{28,0},{1,29},{... | collective-permute-start | bytes 356360 | tf_op jit(solution)/shard_map/ppermute | solution.py:857
  42.0 5.4 %collective-permute-start.14 = (f32[1,8,8,128]{3,2,1,0:T(8,128)S(1)}, f32[1,8,8,128]{3,2,1,0:T(8,128)S(1)}, u32[]{:S(2)}, u32[]{:S(2)}) collective-permute-start(f32[1,8,8,128]{3,2,1,0:T(8,128)S(1)} %get-tuple-element.142), channel_id=1, source_target_pairs={{0,1},{1,0},{2,3},{3,2},{4,5},{5,4},{6,7},{7,6},{8,9},{9,8},{10,11... | collective-permute-start | bytes 98312 | tf_op jit(solution)/shard_map/ppermute | solution.py:851
  42.2 5.7 %collective-permute-start.15 = (f32[1,8,8,128]{3,2,1,0:T(8,128)S(1)}, f32[1,8,8,128]{3,2,1,0:T(8,128)S(1)}, u32[]{:S(2)}, u32[]{:S(2)}) collective-permute-start(f32[1,8,8,128]{3,2,1,0:T(8,128)S(1)} %get-tuple-element.141), channel_id=1, source_target_pairs={{0,3},{1,2},{2,1},{3,0},{4,7},{5,6},{6,5},{7,4},{8,11},{9,10},{10,... | collective-permute-start | bytes 98312 | tf_op jit(solution)/shard_map/ppermute | solution.py:857
  50.0 7.9 %collective-permute-start.18 = (f32[1,16,128]{2,1,0:T(8,128)S(1)}, f32[1,16,128]{2,1,0:T(8,128)S(1)}, u32[]{:S(2)}, u32[]{:S(2)}) collective-permute-start(f32[1,16,128]{2,1,0:T(8,128)S(1)} %get-tuple-element.114), channel_id=1, source_target_pairs={{0,28},{4,8},{8,4},{12,16},{16,12},{20,24},{24,20},{28,0},{1,29},{... | collective-permute-start | bytes 24584 | tf_op jit(solution)/shard_map/ppermute | solution.py:857
  51.8 6.2 %collective-permute-start.16 = (f32[1,232,128]{2,1,0:T(8,128)S(1)}, f32[1,232,128]{2,1,0:T(8,128)S(1)}, u32[]{:S(2)}, u32[]{:S(2)}) collective-permute-start(f32[1,232,128]{2,1,0:T(8,128)S(1)} %get-tuple-element.102), channel_id=1, source_target_pairs={{0,4},{4,0},{8,12},{12,8},{16,20},{20,16},{24,28},{28,24},{1,5},{5... | collective-permute-start | bytes 356360 | tf_op jit(solution)/shard_map/ppermute | solution.py:851
  51.8 12.3 %all-to-all-start = ((f32[32,8,128]{2,1,0:T(8,128)}), f32[32,8,128]{2,1,0:T(8,128)S(1)}, u32[]{:S(2)}, u32[]{:S(2)}) async-start(f32[32,8,128]{2,1,0:T(8,128)} %get-tuple-element.104), calls=%async_computation | async-start | bytes 262144 | tf_op jit(solution)/shard_map/all_to_all | solution.py:1010
  55.5 6.9 %collective-permute-start.17 = (f32[1,232,128]{2,1,0:T(8,128)S(1)}, f32[1,232,128]{2,1,0:T(8,128)S(1)}, u32[]{:S(2)}, u32[]{:S(2)}) collective-permute-start(f32[1,232,128]{2,1,0:T(8,128)S(1)} %get-tuple-element.103), channel_id=1, source_target_pairs={{0,28},{4,8},{8,4},{12,16},{16,12},{20,24},{24,20},{28,0},{1,29},{... | collective-permute-start | bytes 356360 | tf_op jit(solution)/shard_map/ppermute | solution.py:857
  58.0 9.3 %collective-permute-start.19 = (f32[2,8,8,128]{3,2,1,0:T(8,128)S(1)}, f32[2,8,8,128]{3,2,1,0:T(8,128)S(1)}, u32[]{:S(2)}, u32[]{:S(2)}) collective-permute-start(f32[2,8,8,128]{3,2,1,0:T(8,128)S(1)} %pad_maximum_fusion.2), channel_id=1, source_target_pairs={{0,1},{1,0},{2,3},{3,2},{4,5},{5,4},{6,7},{7,6},{8,9},{9,8},{10,11... | collective-permute-start | bytes 196616 | tf_op jit(solution)/shard_map/ppermute | solution.py:851
  59.6 7.7 %collective-permute-start.20 = (f32[2,8,8,128]{3,2,1,0:T(8,128)S(1)}, f32[2,8,8,128]{3,2,1,0:T(8,128)S(1)}, u32[]{:S(2)}, u32[]{:S(2)}) collective-permute-start(f32[2,8,8,128]{3,2,1,0:T(8,128)S(1)} %pad_maximum_fusion.3), channel_id=1, source_target_pairs={{0,3},{1,2},{2,1},{3,0},{4,7},{5,6},{6,5},{7,4},{8,11},{9,10},{10,... | collective-permute-start | bytes 196616 | tf_op jit(solution)/shard_map/ppermute | solution.py:857

commit v4 on v3

--- a/solution.py
+++ b/solution.py
@@ -211,13 +211,14 @@
         out[TAIL, :] = out[TAIL, :] + parts.load(i, b + 1, HEAD)
 
 
-def emit_faces(parts, first, second, corner, n=0):
+def emit_faces(parts, first, second, corner=None, n=0):
     for side, face in zip(dom_sides(), (first, second)):
         for b in range(parts.blocks):
             joined(parts, side, b, face.at[n, face_rows(b)])
-    _, side = dom_sides()
-    corner[n, rows_of(0), :] = parts.load(side, 0, HEAD)
-    corner[n, rows_of(1), :] = parts.load(side, parts.blocks - 1, TAIL)
+    if corner is not None:
+        _, side = dom_sides()
+        corner[n, rows_of(0), :] = parts.load(side, 0, HEAD)
+        corner[n, rows_of(1), :] = parts.load(side, parts.blocks - 1, TAIL)
 
 
 def emit_ends(parts, ends):
@@ -298,7 +299,7 @@
 
 
 def mass_faces_kernel(
-    determinant, prior, first, second, corner, ends, prior_ends, sides, planes, det_face, det_end, prior_face, prior_end,
+    determinant, prior, first, second, ends, prior_ends, sides, planes, det_face, det_end, prior_face, prior_end,
     mass_face, mass_end, sems,
 ):
     blocks, layers = determinant.shape[1], first.shape[2]
@@ -354,8 +355,6 @@
         for b in range(blocks):
             first[n, face_rows(b), :] = mass_face[n, face_first, b]
             second[n, face_rows(b), :] = mass_face[n, 1 - face_first, b]
-        corner[n, rows_of(0), :] = mass_face[n, 1 - face_first, 0, HEAD, :]
-        corner[n, rows_of(1), :] = mass_face[n, 1 - face_first, last, TAIL, :]
 
 
 def prepare_kernel(
@@ -442,7 +441,7 @@
 
 def source_kernel(
     metric, heat, wind, determinant, diagonal, matrices,
-    numerator, first, second, corner, diag_ends, heat_ends, scratch_s, scratch_t,
+    numerator, first, second, diag_ends, heat_ends, scratch_s, scratch_t,
 ):
     blocks, layers = numerator.shape[1], numerator.shape[3]
     weights = height_weights((QUAD_POINT_TALLY, layers))
@@ -469,7 +468,7 @@
 
     lax.fori_loop(0, blocks, block, 0)
     for n, (field, ends) in enumerate(((diagonal, diag_ends), (numerator, heat_ends))):
-        emit_faces(Whole(field), first, second, corner, n)
+        emit_faces(Whole(field), first, second, n=n)
         emit_ends(Whole(field), ends.at[0])
 
 
@@ -539,6 +538,7 @@
             mass, mass_prior, (dom_first, dom_second), None, keep, slot, b, mass_inverse, head
         )
         sending.start(head.at[:, slot], head_out.at[:, slot])
+    for slot, b in elements(True, blocks):
         apply_block(
             head, slot, metric, b, scratch_s, scratch_t, residual, matrices, -1.0,
             start_source(determinant, spread, b),
@@ -561,6 +561,7 @@
             slot, b, mass_inverse, head,
         )
         sending.start(head.at[:, slot], head_out.at[:, slot])
+    for slot, b in elements(False, blocks):
         apply_block(
             head, slot, metric, b, scratch_s, scratch_t, residual, matrices, -1.0,
             start_source(determinant, spread, b),
@@ -671,7 +672,7 @@
     image_inner, image_ends, dom_first, dom_second, batch_first, batch_second,
     diag_inverse, metric, keep, matrices, two_inner, dots_in,
     scaled_out, image_two, first, second, corner, ends, all_dots,
-    scratch_s, scratch_t, image, scaled, sems,
+    scratch_s, scratch_t, image, scaled, dots_out, sems,
 ):
     parts = Parts(image_inner, image_ends)
     sending = Sending(sems)
@@ -690,7 +691,8 @@
     nothing = jnp.zeros_like(energy)
     sums = dots_in[...] + row_sums(nothing, nothing, product, energy)
     for n in range(all_dots.shape[0]):
-        all_dots[n] = sums
+        dots_out[n] = sums
+    sending.start(dots_out, all_dots)
     parts = Parts(two_inner, image_two)
     emit_faces(parts, first, second, corner)
     emit_ends(parts, ends.at[0])
@@ -892,7 +894,9 @@
 
     def faces(count):
         face = (count, blocks * LAST + QUAD_POINT_TALLY, layers)
-        return [face] * 2 + [(count, 2 * QUAD_POINT_TALLY, layers)]
+        return [face] * 2
+
+    corner_shape = (1, 2 * QUAD_POINT_TALLY, layers)
 
     def dom_swaps(first, second, corner):
         corner = far_swap(corner, "dom")
@@ -937,7 +941,7 @@
         ],
         far_in=(0, 1),
     )
-    mass_dom = swaps(*mass_faces[:2], "dom")
+    mass_dom = swaps(*mass_faces, "dom")
     mass, mass_prior, metric, diagonal = call(
         prepare_kernel, "prepare", [block_shape] * 2 + [(6,) + block_shape, block_shape],
         [determinant, prior, pure, mixed, matrices],
@@ -954,7 +958,7 @@
         source_kernel, "source", [block_shape] + faces(2) + [end_shape] * 2,
         [metric, heat, wind, determinant, diagonal, matrices], pair,
     )
-    source_dom = swaps(*source_faces[:2], "dom")
+    source_dom = swaps(*source_faces, "dom")
     mass_batch = swaps(
         *mass_call((mass_end, prior_end), *mass_dom), "batch"
     )
@@ -966,7 +970,7 @@
         pair + [inner_shape, sems((blocks,))], far_out=(0,),
     )
     head_ends, inverse_ends, residual_ends, *res_faces, res_end = call(
-        start_ends_kernel, "start_ends", [ends_shape] * 3 + faces(1) + [end_shape],
+        start_ends_kernel, "start_ends", [ends_shape] * 3 + faces(1) + [corner_shape, end_shape],
         [mass, mass_prior, *mass_dom, *mass_batch, *common, keep, matrices, residual_inner],
         pair + [ends_shape, sems((2,))], far_out=(0,),
     )
@@ -982,7 +986,7 @@
         far_out=(0,),
     )
     direction_ends, diag_ends, image_ends, *image_faces, image_end, dots = call(
-        first_ends_kernel, "first_ends", [ends_shape] * 3 + faces(1) + [end_shape, plane],
+        first_ends_kernel, "first_ends", [ends_shape] * 3 + faces(1) + [corner_shape, end_shape, plane],
         [*residual, *res_batch, metric, keep, matrices, image_inner, dots_inner],
         pair + [ends_shape] * 2 + [sems((2,))], far_out=(0,),
     )
@@ -1003,9 +1007,9 @@
     )
     scaled_ends, two_ends, *two_faces, two_end, all_dots = call(
         second_ends_kernel, "second_ends",
-        [ends_shape] * 2 + faces(1) + [end_shape, (count,) + plane],
+        [ends_shape] * 2 + faces(1) + [corner_shape, end_shape, (count,) + plane],
         [*image, *image_batch, diag_ends, metric, keep, matrices, two_inner, dots],
-        pair + [ends_shape] * 2 + [sems((2,))], far_out=(0,),
+        pair + [ends_shape] * 2 + [(count,) + plane, sems((3,))], far_out=(0, 6),
     )
     all_dots = lax.all_to_all(all_dots, ("dom", "batch"), 0, 0)
     two_dom, two_corners = dom_swaps(*two_faces)

time: 68.3 us -> 67.1 us (0.982)
  Pallas kernels: 25.7 us -> 24.4 us
    pallas_call x13, Pallas kernels: 25.7 us -> 24.4 us  [call(): pl.pallas_call(kernel, name=name, out_shape=[(pltpu.HBM if n in far_out e...]
  transfers between devices with their start and end apart: 22 -> 22, of which waited for: 9 -> 9; matrix products, arithmetic and copies ran while one was open for 0% -> 0% of each run, Pallas kernels for 29% -> 28%
where the time goes in v4:
time: 67.1 us; the launch traced here: 66.8 us
  starting transfers between devices  32.3 us (48%)
  Pallas kernels  24.4 us (36%)
  waiting for transfers between devices  8.86 us (13%)
  between operations  0.95 us (1%)
    pallas_call x13, Pallas kernels, call(): pl.pallas_call(kernel, name=name, out_shape=[(pltpu.HBM if n in far_out e...  24.4 us
    ppermute x12, starting transfers between devices, far_swap(): return lax.ppermute(array, axis, pairs)  23.5 us
    ppermute x12, waiting for transfers between devices, far_swap(): return lax.ppermute(array, axis, pairs)  7.15 us
    ppermute x9, starting transfers between devices, near_swap(): lax.ppermute(array, axis, [(index, index ^ 1) for index in range(count)])  4.54 us
    all_to_all x1, starting transfers between devices, shards(): all_dots = lax.all_to_all(all_dots, ('dom', 'batch'), 0, 0)  4.31 us
    all_to_all x1, waiting for transfers between devices, shards(): all_dots = lax.all_to_all(all_dots, ('dom', 'batch'), 0, 0)  1.69 us
  transfers between devices with their start and end apart: 22, of which 9 were waited for; matrix products, arithmetic and copies ran while one was open for 0% of the time, Pallas kernels for 28%

profile of v4, /device:TPU:0, one launch (start us, length us, event | category | flops | bytes accessed | tf_op | source)
XLA Modules:
  0.0 66.8 jit_solution(2714082474260361352)
XLA Ops:
  0.6 1.4 %mass_faces.1 = (f32[2,232,128]{2,1,0:T(8,128)S(1)}, f32[2,232,128]{2,1,0:T(8,128)S(1)}, f32[1,2,8,8,128]{4,3,2,1,0:T(8,128)S(1)}, f32[1,2,8,8,128]{4,3,2,1,0:T(...) custom-call(bf16[8,4,8,8,128]{4,3,2,1,0:T(8,128)(2,1)} %bitcast.124, f32[8,4,8,8,128]{4,3,2,1,0:T(8,128)} %bitcast.133), custom_call_target="tpu_custom_call" | custom-call | bytes 2000000 | tf_op jit(solution)/shard_map/mass_faces/pallas_call | solution.py:830
  2.5 3.6 %collective-permute-start.1 = (f32[2,232,128]{2,1,0:T(8,128)S(1)}, f32[2,232,128]{2,1,0:T(8,128)S(1)}, u32[]{:S(2)}, u32[]{:S(2)}) collective-permute-start(f32[2,232,128]{2,1,0:T(8,128)S(1)} %get-tuple-element.66), channel_id=1, source_target_pairs={{0,28},{4,8},{8,4},{12,16},{16,12},{20,24},{24,20},{28,0},{1,29},{... | collective-permute-start | bytes 712712 | tf_op jit(solution)/shard_map/ppermute | solution.py:859
  6.1 4.0 %prepare.1 = (f32[8,4,64,128]{3,2,1,0:T(8,128)S(1)}, f32[8,4,64,128]{3,2,1,0:T(8,128)S(1)}, f32[6,8,4,64,128]{4,3,2,1,0:T(8,128)S(1)}, f32[8,4,64,128]{3,2,1,0:T(8,128)S(1)}) custom-call(bf16[8,4,8,8,128]{4,3,2,1,0:T(8,128)(2,1)} %bitcast.125, f32[8,4,8,8,128]{4,3,2,1,0:T(8,128)} %bitcast.134, bf16[3,8,4,8,8,128]{5,4,3,2,1,0:T(8,128)(2,1)} %bitcast.135, ...), custom_call_target="tpu_custom_call" | custom-call | bytes 10000000 | tf_op jit(solution)/shard_map/prepare/pallas_call | solution.py:830
  10.1 3.4 %source.1 = (f32[8,4,64,128]{3,2,1,0:T(8,128)S(1)}, f32[2,232,128]{2,1,0:T(8,128)S(1)}, f32[2,232,128]{2,1,0:T(8,128)S(1)}, f32[1,2,8,8,128]{4,3,2,1,0:T(8,128)S(1)}, f32[1,2,8,8,128]{4,3,2,1,0:T(8,128)S(1)}) custom-call(f32[6,8,4,64,128]{4,3,2,1,0:T(8,128)S(1)} %get-tuple-element.67.metric, f32[8,4,64,128]{3,2,1,0:T(8,128)S(1)} %bitcast.132, ...), custom_call_target="tpu_custom_call" | custom-call | bytes 14000000 | tf_op jit(solution)/shard_map/source/pallas_call | solution.py:830
  13.6 0.6 collective-permute-start.7
  14.5 1.6 %collective-permute-start.2 = (f32[2,8,8,128]{3,2,1,0:T(8,128)S(1)}, f32[2,8,8,128]{3,2,1,0:T(8,128)S(1)}, u32[]{:S(2)}, u32[]{:S(2)}) collective-permute-start(f32[2,8,8,128]{3,2,1,0:T(8,128)S(1)} %get-tuple-element.71), channel_id=1, source_target_pairs={{0,1},{1,0},{2,3},{3,2},{4,5},{5,4},{6,7},{7,6},{8,9},{9,8},{10,11... | collective-permute-start | bytes 196616 | tf_op jit(solution)/shard_map/ppermute | solution.py:853
  16.1 2.5 %collective-permute-start.3 = (f32[2,8,8,128]{3,2,1,0:T(8,128)S(1)}, f32[2,8,8,128]{3,2,1,0:T(8,128)S(1)}, u32[]{:S(2)}, u32[]{:S(2)}) collective-permute-start(f32[2,8,8,128]{3,2,1,0:T(8,128)S(1)} %get-tuple-element.72), channel_id=1, source_target_pairs={{0,3},{1,2},{2,1},{3,0},{4,7},{5,6},{6,5},{7,4},{8,11},{9,10},{10,... | collective-permute-start | bytes 196616 | tf_op jit(solution)/shard_map/ppermute | solution.py:859
  18.6 1.5 %start_inner.1 = (f32[8,2,64,128]{3,2,1,0:T(8,128)}, f32[8,2,64,128]{3,2,1,0:T(8,128)S(1)}, f32[8,2,64,128]{3,2,1,0:T(8,128)S(1)}) custom-call(f32[8,4,64,128]{3,2,1,0:T(8,128)S(1)} %get-tuple-element.63.mass, f32[8,4,64,128]{3,2,1,0:T(8,128)S(1)} %get-tuple-element.64.mass_prior, f32[2,232,128]{2,1,0:T(8,128)S(1)} %collective-permute-done.dom_first.refs_1_.refs_4_, ...), custom_call_target="tpu_custom_call" | custom-call | bytes 8000000 | tf_op jit(solution)/shard_map/start_inner/pallas_call | solution.py:830
  20.2 2.2 %collective-permute-done.3.batch_second = f32[2,8,8,128]{3,2,1,0:T(8,128)S(1)} collective-permute-done((f32[2,8,8,128]{3,2,1,0:T(8,128)S(1)}, f32[2,8,8,128]{3,2,1,0:T(8,128)S(1)}, u32[]{:S(2)}, u32[]{:S(2)}) %collective-permute-start.3) | collective-permute-done | bytes 65568 | tf_op jit(solution)/shard_map/ppermute | solution.py:859
  22.3 2.1 %start_ends.1 = (f32[8,2,64,128]{3,2,1,0:T(8,128)}, f32[8,2,64,128]{3,2,1,0:T(8,128)S(1)}, f32[8,2,64,128]{3,2,1,0:T(8,128)S(1)}, f32[1,232,128]{2,1,0:T(8,128)S...) custom-call(f32[8,4,64,128]{3,2,1,0:T(8,128)S(1)} %get-tuple-element.63.mass, ...), custom_call_target="tpu_custom_call" | custom-call | bytes 8000000 | tf_op jit(solution)/shard_map/start_ends/pallas_call | solution.py:830
  24.5 1.8 %collective-permute-start.8 = (f32[1,16,128]{2,1,0:T(8,128)S(1)}, f32[1,16,128]{2,1,0:T(8,128)S(1)}, u32[]{:S(2)}, u32[]{:S(2)}) collective-permute-start(f32[1,16,128]{2,1,0:T(8,128)S(1)} %get-tuple-element.83), channel_id=1, source_target_pairs={{0,28},{4,8},{8,4},{12,16},{16,12},{20,24},{24,20},{28,0},{1,29},{... | collective-permute-start | bytes 24584 | tf_op jit(solution)/shard_map/ppermute | solution.py:859
  26.3 0.9 %collective-permute-start.5 = (f32[1,232,128]{2,1,0:T(8,128)S(1)}, f32[1,232,128]{2,1,0:T(8,128)S(1)}, u32[]{:S(2)}, u32[]{:S(2)}) collective-permute-start(f32[1,232,128]{2,1,0:T(8,128)S(1)} %get-tuple-element.76), channel_id=1, source_target_pairs={{0,28},{4,8},{8,4},{12,16},{16,12},{20,24},{24,20},{28,0},{1,29},{... | collective-permute-start | bytes 356360 | tf_op jit(solution)/shard_map/ppermute | solution.py:859
  27.2 1.2 %collective-permute-done.8 = f32[1,16,128]{2,1,0:T(8,128)S(1)} collective-permute-done((f32[1,16,128]{2,1,0:T(8,128)S(1)}, f32[1,16,128]{2,1,0:T(8,128)S(1)}, u32[]{:S(2)}, u32[]{:S(2)}) %collective-permute-start.8) | collective-permute-done | bytes 8224 | tf_op jit(solution)/shard_map/ppermute | solution.py:859
  29.2 2.6 %collective-permute-start.10 = (f32[2,8,8,128]{3,2,1,0:T(8,128)S(1)}, f32[2,8,8,128]{3,2,1,0:T(8,128)S(1)}, u32[]{:S(2)}, u32[]{:S(2)}) collective-permute-start(f32[2,8,8,128]{3,2,1,0:T(8,128)S(1)} %pad_maximum_fusion.1), channel_id=1, source_target_pairs={{0,3},{1,2},{2,1},{3,0},{4,7},{5,6},{6,5},{7,4},{8,11},{9,10},{10,... | collective-permute-start | bytes 196616 | tf_op jit(solution)/shard_map/ppermute | solution.py:859
  31.8 0.7 %collective-permute-done.5.res_second = f32[1,232,128]{2,1,0:T(8,128)S(1)} collective-permute-done((f32[1,232,128]{2,1,0:T(8,128)S(1)}, f32[1,232,128]{2,1,0:T(8,128)S(1)}, u32[]{:S(2)}, u32[]{:S(2)}) %collective-permute-start.5) | collective-permute-done | bytes 118816 | tf_op jit(solution)/shard_map/ppermute | solution.py:859
  32.5 2.1 %first_inner.1 = (f32[8,2,64,128]{3,2,1,0:T(8,128)}, f32[8,2,64,128]{3,2,1,0:T(8,128)S(1)}, f32[8,2,64,128]{3,2,1,0:T(8,128)S(1)}, f32[8,128]{1,0:T(8,128)S(1)}) custom-call(f32[8,2,64,128]{3,2,1,0:T(8,128)S(1)} %get-tuple-element.68.residual_inner, f32[8,2,64,128]{3,2,1,0:T(8,128)S(1)} %get-tuple-element.73.residual_ends, ...), custom_call_target="tpu_custom_call" | custom-call | bytes 8000000 | tf_op jit(solution)/shard_map/first_inner/pallas_call | solution.py:830
  34.6 0.7 %collective-permute-done.10.batch_second = f32[2,8,8,128]{3,2,1,0:T(8,128)S(1)} collective-permute-done((f32[2,8,8,128]{3,2,1,0:T(8,128)S(1)}, f32[2,8,8,128]{3,2,1,0:T(8,128)S(1)}, u32[]{:S(2)}, u32[]{:S(2)}) %collective-permute-start.10) | collective-permute-done | bytes 65568 | tf_op jit(solution)/shard_map/ppermute | solution.py:859
  35.3 1.5 %first_ends.1 = (f32[8,2,64,128]{3,2,1,0:T(8,128)}, f32[8,2,64,128]{3,2,1,0:T(8,128)S(1)}, f32[8,2,64,128]{3,2,1,0:T(8,128)S(1)}, f32[1,232,128]{2,1,0:T(8,128)S...) custom-call(f32[8,2,64,128]{3,2,1,0:T(8,128)S(1)} %get-tuple-element, ...), custom_call_target="tpu_custom_call" | custom-call | bytes 6000000 | tf_op jit(solution)/shard_map/first_ends/pallas_call | solution.py:830
  36.8 2.2 %collective-permute-start.13 = (f32[1,16,128]{2,1,0:T(8,128)S(1)}, f32[1,16,128]{2,1,0:T(8,128)S(1)}, u32[]{:S(2)}, u32[]{:S(2)}) collective-permute-start(f32[1,16,128]{2,1,0:T(8,128)S(1)} %get-tuple-element.97), channel_id=1, source_target_pairs={{0,28},{4,8},{8,4},{12,16},{16,12},{20,24},{24,20},{28,0},{1,29},{... | collective-permute-start | bytes 24584 | tf_op jit(solution)/shard_map/ppermute | solution.py:859
  39.5 1.3 %collective-permute-done.13 = f32[1,16,128]{2,1,0:T(8,128)S(1)} collective-permute-done((f32[1,16,128]{2,1,0:T(8,128)S(1)}, f32[1,16,128]{2,1,0:T(8,128)S(1)}, u32[]{:S(2)}, u32[]{:S(2)}) %collective-permute-start.13) | collective-permute-done | bytes 8224 | tf_op jit(solution)/shard_map/ppermute | solution.py:859
  41.0 2.7 %collective-permute-start.15 = (f32[1,8,8,128]{3,2,1,0:T(8,128)S(1)}, f32[1,8,8,128]{3,2,1,0:T(8,128)S(1)}, u32[]{:S(2)}, u32[]{:S(2)}) collective-permute-start(f32[1,8,8,128]{3,2,1,0:T(8,128)S(1)} %get-tuple-element.141), channel_id=1, source_target_pairs={{0,3},{1,2},{2,1},{3,0},{4,7},{5,6},{6,5},{7,4},{8,11},{9,10},{10,... | collective-permute-start | bytes 98312 | tf_op jit(solution)/shard_map/ppermute | solution.py:859
  43.6 1.2 %heat.1 = (f32[8,4,64,128]{3,2,1,0:T(8,128)}, f32[2,8,8,128]{3,2,1,0:T(8,128)S(1)}, f32[2,8,8,128]{3,2,1,0:T(8,128)S(1)}) custom-call(f32[8,4,64,128]{3,2,1,0:T(8,128)S(1)} %get-tuple-element.92.numerator, f32[2,232,128]{2,1,0:T(8,128)S(1)} %collective-permute-done.6.diag_first.dom_first, f32[2,232,128]{2,1,0:T(8,128)S(1)} %collective-permute-done.7.diag_second.dom_second, ...), custom_call_target="tpu_custom_call" | custom-call | bytes 4000000 | tf_op jit(solution)/shard_map/heat/pallas_call | solution.py:830
  44.9 1.4 %second_inner.1 = (f32[8,2,64,128]{3,2,1,0:T(8,128)}, f32[8,2,64,128]{3,2,1,0:T(8,128)S(1)}, f32[8,128]{1,0:T(8,128)S(1)}) custom-call(f32[8,2,64,128]{3,2,1,0:T(8,128)S(1)} %get-tuple-element.79.image_inner, f32[8,2,64,128]{3,2,1,0:T(8,128)S(1)} %get-tuple-element.86.image_ends, f32[1,232,128]{2,1,0:T(8,128)S(1)} %collective-permute-done.11.dom_first, ...), custom_call_target="tpu_custom_call" | custom-call | bytes 8000000 | tf_op jit(solution)/shard_map/second_inner/pallas_call | solution.py:830
  46.8 2.0 %second_ends.1 = (f32[8,2,64,128]{3,2,1,0:T(8,128)}, f32[8,2,64,128]{3,2,1,0:T(8,128)S(1)}, f32[1,232,128]{2,1,0:T(8,128)S(1)}, f32[1,232,128]{2,1,0:T(8,128)S(1...) custom-call(f32[8,2,64,128]{3,2,1,0:T(8,128)S(1)} %get-tuple-element.79.image_inner, ...), custom_call_target="tpu_custom_call" | custom-call | bytes 8000000 | tf_op jit(solution)/shard_map/second_ends/pallas_call | solution.py:830
  48.8 1.2 %collective-permute-start.18 = (f32[1,16,128]{2,1,0:T(8,128)S(1)}, f32[1,16,128]{2,1,0:T(8,128)S(1)}, u32[]{:S(2)}, u32[]{:S(2)}) collective-permute-start(f32[1,16,128]{2,1,0:T(8,128)S(1)} %get-tuple-element.114), channel_id=1, source_target_pairs={{0,28},{4,8},{8,4},{12,16},{16,12},{20,24},{24,20},{28,0},{1,29},{... | collective-permute-start | bytes 24584 | tf_op jit(solution)/shard_map/ppermute | solution.py:859
  50.0 4.3 %all-to-all-start = ((f32[32,8,128]{2,1,0:T(8,128)}), f32[32,8,128]{2,1,0:T(8,128)S(1)}, u32[]{:S(2)}, u32[]{:S(2)}) async-start(f32[32,8,128]{2,1,0:T(8,128)} %get-tuple-element.104), calls=%async_computation | async-start | bytes 262144 | tf_op jit(solution)/shard_map/all_to_all | solution.py:1014
  54.3 2.5 %collective-permute-start.17 = (f32[1,232,128]{2,1,0:T(8,128)S(1)}, f32[1,232,128]{2,1,0:T(8,128)S(1)}, u32[]{:S(2)}, u32[]{:S(2)}) collective-permute-start(f32[1,232,128]{2,1,0:T(8,128)S(1)} %get-tuple-element.103), channel_id=1, source_target_pairs={{0,28},{4,8},{8,4},{12,16},{16,12},{20,24},{24,20},{28,0},{1,29},{... | collective-permute-start | bytes 356360 | tf_op jit(solution)/shard_map/ppermute | solution.py:859
  56.9 1.5 %collective-permute-start.19 = (f32[2,8,8,128]{3,2,1,0:T(8,128)S(1)}, f32[2,8,8,128]{3,2,1,0:T(8,128)S(1)}, u32[]{:S(2)}, u32[]{:S(2)}) collective-permute-start(f32[2,8,8,128]{3,2,1,0:T(8,128)S(1)} %pad_maximum_fusion.2), channel_id=1, source_target_pairs={{0,1},{1,0},{2,3},{3,2},{4,5},{5,4},{6,7},{7,6},{8,9},{9,8},{10,11... | collective-permute-start | bytes 196616 | tf_op jit(solution)/shard_map/ppermute | solution.py:853
  58.4 2.4 %collective-permute-start.20 = (f32[2,8,8,128]{3,2,1,0:T(8,128)S(1)}, f32[2,8,8,128]{3,2,1,0:T(8,128)S(1)}, u32[]{:S(2)}, u32[]{:S(2)}) collective-permute-start(f32[2,8,8,128]{3,2,1,0:T(8,128)S(1)} %pad_maximum_fusion.3), channel_id=1, source_target_pairs={{0,3},{1,2},{2,1},{3,0},{4,7},{5,6},{6,5},{7,4},{8,11},{9,10},{10,... | collective-permute-start | bytes 196616 | tf_op jit(solution)/shard_map/ppermute | solution.py:859
  61.2 1.7 %all-to-all-done.all_dots = f32[32,8,128]{2,1,0:T(8,128)S(1)} async-done(((f32[32,8,128]{2,1,0:T(8,128)}), f32[32,8,128]{2,1,0:T(8,128)S(1)}, u32[]{:S(2)}, u32[]{:S(2)}) %all-to-all-start) | async-done | bytes 131104 | tf_op jit(solution)/shard_map/all_to_all | solution.py:1014
  62.9 3.2 %last.1 = (f32[8,4,64,128]{3,2,1,0:T(8,128)}, f32[8,4,64,128]{3,2,1,0:T(8,128)}, f32[2,8,8,128]{3,2,1,0:T(8,128)S(1)}, f32[2,8,8,128]{3,2,1,0:T(8,128)S(1)}) custom-call(f32[8,2,64,128]{3,2,1,0:T(8,128)S(1)} %get-tuple-element.91.two_inner.image_inner, f32[8,2,64,128]{3,2,1,0:T(8,128)S(1)} %get-tuple-element.101.image_ends, ...), custom_call_target="tpu_custom_call" | custom-call | bytes 12000000 | tf_op jit(solution)/shard_map/last/pallas_call | solution.py:830
  66.1 0.7 %close.1 = (f32[8,4,64,128]{3,2,1,0:T(8,128)}, f32[8,4,64,128]{3,2,1,0:T(8,128)}) custom-call(f32[8,4,64,128]{3,2,1,0:T(8,128)} %get-tuple-element.111.defect, f32[8,4,64,128]{3,2,1,0:T(8,128)} %get-tuple-element.112.heat, f32[2,8,8,128]{3,2,1,0:T(8,128)S(1)} %collective-permute-done.19.batch_first, ...), custom_call_target="tpu_custom_call", output_to_operand_aliasing={{0}: (0, {}), {1}: (1, {})} | custom-call | bytes 2000000 | tf_op jit(solution)/shard_map/close/pallas_call | solution.py:830
  (54 shorter events, 3.2 us)
Async XLA Ops:
  0.6 5.5 %copy-start.1 = (bf16[256,192]{1,0:T(8,128)(2,1)S(1)}, bf16[256,192]{1,0:T(8,128)(2,1)}, u32[]{:S(2)}) copy-start(bf16[256,192]{1,0:T(8,128)(2,1)} %constant.3.clone.matrices) | copy-start | bytes 294916
  2.0 12.4 %collective-permute-start = (f32[2,232,128]{2,1,0:T(8,128)S(1)}, f32[2,232,128]{2,1,0:T(8,128)S(1)}, u32[]{:S(2)}, u32[]{:S(2)}) collective-permute-start(f32[2,232,128]{2,1,0:T(8,128)S(1)} %get-tuple-element.65), channel_id=1, source_target_pairs={{0,4},{4,0},{8,12},{12,8},{16,20},{20,16},{24,28},{28,24},{1,5},{5... | collective-permute-start | bytes 712712 | tf_op jit(solution)/shard_map/ppermute | solution.py:853
  2.5 11.9 %collective-permute-start.1 = (f32[2,232,128]{2,1,0:T(8,128)S(1)}, f32[2,232,128]{2,1,0:T(8,128)S(1)}, u32[]{:S(2)}, u32[]{:S(2)}) collective-permute-start(f32[2,232,128]{2,1,0:T(8,128)S(1)} %get-tuple-element.66), channel_id=1, source_target_pairs={{0,28},{4,8},{8,4},{12,16},{16,12},{20,24},{24,20},{28,0},{1,29},{... | collective-permute-start | bytes 712712 | tf_op jit(solution)/shard_map/ppermute | solution.py:859
  6.1 4.0 %copy-start = (bf16[1,8,4,8,8,128]{5,4,3,2,1,0:T(8,128)(2,1)S(1)}, bf16[1,8,4,8,8,128]{5,4,3,2,1,0:T(8,128)(2,1)}, u32[]{:S(2)}) copy-start(bf16[1,8,4,8,8,128]{5,4,3,2,1,0:T(8,128)(2,1)} %param.13) | copy-start | bytes 1572868
  6.1 4.0 %copy-start.3 = (bf16[3,1,8,4,8,8,128]{6,5,4,3,2,1,0:T(8,128)(2,1)S(1)}, bf16[3,1,8,4,8,8,128]{6,5,4,3,2,1,0:T(8,128)(2,1)}, u32[]{:S(2)}) copy-start(bf16[3,1,8,4,8,8,128]{6,5,4,3,2,1,0:T(8,128)(2,1)} %param.10) | copy-start | bytes 4718596
  6.1 4.0 %copy-start.4 = (f32[1,8,4,8,8,128]{5,4,3,2,1,0:T(8,128)S(1)}, f32[1,8,4,8,8,128]{5,4,3,2,1,0:T(8,128)}, u32[]{:S(2)}) copy-start(f32[1,8,4,8,8,128]{5,4,3,2,1,0:T(8,128)} %param.9) | copy-start | bytes 3145732
  10.1 4.2 %copy-start.5 = (s32[1,8,4,8]{3,2,1,0:T(4,128)S(1)}, s32[1,8,4,8]{3,2,1,0:T(4,128)}, u32[]{:S(2)}) copy-start(s32[1,8,4,8]{3,2,1,0:T(4,128)} %param.16) | copy-start | bytes 3076
  13.6 5.1 %copy-start.2 = (f32[1,8,4,8,8,128]{5,4,3,2,1,0:T(8,128)S(1)}, f32[1,8,4,8,8,128]{5,4,3,2,1,0:T(8,128)}, u32[]{:S(2)}) copy-start(f32[1,8,4,8,8,128]{5,4,3,2,1,0:T(8,128)} %param.14) | copy-start | bytes 3145732
  13.6 5.0 %collective-permute-start.6 = (f32[2,232,128]{2,1,0:T(8,128)S(1)}, f32[2,232,128]{2,1,0:T(8,128)S(1)}, u32[]{:S(2)}, u32[]{:S(2)}) collective-permute-start(f32[2,232,128]{2,1,0:T(8,128)S(1)} %get-tuple-element.77), channel_id=1, source_target_pairs={{0,4},{4,0},{8,12},{12,8},{16,20},{20,16},{24,28},{28,24},{1,5},{5... | collective-permute-start | bytes 712712 | tf_op jit(solution)/shard_map/ppermute | solution.py:853
  13.6 13.6 %collective-permute-start.7 = (f32[2,232,128]{2,1,0:T(8,128)S(1)}, f32[2,232,128]{2,1,0:T(8,128)S(1)}, u32[]{:S(2)}, u32[]{:S(2)}) collective-permute-start(f32[2,232,128]{2,1,0:T(8,128)S(1)} %get-tuple-element.78), channel_id=1, source_target_pairs={{0,28},{4,8},{8,4},{12,16},{16,12},{20,24},{24,20},{28,0},{1,29},{... | collective-permute-start | bytes 712712 | tf_op jit(solution)/shard_map/ppermute | solution.py:859
  14.5 5.7 %collective-permute-start.2 = (f32[2,8,8,128]{3,2,1,0:T(8,128)S(1)}, f32[2,8,8,128]{3,2,1,0:T(8,128)S(1)}, u32[]{:S(2)}, u32[]{:S(2)}) collective-permute-start(f32[2,8,8,128]{3,2,1,0:T(8,128)S(1)} %get-tuple-element.71), channel_id=1, source_target_pairs={{0,1},{1,0},{2,3},{3,2},{4,5},{5,4},{6,7},{7,6},{8,9},{9,8},{10,11... | collective-permute-start | bytes 196616 | tf_op jit(solution)/shard_map/ppermute | solution.py:853
  16.1 6.2 %collective-permute-start.3 = (f32[2,8,8,128]{3,2,1,0:T(8,128)S(1)}, f32[2,8,8,128]{3,2,1,0:T(8,128)S(1)}, u32[]{:S(2)}, u32[]{:S(2)}) collective-permute-start(f32[2,8,8,128]{3,2,1,0:T(8,128)S(1)} %get-tuple-element.72), channel_id=1, source_target_pairs={{0,3},{1,2},{2,1},{3,0},{4,7},{5,6},{6,5},{7,4},{8,11},{9,10},{10,... | collective-permute-start | bytes 196616 | tf_op jit(solution)/shard_map/ppermute | solution.py:859
  24.5 4.0 %collective-permute-start.8 = (f32[1,16,128]{2,1,0:T(8,128)S(1)}, f32[1,16,128]{2,1,0:T(8,128)S(1)}, u32[]{:S(2)}, u32[]{:S(2)}) collective-permute-start(f32[1,16,128]{2,1,0:T(8,128)S(1)} %get-tuple-element.83), channel_id=1, source_target_pairs={{0,28},{4,8},{8,4},{12,16},{16,12},{20,24},{24,20},{28,0},{1,29},{... | collective-permute-start | bytes 24584 | tf_op jit(solution)/shard_map/ppermute | solution.py:859
  26.3 2.2 %collective-permute-start.4 = (f32[1,232,128]{2,1,0:T(8,128)S(1)}, f32[1,232,128]{2,1,0:T(8,128)S(1)}, u32[]{:S(2)}, u32[]{:S(2)}) collective-permute-start(f32[1,232,128]{2,1,0:T(8,128)S(1)} %get-tuple-element.75), channel_id=1, source_target_pairs={{0,4},{4,0},{8,12},{12,8},{16,20},{20,16},{24,28},{28,24},{1,5},{5... | collective-permute-start | bytes 356360 | tf_op jit(solution)/shard_map/ppermute | solution.py:853
  26.3 6.2 %collective-permute-start.5 = (f32[1,232,128]{2,1,0:T(8,128)S(1)}, f32[1,232,128]{2,1,0:T(8,128)S(1)}, u32[]{:S(2)}, u32[]{:S(2)}) collective-permute-start(f32[1,232,128]{2,1,0:T(8,128)S(1)} %get-tuple-element.76), channel_id=1, source_target_pairs={{0,28},{4,8},{8,4},{12,16},{16,12},{20,24},{24,20},{28,0},{1,29},{... | collective-permute-start | bytes 356360 | tf_op jit(solution)/shard_map/ppermute | solution.py:859
  28.6 6.0 %collective-permute-start.9 = (f32[2,8,8,128]{3,2,1,0:T(8,128)S(1)}, f32[2,8,8,128]{3,2,1,0:T(8,128)S(1)}, u32[]{:S(2)}, u32[]{:S(2)}) collective-permute-start(f32[2,8,8,128]{3,2,1,0:T(8,128)S(1)} %pad_maximum_fusion), channel_id=1, source_target_pairs={{0,1},{1,0},{2,3},{3,2},{4,5},{5,4},{6,7},{7,6},{8,9},{9,8},{10,11... | collective-permute-start | bytes 196616 | tf_op jit(solution)/shard_map/ppermute | solution.py:853
  29.2 6.1 %collective-permute-start.10 = (f32[2,8,8,128]{3,2,1,0:T(8,128)S(1)}, f32[2,8,8,128]{3,2,1,0:T(8,128)S(1)}, u32[]{:S(2)}, u32[]{:S(2)}) collective-permute-start(f32[2,8,8,128]{3,2,1,0:T(8,128)S(1)} %pad_maximum_fusion.1), channel_id=1, source_target_pairs={{0,3},{1,2},{2,1},{3,0},{4,7},{5,6},{6,5},{7,4},{8,11},{9,10},{10,... | collective-permute-start | bytes 196616 | tf_op jit(solution)/shard_map/ppermute | solution.py:859
  36.7 4.1 %collective-permute-start.11 = (f32[1,232,128]{2,1,0:T(8,128)S(1)}, f32[1,232,128]{2,1,0:T(8,128)S(1)}, u32[]{:S(2)}, u32[]{:S(2)}) collective-permute-start(f32[1,232,128]{2,1,0:T(8,128)S(1)} %get-tuple-element.87), channel_id=1, source_target_pairs={{0,4},{4,0},{8,12},{12,8},{16,20},{20,16},{24,28},{28,24},{1,5},{5... | collective-permute-start | bytes 356360 | tf_op jit(solution)/shard_map/ppermute | solution.py:853
  36.8 4.0 %collective-permute-start.13 = (f32[1,16,128]{2,1,0:T(8,128)S(1)}, f32[1,16,128]{2,1,0:T(8,128)S(1)}, u32[]{:S(2)}, u32[]{:S(2)}) collective-permute-start(f32[1,16,128]{2,1,0:T(8,128)S(1)} %get-tuple-element.97), channel_id=1, source_target_pairs={{0,28},{4,8},{8,4},{12,16},{16,12},{20,24},{24,20},{28,0},{1,29},{... | collective-permute-start | bytes 24584 | tf_op jit(solution)/shard_map/ppermute | solution.py:859
  39.1 5.8 %collective-permute-start.12 = (f32[1,232,128]{2,1,0:T(8,128)S(1)}, f32[1,232,128]{2,1,0:T(8,128)S(1)}, u32[]{:S(2)}, u32[]{:S(2)}) collective-permute-start(f32[1,232,128]{2,1,0:T(8,128)S(1)} %get-tuple-element.88), channel_id=1, source_target_pairs={{0,28},{4,8},{8,4},{12,16},{16,12},{20,24},{24,20},{28,0},{1,29},{... | collective-permute-start | bytes 356360 | tf_op jit(solution)/shard_map/ppermute | solution.py:859
  40.9 5.4 %collective-permute-start.14 = (f32[1,8,8,128]{3,2,1,0:T(8,128)S(1)}, f32[1,8,8,128]{3,2,1,0:T(8,128)S(1)}, u32[]{:S(2)}, u32[]{:S(2)}) collective-permute-start(f32[1,8,8,128]{3,2,1,0:T(8,128)S(1)} %get-tuple-element.142), channel_id=1, source_target_pairs={{0,1},{1,0},{2,3},{3,2},{4,5},{5,4},{6,7},{7,6},{8,9},{9,8},{10,11... | collective-permute-start | bytes 98312 | tf_op jit(solution)/shard_map/ppermute | solution.py:853
  41.0 5.8 %collective-permute-start.15 = (f32[1,8,8,128]{3,2,1,0:T(8,128)S(1)}, f32[1,8,8,128]{3,2,1,0:T(8,128)S(1)}, u32[]{:S(2)}, u32[]{:S(2)}) collective-permute-start(f32[1,8,8,128]{3,2,1,0:T(8,128)S(1)} %get-tuple-element.141), channel_id=1, source_target_pairs={{0,3},{1,2},{2,1},{3,0},{4,7},{5,6},{6,5},{7,4},{8,11},{9,10},{10,... | collective-permute-start | bytes 98312 | tf_op jit(solution)/shard_map/ppermute | solution.py:859
  48.8 8.0 %collective-permute-start.18 = (f32[1,16,128]{2,1,0:T(8,128)S(1)}, f32[1,16,128]{2,1,0:T(8,128)S(1)}, u32[]{:S(2)}, u32[]{:S(2)}) collective-permute-start(f32[1,16,128]{2,1,0:T(8,128)S(1)} %get-tuple-element.114), channel_id=1, source_target_pairs={{0,28},{4,8},{8,4},{12,16},{16,12},{20,24},{24,20},{28,0},{1,29},{... | collective-permute-start | bytes 24584 | tf_op jit(solution)/shard_map/ppermute | solution.py:859
  50.0 6.8 %collective-permute-start.16 = (f32[1,232,128]{2,1,0:T(8,128)S(1)}, f32[1,232,128]{2,1,0:T(8,128)S(1)}, u32[]{:S(2)}, u32[]{:S(2)}) collective-permute-start(f32[1,232,128]{2,1,0:T(8,128)S(1)} %get-tuple-element.102), channel_id=1, source_target_pairs={{0,4},{4,0},{8,12},{12,8},{16,20},{20,16},{24,28},{28,24},{1,5},{5... | collective-permute-start | bytes 356360 | tf_op jit(solution)/shard_map/ppermute | solution.py:853
  50.0 12.9 %all-to-all-start = ((f32[32,8,128]{2,1,0:T(8,128)}), f32[32,8,128]{2,1,0:T(8,128)S(1)}, u32[]{:S(2)}, u32[]{:S(2)}) async-start(f32[32,8,128]{2,1,0:T(8,128)} %get-tuple-element.104), calls=%async_computation | async-start | bytes 262144 | tf_op jit(solution)/shard_map/all_to_all | solution.py:1014
  54.3 6.9 %collective-permute-start.17 = (f32[1,232,128]{2,1,0:T(8,128)S(1)}, f32[1,232,128]{2,1,0:T(8,128)S(1)}, u32[]{:S(2)}, u32[]{:S(2)}) collective-permute-start(f32[1,232,128]{2,1,0:T(8,128)S(1)} %get-tuple-element.103), channel_id=1, source_target_pairs={{0,28},{4,8},{8,4},{12,16},{16,12},{20,24},{24,20},{28,0},{1,29},{... | collective-permute-start | bytes 356360 | tf_op jit(solution)/shard_map/ppermute | solution.py:859
  56.9 9.3 %collective-permute-start.19 = (f32[2,8,8,128]{3,2,1,0:T(8,128)S(1)}, f32[2,8,8,128]{3,2,1,0:T(8,128)S(1)}, u32[]{:S(2)}, u32[]{:S(2)}) collective-permute-start(f32[2,8,8,128]{3,2,1,0:T(8,128)S(1)} %pad_maximum_fusion.2), channel_id=1, source_target_pairs={{0,1},{1,0},{2,3},{3,2},{4,5},{5,4},{6,7},{7,6},{8,9},{9,8},{10,11... | collective-permute-start | bytes 196616 | tf_op jit(solution)/shard_map/ppermute | solution.py:853
  58.4 7.7 %collective-permute-start.20 = (f32[2,8,8,128]{3,2,1,0:T(8,128)S(1)}, f32[2,8,8,128]{3,2,1,0:T(8,128)S(1)}, u32[]{:S(2)}, u32[]{:S(2)}) collective-permute-start(f32[2,8,8,128]{3,2,1,0:T(8,128)S(1)} %pad_maximum_fusion.3), channel_id=1, source_target_pairs={{0,3},{1,2},{2,1},{3,0},{4,7},{5,6},{6,5},{7,4},{8,11},{9,10},{10,... | collective-permute-start | bytes 196616 | tf_op jit(solution)/shard_map/ppermute | solution.py:859
